TPU v7x, 1024 devices: a whole 4x4x32 slice. The times are simulated.
1024 devices in a mesh: doc: 4 (over y), seq: 64 (over z, core), tensor: 4 (over x).
Axes of the slice: x: 4, y: 4, z: 32, core: 2. Of those that a mesh axis runs over, the one named last changes fastest.
Arguments:
- queries: bfloat16 [4, 16384, 4096], P('doc', 'seq', 'tensor'), may hold values from -400 to 400
- vision: bfloat16 [4, 64, 128, 8192], P('doc', 'seq', 'tensor'), may hold values from -6 to 6
- w_key: bfloat16 [8192, 512], P(('doc', 'seq'), 'tensor'), may hold values from -0.0625 to 0.0625
- w_value: bfloat16 [8192, 512], P(('doc', 'seq'), 'tensor'), may hold values from -0.0625 to 0.0625
- attn_gate: float32 [1], replicated, may hold values from 0.2 to 1.2
- token_image: int32 [4, 16384, 1], P('doc', 'seq'), may hold values from 0 to 63; in each aligned block of 256 rows (0 to 255, 256 to 511, ..., all dimensions but the last counted through in order) at most 8 rows name the same one
- image_owner: int32 [4, 64], P('doc'), may hold values from 0 to 63, each once within a row
- image_len: int32 [4, 64], P('doc', 'seq'), may hold values from 32 to 128, as said below
Outputs:
- gated: bfloat16 [4, 16384, 4096], P('doc', 'seq', 'tensor')
Inputs may be any that keep to these rules, and one draw needn't show every extreme that they name: `token_image`: in each group, the 256 tokens of one index of seq name one image at most 8 times; some image is named exactly 8 times by some index. `image_len`: each group has some image with all 128 vision tokens valid.
All inputs are finite; a program needn't handle non-finite values.
Results may differ from a plain program's by a relative error of at most 0.012.
The roundings to bfloat16 on the way count: a program that leaves them out, or rounds other values in their place, can miss the bound.
Values may be sent and summed in bfloat16 or wider, within the bound.
No kernel may reach another device: no remote copies, remote signals or barrier semaphores. Data moves between devices by JAX's collectives and lax.ppermute only.
A program may use at most 32 MiB of HBM per device.

v0:
```python
import jax
import jax.numpy as jnp
from jax import lax
from jax.sharding import PartitionSpec as P

HD = 128


def head_norm(x):
    return x * lax.rsqrt(jnp.mean(x * x, axis=-1, keepdims=True) + 1e-06)


def shards(queries, vision, w_key, w_value, attn_gate, token_image, image_owner, image_len):
    image = lax.all_gather(vision[0, 0], "tensor", axis=0, tiled=True)
    vtok = image.shape[0]
    width = queries.shape[2]
    kv_width = w_key.shape[1]
    head_size = HD
    heads = width // head_size
    kv_heads = kv_width // head_size
    group_size = heads // kv_heads
    key_part = jnp.dot(
        image,
        lax.all_gather(w_key, ("doc", "seq"), axis=0, tiled=True),
        preferred_element_type=jnp.float32,
    )
    value_part = jnp.dot(
        image,
        lax.all_gather(w_value, ("doc", "seq"), axis=0, tiled=True),
        preferred_element_type=jnp.float32,
    )
    keys = head_norm(key_part.reshape(vtok, kv_heads, head_size)).astype(jnp.bfloat16)
    values = value_part.astype(jnp.bfloat16).reshape(vtok, kv_heads, head_size)
    n_seq = lax.axis_size("seq")
    tok_rows = queries.shape[1]
    capacity = max(8, 2 * tok_rows // n_seq)
    owners = jnp.arange(n_seq, dtype=jnp.int32)
    image_ids = token_image[0, :, 0]
    picked = image_ids[:, None] == owners[None, :]
    target = jnp.sum(jnp.where(picked, image_owner[0][None, :], 0), axis=1)
    onehot = (target[:, None] == owners[None, :]).astype(jnp.int32)
    ranks = jnp.cumsum(onehot, axis=0) - onehot
    place = jnp.sum(ranks * onehot, axis=1)
    flat_slot = target * capacity + place
    dispatch = (
        flat_slot[:, None] == jnp.arange(n_seq * capacity, dtype=jnp.int32)[None, :]
    ).astype(jnp.bfloat16)
    outgoing = jnp.dot(dispatch.T, queries[0], preferred_element_type=jnp.float32).astype(
        jnp.bfloat16
    )
    outgoing = outgoing.reshape(n_seq, capacity, width)
    length = image_len[0, 0]
    factor = jnp.tanh(attn_gate[0])
    scale = head_size ** (-0.5)
    valid = jnp.arange(vtok) < length
    received = lax.all_to_all(outgoing, "seq", split_axis=0, concat_axis=0, tiled=True)
    rows = received.reshape(-1, kv_heads, group_size, head_size)
    scores = jnp.einsum("qcgd,kcd->qcgk", rows, keys, preferred_element_type=jnp.float32) * scale
    scores = jnp.where(valid[None, None, None, :], scores, -jnp.inf)
    top = jnp.max(scores, axis=-1, keepdims=True)
    probs = jnp.exp(scores - top)
    total = jnp.sum(probs, axis=-1)
    mixed = jnp.einsum(
        "qcgk,kcd->qcgd", probs.astype(jnp.bfloat16), values, preferred_element_type=jnp.float32
    )
    answer = (factor * (mixed / total[..., None])).astype(jnp.bfloat16).reshape(received.shape)
    returned = lax.all_to_all(answer, "seq", split_axis=0, concat_axis=0, tiled=True)
    combined = jnp.dot(
        dispatch, returned.reshape(n_seq * capacity, width), preferred_element_type=jnp.float32
    )
    return combined.astype(jnp.bfloat16)[None]


def solution(mesh):
    placed = (
        P("doc", "seq", "tensor"),
        P("doc", "seq", "tensor", None),
        P(("doc", "seq"), "tensor"),
        P(("doc", "seq"), "tensor"),
        P(),
        P("doc", "seq", None),
        P("doc", None),
        P("doc", "seq"),
    )
    return jax.shard_map(
        shards, mesh=mesh, in_specs=placed, out_specs=P("doc", "seq", "tensor"), check_vma=False
    )
```

profile of v0, /device:TPU:1, one launch (start us, length us, event | category | flops | bytes accessed | tf_op | source)
XLA Modules:
  0.0 721.0 jit_solution(16748398952712820415)
XLA Ops:
  6.5 0.0 copy-start
  6.5 0.0 all-gather.9.cloned.1.call-start
  6.5 0.7 all-gather.9.cloned.1.call-update
  7.3 0.8 select_reduce_fusion
  8.1 0.6 reduce-window.6
  8.7 0.2 slice_reduce_fusion
  8.9 0.1 fusion.34
  9.0 0.0 copy-done
  9.0 1.6 fusion.9
  10.6 30.4 %all-to-all-start = ((bf16[64,8,1024]{2,1,0:T(8,128)(2,1)}), bf16[64,8,1024]{2,1,0:T(8,128)(2,1)S(1)}, u32[]{:S(2)}, u32[]{:S(2)}) async-start(bf16[64,8,1024]{2,1,0:T(8,128)(2,1)} %fusion.9), calls=%async_computation | async-start | bytes 2097152 | tf_op jit(solution)/shard_map/all_to_all | solution.py:56
  41.0 0.0 all-gather.7.cloned.1.call-start
  41.1 0.7 all-gather.7.cloned.1.call-update
  41.8 0.0 all-gather.5.cloned.1.call-start
  41.8 0.7 all-gather.5.cloned.1.call-update
  43.8 23.3 %all-gather.9.cloned.1.call-done = bf16[1,1,128,8192]{3,2,1,0:T(8,128)(2,1)} async-done(((bf16[1,1,32,8192]{3,2,1,0:T(8,128)(2,1)}), bf16[1,1,128,8192]{3,2,1,0:T(8,128)(2,1)}) %all-gather.9.cloned.1.call-update) | async-done | bytes 2097168 | tf_op jit(solution)/shard_map/all_gather | solution.py:14
  67.1 270.0 %all-gather.7.cloned.1.call-done = bf16[8192,128]{1,0:T(8,128)(2,1)} async-done(((bf16[32,128]{1,0:T(8,128)(2,1)}), bf16[8192,128]{1,0:T(8,128)(2,1)}) %all-gather.7.cloned.1.call-update) | async-done | bytes 2097168 | tf_op jit(solution)/shard_map/all_gather | solution.py:24
  337.1 3.2 multiply_reduce_fusion
  340.3 0.0 all-to-all-done
  340.3 0.3 copy.20
  340.6 0.6 bitcast_reduce_fusion
  341.2 0.5 fusion.7
  341.7 244.4 %all-gather.5.cloned.1.call-done = bf16[8192,128]{1,0:T(8,128)(2,1)} async-done(((bf16[32,128]{1,0:T(8,128)(2,1)}), bf16[8192,128]{1,0:T(8,128)(2,1)}) %all-gather.5.cloned.1.call-update) | async-done | bytes 2097168 | tf_op jit(solution)/shard_map/all_gather | solution.py:29
  586.1 4.8 fusion.10
  591.0 1.7 copy.15
  592.7 0.5 reshape.87
  593.2 120.0 %all_to_all.10 = bf16[64,8,1024]{2,1,0:T(8,128)(2,1)S(1)} all-to-all(bf16[64,8,1024]{2,1,0:T(8,128)(2,1)S(1)} %reshape.87), channel_id=1, replica_groups=mesh['doc'=4,'seq'=64,'tensor'=4] {'seq'}, dimensions={0} | all-to-all | bytes 2097152 | tf_op jit(solution)/shard_map/all_to_all | solution.py:67
  713.2 1.3 fusion.11
  (6 shorter events, 0.1 us)
Async XLA Ops:
  6.5 2.5 copy-start
  6.5 60.6 %all-gather.9.cloned.1.call-start = ((), (), s32[]{:S(2)}) async-start(), calls=%async_computation.4 | async-start | bytes 2621440 | tf_op jit(solution)/shard_map/all_gather | solution.py:14
  10.6 329.7 %all-to-all-start = ((bf16[64,8,1024]{2,1,0:T(8,128)(2,1)}), bf16[64,8,1024]{2,1,0:T(8,128)(2,1)S(1)}, u32[]{:S(2)}, u32[]{:S(2)}) async-start(bf16[64,8,1024]{2,1,0:T(8,128)(2,1)} %fusion.9), calls=%async_computation | async-start | bytes 2097152 | tf_op jit(solution)/shard_map/all_to_all | solution.py:56
  41.0 296.1 %all-gather.7.cloned.1.call-start = ((), (), s32[]{:S(2)}) async-start(), calls=%async_computation.3 | async-start | bytes 2105344 | tf_op jit(solution)/shard_map/all_gather | solution.py:24
  41.8 544.4 %all-gather.5.cloned.1.call-start = ((), (), s32[]{:S(2)}) async-start(), calls=%async_computation.2 | async-start | bytes 2105344 | tf_op jit(solution)/shard_map/all_gather | solution.py:29
Sparse Core Ops, SparseCore 0:
  10.0 57.0 all-gather.8
  71.3 265.8 all-gather.6
  341.3 244.8 all-gather.4
where the time goes:
time: 723 us; the launch traced here: 721 us
  waiting for transfers between devices  540 us (75%)
  blocking collectives  120 us (17%)
  starting transfers between devices  30.5 us (4%)
  between operations  14.5 us (2%)
  matrix products  11.4 us (2%)
    all_gather x1, waiting for transfers between devices, shards(): lax.all_gather(w_key, ('doc', 'seq'), axis=0, tiled=True)  270 us
    all_gather x1, waiting for transfers between devices, shards(): lax.all_gather(w_value, ('doc', 'seq'), axis=0, tiled=True)  244 us
    all_to_all x1, blocking collectives, shards(): lax.all_to_all(answer, 'seq', split_axis=0, concat_axis=0, tiled=True)  120 us
    all_to_all x1, starting transfers between devices, shards(): lax.all_to_all(outgoing, 'seq', split_axis=0, concat_axis=0, tiled=True)  30.4 us
    all_gather x1, waiting for transfers between devices, shards(): image = lax.all_gather(vision[0, 0], 'tensor', axis=0, tiled=True)  23.3 us
  transfers between devices with their start and end apart: 4, of which 3 were waited for; matrix products, arithmetic and copies ran while one was open for 1% of the time, Pallas kernels for 0%

commit v1 on v0

v1 whole, which is shorter than its diff:
```python
import functools

import jax
import jax.numpy as jnp
from jax import lax
from jax.experimental import pallas as pl
from jax.experimental.pallas import tpu as pltpu
from jax.sharding import PartitionSpec as P

HD = 128
CAP = 8
BF = jnp.bfloat16
F32 = jnp.float32


def head_norm(x):
    return x * lax.rsqrt(jnp.mean(x * x, axis=-1, keepdims=True) + 1e-06)


def attend(lens_ref, gate_ref, q_ref, kv_ref, out_ref):
    heads = q_ref.shape[1] // HD
    vtok = kv_ref.shape[1]
    pairs = kv_ref.shape[0] // 2
    factor = jnp.tanh(jnp.full((1, HD), gate_ref[0], F32))
    shape = (heads * 2 * CAP, 2 * vtok)
    row = lax.broadcasted_iota(jnp.int32, shape, 0)
    col = lax.broadcasted_iota(jnp.int32, shape, 1)
    row_image = (row // CAP) % 2
    first = col < vtok
    key = jnp.where(first, col, col - vtok)
    same = first == (row_image == 0)

    def body(i, carry):
        rows = pl.ds(pl.multiple_of(i * 2 * CAP, 2 * CAP), 2 * CAP)
        q = jnp.concatenate([q_ref[rows, h * HD : (h + 1) * HD] for h in range(heads)], axis=0)
        kv = kv_ref[pl.ds(2 * i, 2)].reshape(2 * vtok, 2 * HD)
        k, v = kv[:, :HD], kv[:, HD:]
        s = lax.dot_general(q, k, (((1,), (1,)), ((), ())), preferred_element_type=F32)
        s = s * (HD ** -0.5)
        length = jnp.where(first, lens_ref[2 * i], lens_ref[2 * i + 1])
        s = jnp.where(same & (key < length), s, -jnp.inf)
        top = jnp.max(s, axis=1, keepdims=True)
        p = jnp.exp(s - top)
        total = jnp.sum(p, axis=1, keepdims=True)
        mixed = jnp.dot(p.astype(BF), v, preferred_element_type=F32)
        ans = (factor * (mixed / total)).astype(BF)
        for h in range(heads):
            out_ref[rows, h * HD : (h + 1) * HD] = ans[h * 2 * CAP : (h + 1) * 2 * CAP]
        return carry

    lax.fori_loop(0, pairs, body, 0)


def attention(lens, gate, q, kv):
    return pl.pallas_call(
        attend,
        out_shape=jax.ShapeDtypeStruct(q.shape, BF),
        in_specs=[
            pl.BlockSpec(memory_space=pltpu.SMEM),
            pl.BlockSpec(memory_space=pltpu.SMEM),
            pl.BlockSpec(memory_space=pltpu.VMEM),
            pl.BlockSpec(memory_space=pltpu.VMEM),
        ],
        out_specs=pl.BlockSpec(memory_space=pltpu.VMEM),
        compiler_params=pltpu.CompilerParams(vmem_limit_bytes=32 * 1024 * 1024),
    )(lens, gate, q, kv)


def chip_shift(n_seq, d):
    return [(i, (i + 2 * d) % n_seq) for i in range(n_seq)]


def shards(queries, vision, w_key, w_value, attn_gate, token_image, image_owner, image_len):
    n_doc = lax.axis_size("doc")
    n_seq = lax.axis_size("seq")
    n_z = n_seq // 2
    seq = lax.axis_index("seq")
    core = seq % 2
    z = seq // 2
    rows32, width = vision.shape[2], vision.shape[3]
    slice_w = width // n_doc
    swap = [(i, i ^ 1) for i in range(n_seq)]

    with jax.named_scope("vision_doc"):
        cols = lax.all_to_all(vision[0, 0], "doc", split_axis=1, concat_axis=0, tiled=True)
    with jax.named_scope("vision_tensor"):
        x = lax.all_gather(cols, "tensor", axis=0, tiled=True)

    wrows = w_key.shape[0]
    w = jnp.concatenate([w_key, w_value], axis=1)
    extra = jnp.broadcast_to(image_len.astype(BF), (16, w.shape[1]))
    packed = jnp.concatenate([w, extra], axis=0)
    groups = [[2 * q + c for q in range(n_z)] for c in range(2)]
    with jax.named_scope("weights_z"):
        own = lax.all_gather(packed, "seq", axis=0, tiled=False, axis_index_groups=groups)
    with jax.named_scope("weights_core"):
        other = lax.ppermute(own, "seq", swap)
    even = jnp.where(core == 0, own, other)
    odd = jnp.where(core == 0, other, own)
    both = jnp.stack([even, odd], axis=1)
    w_all = both[:, :, :wrows].reshape(n_seq * wrows, w.shape[1])
    lens = both[:, :, wrows, 0].reshape(n_seq).astype(jnp.int32)

    with jax.named_scope("project"):
        part = jnp.dot(x, w_all, preferred_element_type=F32)
    with jax.named_scope("reduce_doc"):
        part = part.reshape(-1, n_doc, rows32, w.shape[1])
        part = lax.all_to_all(part, "doc", split_axis=1, concat_axis=1, tiled=True)
        kv = jnp.sum(part, axis=1).reshape(-1, w.shape[1])
    kv = jnp.concatenate([head_norm(kv[:, :HD]), kv[:, HD:]], axis=1).astype(BF)

    with jax.named_scope("kv_far"):
        far = [[2 * (a + 8 * j) + c for j in range(n_z // 8)] for a in range(8) for c in range(2)]
        s0 = lax.all_gather(kv, "seq", axis=0, tiled=False, axis_index_groups=far)
    nj = s0.shape[0]
    with jax.named_scope("kv_mid"):
        p3 = lax.ppermute(s0, "seq", chip_shift(n_seq, -3))
        m3 = lax.ppermute(s0, "seq", chip_shift(n_seq, 3))
    with jax.named_scope("kv_near"):
        h = nj // 2
        up = lax.ppermute(jnp.concatenate([s0, m3, p3[:h]], axis=0), "seq", chip_shift(n_seq, -1))
        dn = lax.ppermute(jnp.concatenate([m3[h:], s0, p3], axis=0), "seq", chip_shift(n_seq, 1))
    mine = jnp.concatenate([s0, p3, m3, up, dn], axis=0)
    classes = [0, 3, 5, 1, 6, 4, 7, 2]
    with jax.named_scope("kv_core"):
        theirs = lax.ppermute(mine, "seq", swap)
    kv_all = jnp.concatenate([mine, theirs], axis=0)

    owners = jnp.arange(n_seq, dtype=jnp.int32)
    oz, oc = owners // 2, owners % 2
    delta = (oz - z) % 8
    place_of = sum(jnp.where(delta == c, i, 0) for i, c in enumerate(classes))
    pos = place_of * nj + oz // 8 + n_z * (oc != core).astype(jnp.int32)
    at = owners[:, None] == pos[None, :]
    lens_at = jnp.sum(jnp.where(at, lens[None, :], 0), axis=1)

    image_ids = token_image[0, :, 0]
    owner_pos = jnp.sum(
        jnp.where(image_owner[0][:, None] == owners[None, :], pos[None, :], 0), axis=1
    )
    picked = image_ids[:, None] == owners[None, :]
    target = jnp.sum(jnp.where(picked, owner_pos[None, :], 0), axis=1)
    onehot = (target[:, None] == owners[None, :]).astype(jnp.int32)
    ranks = jnp.cumsum(onehot, axis=0) - onehot
    slot = target * CAP + jnp.sum(ranks * onehot, axis=1)
    dispatch = (slot[:, None] == jnp.arange(n_seq * CAP, dtype=jnp.int32)[None, :]).astype(BF)
    with jax.named_scope("dispatch"):
        q = jnp.dot(dispatch.T, queries[0], preferred_element_type=F32).astype(BF)
    with jax.named_scope("attention"):
        answer = attention(lens_at, attn_gate, q, kv_all)
    with jax.named_scope("combine"):
        out = jnp.dot(dispatch, answer, preferred_element_type=F32)
    return out.astype(BF)[None]


def solution(mesh):
    placed = (
        P("doc", "seq", "tensor"),
        P("doc", "seq", "tensor", None),
        P(("doc", "seq"), "tensor"),
        P(("doc", "seq"), "tensor"),
        P(),
        P("doc", "seq", None),
        P("doc", None),
        P("doc", "seq"),
    )
    return jax.shard_map(
        shards, mesh=mesh, in_specs=placed, out_specs=P("doc", "seq", "tensor"), check_vma=False
    )
```

time: 723 us -> 260 us (0.36)
  waiting for transfers between devices: 540 us -> 23.6 us
  local copies, waits for them, and re-layouts: 2.67 us -> 29 us
  other arithmetic: 2.08 us -> 19.2 us
  Pallas kernels: 0 us -> 14.8 us
    all_gather x3 -> x1, waiting for transfers between devices: 538 us -> 0.02 us  [shards(): x = lax.all_gather(cols, 'tensor', axis=0, tiled=True)]
    all_to_all x1 -> x2, blocking collectives: 120 us -> 23.5 us  [the longest x1 11.9 us: shards(): lax.all_to_all(vision[0, 0], 'doc', split_axis=1, concat_axis=0, tiled=True)]
    all_gather x0 -> x2, blocking collectives: none -> 92.6 us  [the longest x1 63.2 us: shards(): lax.all_gather(packed, 'seq', axis=0, tiled=False, axis_index_groups=groups)]
    ppermute x0 -> x6, starting transfers between devices: none -> 37.5 us  [the longest x1 14.5 us: shards(): other = lax.ppermute(own, 'seq', swap)]
    all_to_all x1 -> x0, starting transfers between devices: 30.4 us -> none  [shards(): lax.all_to_all(outgoing, 'seq', split_axis=0, concat_axis=0, tiled=True)]
    ppermute x0 -> x6, waiting for transfers between devices: none -> 23.6 us  [the longest x1 8.08 us: shards(): m3 = lax.ppermute(s0, 'seq', chip_shift(n_seq, 3))]
    another operation x2 -> x4, other arithmetic: 0.65 us -> 17 us  [the longest x2 16.4 us: shards(): both = jnp.stack([even, odd], axis=1)]
    pallas_call x0 -> x1, Pallas kernels: none -> 14.8 us  [attention(): pl.pallas_call(attend, out_shape=jax.ShapeDtypeStruct(q.shape, BF), in_sp...]
  transfers between devices with their start and end apart: 4 -> 7, of which waited for: 3 -> 6; matrix products, arithmetic and copies ran while one was open for 1% -> 17% of each run, Pallas kernels for 0% -> 0%
where the time goes in v1:
time: 260 us; the launch traced here: 259 us
  blocking collectives  116 us (45%)
  starting transfers between devices  37.5 us (14%)
  local copies, waits for them, and re-layouts  29 us (11%)
  waiting for transfers between devices  23.6 us (9%)
  other arithmetic  19.2 us (7%)
  between operations  15 us (6%)
  Pallas kernels  14.8 us (6%)
  matrix products  4.18 us (2%)
    all_gather x1, blocking collectives, shards(): lax.all_gather(packed, 'seq', axis=0, tiled=False, axis_index_groups=groups)  63.2 us
    all_gather x1, blocking collectives, shards(): s0 = lax.all_gather(kv, 'seq', axis=0, tiled=False, axis_index_groups=far)  29.4 us
    another operation x2, other arithmetic, shards(): both = jnp.stack([even, odd], axis=1)  16.4 us
    pallas_call x1, Pallas kernels, attention(): pl.pallas_call(attend, out_shape=jax.ShapeDtypeStruct(q.shape, BF), in_sp...  14.8 us
    ppermute x1, starting transfers between devices, shards(): other = lax.ppermute(own, 'seq', swap)  14.5 us
    another operation x2, local copies, waits for them, and re-layouts, shards(): both = jnp.stack([even, odd], axis=1)  13.8 us
    all_to_all x1, blocking collectives, shards(): lax.all_to_all(vision[0, 0], 'doc', split_axis=1, concat_axis=0, tiled=True)  11.9 us
    all_to_all x1, blocking collectives, shards(): part = lax.all_to_all(part, 'doc', split_axis=1, concat_axis=1, tiled=True)  11.6 us
  transfers between devices with their start and end apart: 7, of which 6 were waited for; matrix products, arithmetic and copies ran while one was open for 17% of the time, Pallas kernels for 0%

profile of v1, /device:TPU:1, one launch (start us, length us, event | category | flops | bytes accessed | tf_op | source)
XLA Modules:
  0.0 259.3 jit_solution(16408030567939634150)
XLA Ops:
  6.5 0.0 copy-start
  6.5 0.0 all-gather.3.cloned.1.call-start
  6.5 1.5 all_to_all.17
  8.0 0.3 copy.63
  8.3 11.9 %all_to_all.24 = bf16[32,4,2048]{2,0,1:T(8,128)(2,1)} all-to-all(bf16[32,4,2048]{2,0,1:T(8,128)(2,1)S(1)} %copy.63), channel_id=1, replica_groups=mesh['doc'=4,'seq'=64,'tensor'=4] {'doc'}, dimensions={1} | all-to-all | bytes 1048576 | tf_op jit(solution)/shard_map/vision_doc/all_to_all | solution.py:85
  20.2 0.0 all-gather.3.cloned.1.call-update
  20.9 0.7 fusion.12
  21.6 63.2 %all-gather = bf16[1536,256]{1,0:T(8,128)(2,1)S(1)} all-gather(bf16[48,256]{1,0:T(8,128)(2,1)S(1)} %fusion.12), channel_id=2, replica_groups={{0,8,16,24,32,40,48,56,64,72,80,88,96,104,112,120,128,136,144,152,160,1..., dimensions={0}, use_global_device_ids=true | all-gather | bytes 811008 | tf_op jit(solution)/shard_map/weights_z/all_gather | solution.py:95
  84.8 14.5 %collective-permute-start = (bf16[32,48,256]{2,1,0:T(8,128)(2,1)S(1)}, bf16[32,48,256]{2,1,0:T(8,128)(2,1)}, u32[]{:S(2)}, u32[]{:S(2)}) collective-permute-start(bf16[32,48,256]{2,1,0:T(8,128)(2,1)S(1)} %bitcast.54), channel_id=1, source_target_pairs={{0,4},{4,0},{8,12},{12,8},{16,20},{20,16},{24,28},{28,24},{32,36},... | collective-permute-start | bytes 2359304 | tf_op jit(solution)/shard_map/weights_core/ppermute | solution.py:97
  99.3 2.0 collective-permute-done
  101.3 1.2 select_bitcast_fusion.1
  102.5 6.9 %copy.60 = bf16[32,1,48,256]{0,1,3,2:T(2,128)(2,1)} copy(bf16[32,1,48,256]{3,2,0,1:T(8,128)(2,1)S(1)} %get-tuple-element.8) | data formatting | bytes 1572864 | tf_op jit(solution)/shard_map/stack | solution.py:100
  109.5 6.9 %copy.59 = bf16[32,1,48,256]{0,1,3,2:T(2,128)(2,1)} copy(bf16[32,1,48,256]{3,2,0,1:T(8,128)(2,1)S(1)} %get-tuple-element.7) | data formatting | bytes 1572864 | tf_op jit(solution)/shard_map/stack | solution.py:100
  116.3 15.1 %pad_maximum_fusion = bf16[32,2,32,256]{0,1,3,2:T(2,128)(2,1)} fusion(bf16[32,1,48,256]{0,1,3,2:T(2,128)(2,1)} %copy.60, bf16[32,1,48,256]{0,1,3,2:T(2,128)(2,1)} %copy.59), kind=kLoop, calls=%fused_computation | loop fusion | flops 2097152 | bytes 2621440 | tf_op jit(solution)/shard_map/stack | solution.py:100
  131.5 6.2 %copy.62 = bf16[32,2,32,256]{3,2,1,0:T(8,128)(2,1)S(1)} copy(bf16[32,2,32,256]{0,1,3,2:T(2,128)(2,1)} %pad_maximum_fusion) | data formatting | bytes 2097152 | tf_op jit(solution)/shard_map/slice | solution.py:101
  137.7 0.0 all-gather.3.cloned.1.call-done
  137.8 2.3 convolution_bitcast_fusion
  140.1 0.2 copy.64
  140.3 11.6 %all_to_all.25 = f32[4,4,32,256]{3,2,0,1:T(8,128)S(1)} all-to-all(f32[4,4,32,256]{3,2,0,1:T(8,128)S(1)} %copy.65), channel_id=1, replica_groups=mesh['doc'=4,'seq'=64,'tensor'=4] {'doc'}, dimensions={1} | all-to-all | bytes 1048576 | tf_op jit(solution)/shard_map/reduce_doc/all_to_all | solution.py:108
  152.0 0.1 multiply_reduce_fusion
  152.1 0.1 fusion.10
  152.3 29.4 %all_gather.16 = bf16[4,128,256]{2,1,0:T(8,128)(2,1)S(1)} all-gather(bf16[1,128,256]{2,1,0:T(8,128)(2,1)S(1)} %pad_maximum_fusion.3), channel_id=1, replica_groups={{0,64,128,192},{4,68,132,196},{8,72,136,200},{12,76,140,204},{16,80,144..., dimensions={0}, use_global_device_ids=true | all-gather | bytes 327680 | tf_op jit(solution)/shard_map/kv_far/all_gather | solution.py:114
  181.7 1.9 collective-permute-start.2
  183.6 6.4 %collective-permute-start.1 = (bf16[4,128,256]{2,1,0:T(8,128)(2,1)S(1)}, bf16[4,128,256]{2,1,0:T(8,128)(2,1)S(1)}, u32[]{:S(2)}, u32[]{:S(2)}) collective-permute-start(bf16[4,128,256]{2,1,0:T(8,128)(2,1)S(1)} %all_gather.16), channel_id=1, source_target_pairs={{0,232},{4,236},{8,240},{12,244},{16,248},{20,252},{24,0},{28,4},{... | collective-permute-start | bytes 786440 | tf_op jit(solution)/shard_map/kv_mid/ppermute | solution.py:117
  190.0 8.1 %collective-permute-done.2 = bf16[4,128,256]{2,1,0:T(8,128)(2,1)S(1)} collective-permute-done((bf16[4,128,256]{2,1,0:T(8,128)(2,1)S(1)}, bf16[4,128,256]{2,1,0:T(8,128)(2,1)S(1)}, u32[]{:S(2)}, u32[]{:S(2)}) %collective-permute-start.2) | collective-permute-done | bytes 262176 | tf_op jit(solution)/shard_map/kv_mid/ppermute | solution.py:118
  198.1 1.3 collective-permute-done.1
  199.4 0.1 pad_maximum_fusion.2
  199.5 5.5 %collective-permute-start.3 = (bf16[10,128,256]{2,1,0:T(8,128)(2,1)S(1)}, bf16[10,128,256]{2,1,0:T(8,128)(2,1)S(1)}, u32[]{:S(2)}, u32[]{:S(2)}) collective-permute-start(bf16[10,128,256]{2,1,0:T(8,128)(2,1)S(1)} %get-tuple-element.20), channel_id=1, source_target_pairs={{0,248},{4,252},{8,0},{12,4},{16,8},{20,12},{24,16},{28,20},{32,24... | collective-permute-start | bytes 1966088 | tf_op jit(solution)/shard_map/kv_near/ppermute | solution.py:121
  205.0 2.8 %collective-permute-start.4 = (bf16[10,128,256]{2,1,0:T(8,128)(2,1)S(1)}, bf16[10,128,256]{2,1,0:T(8,128)(2,1)S(1)}, u32[]{:S(2)}, u32[]{:S(2)}) collective-permute-start(bf16[10,128,256]{2,1,0:T(8,128)(2,1)S(1)} %get-tuple-element.19), channel_id=1, source_target_pairs={{0,8},{4,12},{8,16},{12,20},{16,24},{20,28},{24,32},{28,36},{32,40... | collective-permute-start | bytes 1966088 | tf_op jit(solution)/shard_map/kv_near/ppermute | solution.py:122
  207.8 0.8 constant_dynamic-update-slice_fusion.4
  208.7 0.8 constant_dynamic-update-slice_fusion.3
  209.5 0.8 constant_dynamic-update-slice_fusion.2
  210.3 6.1 %collective-permute-done.3 = bf16[10,128,256]{2,1,0:T(8,128)(2,1)S(1)} collective-permute-done((bf16[10,128,256]{2,1,0:T(8,128)(2,1)S(1)}, bf16[10,128,256]{2,1,0:T(8,128)(2,1)S(1)}, u32[]{:S(2)}, u32[]{:S(2)}) %collective-permute-start.3) | collective-permute-done | bytes 655392 | tf_op jit(solution)/shard_map/kv_near/ppermute | solution.py:121
  216.5 1.2 constant_dynamic-update-slice_fusion.1
  217.7 5.5 %collective-permute-done.4 = bf16[10,128,256]{2,1,0:T(8,128)(2,1)S(1)} collective-permute-done((bf16[10,128,256]{2,1,0:T(8,128)(2,1)S(1)}, bf16[10,128,256]{2,1,0:T(8,128)(2,1)S(1)}, u32[]{:S(2)}, u32[]{:S(2)}) %collective-permute-start.4) | collective-permute-done | bytes 655392 | tf_op jit(solution)/shard_map/kv_near/ppermute | solution.py:122
  223.2 1.3 constant_dynamic-update-slice_fusion
  224.5 6.5 %collective-permute-start.5 = (bf16[32,128,256]{2,1,0:T(8,128)(2,1)}, bf16[32,128,256]{2,1,0:T(8,128)(2,1)S(1)}, u32[]{:S(2)}, u32[]{:S(2)}) collective-permute-start(bf16[32,128,256]{2,1,0:T(8,128)(2,1)} %get-tuple-element.9), channel_id=1, source_target_pairs={{0,4},{4,0},{8,12},{12,8},{16,20},{20,16},{24,28},{28,24},{32,36},... | collective-permute-start | bytes 6291464 | tf_op jit(solution)/shard_map/kv_core/ppermute | solution.py:126
  231.7 0.0 copy-start.2
  231.7 0.0 copy-start.1
  231.7 0.7 maximum_convert_fusion
  232.4 0.1 copy.61
  232.5 0.1 reshape.160
  232.6 0.0 copy-done.2
  232.6 0.2 select_reduce_fusion.2
  232.7 0.0 copy-done.1
  232.8 0.1 select_reduce_fusion
  232.9 0.6 reduce-window.6
  233.5 0.2 slice_reduce_fusion
  233.7 0.1 fusion.6
  233.8 0.0 copy-done
  233.8 0.6 convolution_convert_fusion.q_ref
  234.4 0.5 collective-permute-done.5
  234.9 1.5 constant_dynamic-update-slice_fusion.5.kv_ref
  236.4 14.8 %attention.1 = bf16[512,1024]{1,0:T(8,128)(2,1)S(1)} custom-call(s32[64]{0:T(128)S(1)} %get-tuple-element.6.lens_ref, f32[1]{0:T(128)S(6)} %copy.77.gate_ref, bf16[512,1024]{1,0:T(8,128)(2,1)S(1)} %convolution_convert_fusion.q_ref, bf16[64,128,256]{2,1,0:T(8,128)(2,1)} %constant_dynamic-update-slice_fusion.5.kv_ref), custom_call_target="tpu_custom_call" | custom-call | tf_op jit(solution)/shard_map/attention/pallas_call | solution.py:55
  251.2 1.3 fusion
  (12 shorter events, 0.2 us)
Async XLA Ops:
  6.5 227.3 %copy-start = (bf16[1,256,1024]{2,1,0:T(8,128)(2,1)S(1)}, bf16[1,256,1024]{2,1,0:T(8,128)(2,1)}, u32[]{:S(2)}) copy-start(bf16[1,256,1024]{2,1,0:T(8,128)(2,1)} %param.8) | copy-start | bytes 1572868
  6.5 131.2 %all-gather.3.cloned.1.call-start = ((), (), s32[]{:S(2)}) async-start(), calls=%async_computation.2 | async-start | bytes 2621440 | tf_op jit(solution)/shard_map/vision_tensor/all_gather | solution.py:87
  84.8 16.5 %collective-permute-start = (bf16[32,48,256]{2,1,0:T(8,128)(2,1)S(1)}, bf16[32,48,256]{2,1,0:T(8,128)(2,1)}, u32[]{:S(2)}, u32[]{:S(2)}) collective-permute-start(bf16[32,48,256]{2,1,0:T(8,128)(2,1)S(1)} %bitcast.54), channel_id=1, source_target_pairs={{0,4},{4,0},{8,12},{12,8},{16,20},{20,16},{24,28},{28,24},{32,36},... | collective-permute-start | bytes 2359304 | tf_op jit(solution)/shard_map/weights_core/ppermute | solution.py:97
  181.7 16.4 %collective-permute-start.2 = (bf16[4,128,256]{2,1,0:T(8,128)(2,1)S(1)}, bf16[4,128,256]{2,1,0:T(8,128)(2,1)S(1)}, u32[]{:S(2)}, u32[]{:S(2)}) collective-permute-start(bf16[4,128,256]{2,1,0:T(8,128)(2,1)S(1)} %all_gather.16), channel_id=1, source_target_pairs={{0,24},{4,28},{8,32},{12,36},{16,40},{20,44},{24,48},{28,52},{32,5... | collective-permute-start | bytes 786440 | tf_op jit(solution)/shard_map/kv_mid/ppermute | solution.py:118
  183.6 15.8 %collective-permute-start.1 = (bf16[4,128,256]{2,1,0:T(8,128)(2,1)S(1)}, bf16[4,128,256]{2,1,0:T(8,128)(2,1)S(1)}, u32[]{:S(2)}, u32[]{:S(2)}) collective-permute-start(bf16[4,128,256]{2,1,0:T(8,128)(2,1)S(1)} %all_gather.16), channel_id=1, source_target_pairs={{0,232},{4,236},{8,240},{12,244},{16,248},{20,252},{24,0},{28,4},{... | collective-permute-start | bytes 786440 | tf_op jit(solution)/shard_map/kv_mid/ppermute | solution.py:117
  199.5 16.9 %collective-permute-start.3 = (bf16[10,128,256]{2,1,0:T(8,128)(2,1)S(1)}, bf16[10,128,256]{2,1,0:T(8,128)(2,1)S(1)}, u32[]{:S(2)}, u32[]{:S(2)}) collective-permute-start(bf16[10,128,256]{2,1,0:T(8,128)(2,1)S(1)} %get-tuple-element.20), channel_id=1, source_target_pairs={{0,248},{4,252},{8,0},{12,4},{16,8},{20,12},{24,16},{28,20},{32,24... | collective-permute-start | bytes 1966088 | tf_op jit(solution)/shard_map/kv_near/ppermute | solution.py:121
  205.0 18.2 %collective-permute-start.4 = (bf16[10,128,256]{2,1,0:T(8,128)(2,1)S(1)}, bf16[10,128,256]{2,1,0:T(8,128)(2,1)S(1)}, u32[]{:S(2)}, u32[]{:S(2)}) collective-permute-start(bf16[10,128,256]{2,1,0:T(8,128)(2,1)S(1)} %get-tuple-element.19), channel_id=1, source_target_pairs={{0,8},{4,12},{8,16},{12,20},{16,24},{20,28},{24,32},{28,36},{32,40... | collective-permute-start | bytes 1966088 | tf_op jit(solution)/shard_map/kv_near/ppermute | solution.py:122
  224.5 10.4 %collective-permute-start.5 = (bf16[32,128,256]{2,1,0:T(8,128)(2,1)}, bf16[32,128,256]{2,1,0:T(8,128)(2,1)S(1)}, u32[]{:S(2)}, u32[]{:S(2)}) collective-permute-start(bf16[32,128,256]{2,1,0:T(8,128)(2,1)} %get-tuple-element.9), channel_id=1, source_target_pairs={{0,4},{4,0},{8,12},{12,8},{16,20},{20,16},{24,28},{28,24},{32,36},... | collective-permute-start | bytes 6291464 | tf_op jit(solution)/shard_map/kv_core/ppermute | solution.py:126
  231.7 0.9 copy-start.2
  231.7 1.1 copy-start.1
Sparse Core Ops, SparseCore 0:
  20.3 56.9 all-gather.2

commit v2 on v1

--- a/solution.py
+++ b/solution.py
@@ -17,38 +17,69 @@
     return x * lax.rsqrt(jnp.mean(x * x, axis=-1, keepdims=True) + 1e-06)
 
 
+def project(place_ref, x_ref, own_ref, other_ref, out_ref, w_ref):
+    rows = w_ref.shape[0] // (own_ref.shape[0] * 2)
+    half = own_ref.shape[0] // 2
+    core, odd = place_ref[0], place_ref[1]
+    for k, ref in enumerate((own_ref, other_ref)):
+        for o in range(2):
+            for j in range(half):
+                owner = 2 * (2 * j + (o + odd) % 2) + (k + core) % 2
+                at = pl.ds(pl.multiple_of(owner * rows, rows), rows)
+                w_ref[at] = ref[o * half + j, :rows]
+    out_ref[...] = jnp.dot(x_ref[...], w_ref[...], preferred_element_type=F32)
+
+
+def projection(place, x, own, other):
+    cols = own.shape[2]
+    return pl.pallas_call(
+        project,
+        out_shape=jax.ShapeDtypeStruct((x.shape[0], cols), F32),
+        in_specs=[pl.BlockSpec(memory_space=pltpu.SMEM)]
+        + [pl.BlockSpec(memory_space=pltpu.VMEM)] * 3,
+        out_specs=pl.BlockSpec(memory_space=pltpu.VMEM),
+        scratch_shapes=[pltpu.VMEM((x.shape[1], cols), BF)],
+        compiler_params=pltpu.CompilerParams(vmem_limit_bytes=32 * 1024 * 1024),
+    )(place, x, own, other)
+
+
+UNROLL = 4
+
+
 def attend(lens_ref, gate_ref, q_ref, kv_ref, out_ref):
     heads = q_ref.shape[1] // HD
     vtok = kv_ref.shape[1]
     pairs = kv_ref.shape[0] // 2
-    factor = jnp.tanh(jnp.full((1, HD), gate_ref[0], F32))
-    shape = (heads * 2 * CAP, 2 * vtok)
-    row = lax.broadcasted_iota(jnp.int32, shape, 0)
-    col = lax.broadcasted_iota(jnp.int32, shape, 1)
-    row_image = (row // CAP) % 2
-    first = col < vtok
-    key = jnp.where(first, col, col - vtok)
-    same = first == (row_image == 0)
-
-    def body(i, carry):
+    factor = jnp.tanh(jnp.full((1, 1), gate_ref[0], F32))
+    col = lax.broadcasted_iota(jnp.int32, (1, 2 * vtok), 1)
+
+    def one(i):
         rows = pl.ds(pl.multiple_of(i * 2 * CAP, 2 * CAP), 2 * CAP)
         q = jnp.concatenate([q_ref[rows, h * HD : (h + 1) * HD] for h in range(heads)], axis=0)
         kv = kv_ref[pl.ds(2 * i, 2)].reshape(2 * vtok, 2 * HD)
         k, v = kv[:, :HD], kv[:, HD:]
         s = lax.dot_general(q, k, (((1,), (1,)), ((), ())), preferred_element_type=F32)
-        s = s * (HD ** -0.5)
-        length = jnp.where(first, lens_ref[2 * i], lens_ref[2 * i + 1])
-        s = jnp.where(same & (key < length), s, -jnp.inf)
+        s = s.reshape(heads, 2, CAP, 2 * vtok) * (HD ** -0.5)
+        last = vtok + lens_ref[2 * i + 1]
+        ok0 = col < lens_ref[2 * i]
+        ok1 = (col >= vtok) & (col < last)
+        s0 = jnp.where(ok0[None], s[:, 0], -jnp.inf)
+        s1 = jnp.where(ok1[None], s[:, 1], -jnp.inf)
+        s = jnp.stack([s0, s1], axis=1).reshape(heads * 2 * CAP, 2 * vtok)
         top = jnp.max(s, axis=1, keepdims=True)
         p = jnp.exp(s - top)
         total = jnp.sum(p, axis=1, keepdims=True)
         mixed = jnp.dot(p.astype(BF), v, preferred_element_type=F32)
-        ans = (factor * (mixed / total)).astype(BF)
+        ans = (mixed * (factor / total)).astype(BF)
         for h in range(heads):
             out_ref[rows, h * HD : (h + 1) * HD] = ans[h * 2 * CAP : (h + 1) * 2 * CAP]
+
+    def body(i, carry):
+        for u in range(UNROLL):
+            one(i * UNROLL + u)
         return carry
 
-    lax.fori_loop(0, pairs, body, 0)
+    lax.fori_loop(0, pairs // UNROLL, body, 0)
 
 
 def attention(lens, gate, q, kv):
@@ -90,19 +121,16 @@
     w = jnp.concatenate([w_key, w_value], axis=1)
     extra = jnp.broadcast_to(image_len.astype(BF), (16, w.shape[1]))
     packed = jnp.concatenate([w, extra], axis=0)
-    groups = [[2 * q + c for q in range(n_z)] for c in range(2)]
+    groups = [[2 * (2 * j + o) + c for j in range(n_z // 2)] for o in range(2) for c in range(2)]
     with jax.named_scope("weights_z"):
-        own = lax.all_gather(packed, "seq", axis=0, tiled=False, axis_index_groups=groups)
+        near = lax.all_gather(packed, "seq", axis=0, tiled=False, axis_index_groups=groups)
+    with jax.named_scope("weights_pair"):
+        beside = lax.ppermute(near, "seq", [(i, i ^ 2) for i in range(n_seq)])
+    own = jnp.concatenate([near, beside], axis=0)
     with jax.named_scope("weights_core"):
         other = lax.ppermute(own, "seq", swap)
-    even = jnp.where(core == 0, own, other)
-    odd = jnp.where(core == 0, other, own)
-    both = jnp.stack([even, odd], axis=1)
-    w_all = both[:, :, :wrows].reshape(n_seq * wrows, w.shape[1])
-    lens = both[:, :, wrows, 0].reshape(n_seq).astype(jnp.int32)
-
     with jax.named_scope("project"):
-        part = jnp.dot(x, w_all, preferred_element_type=F32)
+        part = projection(jnp.stack([core, z % 2]), x, own, other)
     with jax.named_scope("reduce_doc"):
         part = part.reshape(-1, n_doc, rows32, w.shape[1])
         part = lax.all_to_all(part, "doc", split_axis=1, concat_axis=1, tiled=True)
@@ -132,6 +160,9 @@
     place_of = sum(jnp.where(delta == c, i, 0) for i, c in enumerate(classes))
     pos = place_of * nj + oz // 8 + n_z * (oc != core).astype(jnp.int32)
     at = owners[:, None] == pos[None, :]
+    lens = jnp.concatenate([own[:, wrows, 0], other[:, wrows, 0]]).astype(jnp.int32)
+    from_w = n_z * (oc != core).astype(jnp.int32) + (n_z // 2) * ((oz - z) % 2) + oz // 2
+    lens = jnp.sum(jnp.where(from_w[:, None] == owners[None, :], lens[None, :], 0), axis=1)
     lens_at = jnp.sum(jnp.where(at, lens[None, :], 0), axis=1)
 
     image_ids = token_image[0, :, 0]

time: 260 us -> 207 us (0.80); the launches traced: 259 us -> 203 us
  blocking collectives: 116 us -> 97 us
  local copies, waits for them, and re-layouts: 29 us -> 11.9 us
  other arithmetic: 19.2 us -> 2.19 us
  Pallas kernels: 14.8 us -> 9.15 us
  starting transfers between devices: 37.5 us -> 42.7 us
    all_gather x1, blocking collectives: 63.2 us -> 44 us  [shards(): lax.all_gather(packed, 'seq', axis=0, tiled=False, axis_index_groups=groups)]
    another operation x4 -> x3, other arithmetic: 17 us -> 0.72 us  [the longest x2 16.4 us: shards(): both = jnp.stack([even, odd], axis=1)]
    another operation x3 -> x1, local copies, waits for them, and re-layouts: 13.8 us -> 0.01 us  [the longest x2 13.8 us: shards(): both = jnp.stack([even, odd], axis=1)]
    pallas_call x1, Pallas kernels: 14.8 us -> 7.81 us  [attention(): pl.pallas_call(attend, out_shape=jax.ShapeDtypeStruct(q.shape, BF), in_sp...]
    slice x2, local copies, waits for them, and re-layouts: 6.41 us -> 0.51 us  [the longest x1 0.32 us: shards(): other[:, wrows, 0]]
    ppermute x0 -> x1, waiting for transfers between devices: none -> 5.55 us  [shards(): beside = lax.ppermute(near, 'seq', [(i, i ^ 2) for i in range(n_seq)])]
    ppermute x1, waiting for transfers between devices: 5.52 us -> 0.01 us  [shards(): lax.ppermute(jnp.concatenate([m3[h:], s0, p3], axis=0), 'seq', chip_shift...]
    ppermute x1, waiting for transfers between devices: 1.31 us -> 6.68 us  [shards(): p3 = lax.ppermute(s0, 'seq', chip_shift(n_seq, -3))]
  transfers between devices with their start and end apart: 7 -> 8, of which waited for: 6 -> 6; matrix products, arithmetic and copies ran while one was open for 17% -> 3% of each run, Pallas kernels for 0% -> 0%
where the time goes in v2:
time: 207 us; the launch traced here: 203 us
  blocking collectives  97 us (47%)
  starting transfers between devices  42.7 us (21%)
  waiting for transfers between devices  23.1 us (11%)
  between operations  15 us (7%)
  local copies, waits for them, and re-layouts  11.9 us (6%)
  Pallas kernels  9.15 us (4%)
  other arithmetic  2.19 us (1%)
    all_gather x1, blocking collectives, shards(): lax.all_gather(packed, 'seq', axis=0, tiled=False, axis_index_groups=groups)  44 us
    all_gather x1, blocking collectives, shards(): s0 = lax.all_gather(kv, 'seq', axis=0, tiled=False, axis_index_groups=far)  29.9 us
    all_to_all x1, blocking collectives, shards(): lax.all_to_all(vision[0, 0], 'doc', split_axis=1, concat_axis=0, tiled=True)  11.9 us
    ppermute x1, starting transfers between devices, shards(): other = lax.ppermute(own, 'seq', swap)  11.3 us
    all_to_all x1, blocking collectives, shards(): part = lax.all_to_all(part, 'doc', split_axis=1, concat_axis=1, tiled=True)  11.3 us
    ppermute x1, starting transfers between devices, shards(): theirs = lax.ppermute(mine, 'seq', swap)  8.58 us
    pallas_call x1, Pallas kernels, attention(): pl.pallas_call(attend, out_shape=jax.ShapeDtypeStruct(q.shape, BF), in_sp...  7.81 us
    ppermute x1, waiting for transfers between devices, shards(): p3 = lax.ppermute(s0, 'seq', chip_shift(n_seq, -3))  6.68 us
  transfers between devices with their start and end apart: 8, of which 6 were waited for; matrix products, arithmetic and copies ran while one was open for 3% of the time, Pallas kernels for 0%

profile of v2, /device:TPU:1, one launch (start us, length us, event | category | flops | bytes accessed | tf_op | source)
XLA Modules:
  0.0 202.9 jit_solution(17950150143805063374)
XLA Ops:
  6.5 0.0 copy-start
  6.5 0.0 copy-start.2
  6.5 0.0 copy-start.3
  6.5 0.0 all-gather.3.cloned.1.call-start
  6.5 1.5 all_to_all.17
  8.0 0.3 copy.16
  8.3 11.9 %all_to_all.24 = bf16[32,4,2048]{2,0,1:T(8,128)(2,1)} all-to-all(bf16[32,4,2048]{2,0,1:T(8,128)(2,1)S(1)} %copy.16), channel_id=1, replica_groups=mesh['doc'=4,'seq'=64,'tensor'=4] {'doc'}, dimensions={1} | all-to-all | bytes 1048576 | tf_op jit(solution)/shard_map/vision_doc/all_to_all | solution.py:116
  20.2 0.0 all-gather.3.cloned.1.call-update
  20.9 0.0 copy-done.2
  20.9 0.0 copy-done.3
  20.9 44.0 %all-gather = bf16[768,256]{1,0:T(8,128)(2,1)S(1)} all-gather(bf16[48,256]{1,0:T(8,128)(2,1)S(1)} %fusion.12), channel_id=2, replica_groups={{0,16,32,48,64,80,96,112,128,144,160,176,192,208,224,240},{4,20,36,52,6..., dimensions={0}, use_global_device_ids=true | all-gather | bytes 417792 | tf_op jit(solution)/shard_map/weights_z/all_gather | solution.py:126
  64.9 3.9 %collective-permute-start = (bf16[16,48,256]{2,1,0:T(8,128)(2,1)S(1)}, bf16[16,48,256]{2,1,0:T(8,128)(2,1)S(1)}, u32[]{:S(2)}, u32[]{:S(2)}) collective-permute-start(bf16[16,48,256]{2,1,0:T(8,128)(2,1)S(1)} %bitcast.44), channel_id=1, source_target_pairs={{0,8},{4,12},{8,0},{12,4},{16,24},{20,28},{24,16},{28,20},{32,40},... | collective-permute-start | bytes 1179656 | tf_op jit(solution)/shard_map/weights_pair/ppermute | solution.py:128
  68.8 5.6 %collective-permute-done = bf16[16,48,256]{2,1,0:T(8,128)(2,1)S(1)} collective-permute-done((bf16[16,48,256]{2,1,0:T(8,128)(2,1)S(1)}, bf16[16,48,256]{2,1,0:T(8,128)(2,1)S(1)}, u32[]{:S(2)}, u32[]{:S(2)}) %collective-permute-start) | collective-permute-done | bytes 393248 | tf_op jit(solution)/shard_map/weights_pair/ppermute | solution.py:128
  74.4 0.1 pad_maximum_fusion.own_ref
  74.4 11.3 %collective-permute-start.1 = (bf16[32,48,256]{2,1,0:T(8,128)(2,1)S(1)}, bf16[32,48,256]{2,1,0:T(8,128)(2,1)S(1)}, u32[]{:S(2)}, u32[]{:S(2)}) collective-permute-start(bf16[32,48,256]{2,1,0:T(8,128)(2,1)S(1)} %pad_maximum_fusion.own_ref), channel_id=1, source_target_pairs={{0,4},{4,0},{8,12},{12,8},{16,20},{20,16},{24,28},{28,24},{32,36},... | collective-permute-start | bytes 2359304 | tf_op jit(solution)/shard_map/weights_core/ppermute | solution.py:131
  85.8 0.1 pad_add_fusion.place_ref
  85.8 1.8 collective-permute-done.1.other_ref
  87.6 0.0 all-gather.3.cloned.1.call-done.x_ref
  87.6 0.0 copy-start.1
  87.6 1.6 copy-done.1
  89.2 1.3 project.1
  90.6 11.3 %all_to_all.25 = f32[4,4,32,256]{3,2,0,1:T(8,128)S(1)} all-to-all(f32[4,4,32,256]{3,2,0,1:T(8,128)S(1)} %copy.17), channel_id=1, replica_groups=mesh['doc'=4,'seq'=64,'tensor'=4] {'doc'}, dimensions={1} | all-to-all | bytes 1048576 | tf_op jit(solution)/shard_map/reduce_doc/all_to_all | solution.py:136
  101.9 0.1 multiply_reduce_fusion
  102.1 0.1 fusion.10
  102.2 29.9 %all_gather.16 = bf16[4,128,256]{2,1,0:T(8,128)(2,1)S(1)} all-gather(bf16[1,128,256]{2,1,0:T(8,128)(2,1)S(1)} %pad_maximum_fusion.3), channel_id=1, replica_groups={{0,64,128,192},{4,68,132,196},{8,72,136,200},{12,76,140,204},{16,80,144..., dimensions={0}, use_global_device_ids=true | all-gather | bytes 327680 | tf_op jit(solution)/shard_map/kv_far/all_gather | solution.py:142
  132.0 1.9 collective-permute-start.3
  134.0 6.4 %collective-permute-start.2 = (bf16[4,128,256]{2,1,0:T(8,128)(2,1)S(1)}, bf16[4,128,256]{2,1,0:T(8,128)(2,1)S(1)}, u32[]{:S(2)}, u32[]{:S(2)}) collective-permute-start(bf16[4,128,256]{2,1,0:T(8,128)(2,1)S(1)} %all_gather.16), channel_id=1, source_target_pairs={{0,232},{4,236},{8,240},{12,244},{16,248},{20,252},{24,0},{28,4},{... | collective-permute-start | bytes 786440 | tf_op jit(solution)/shard_map/kv_mid/ppermute | solution.py:145
  140.3 3.1 %collective-permute-done.3 = bf16[4,128,256]{2,1,0:T(8,128)(2,1)S(1)} collective-permute-done((bf16[4,128,256]{2,1,0:T(8,128)(2,1)S(1)}, bf16[4,128,256]{2,1,0:T(8,128)(2,1)S(1)}, u32[]{:S(2)}, u32[]{:S(2)}) %collective-permute-start.3) | collective-permute-done | bytes 262176 | tf_op jit(solution)/shard_map/kv_mid/ppermute | solution.py:146
  143.5 6.7 %collective-permute-done.2 = bf16[4,128,256]{2,1,0:T(8,128)(2,1)S(1)} collective-permute-done((bf16[4,128,256]{2,1,0:T(8,128)(2,1)S(1)}, bf16[4,128,256]{2,1,0:T(8,128)(2,1)S(1)}, u32[]{:S(2)}, u32[]{:S(2)}) %collective-permute-start.2) | collective-permute-done | bytes 262176 | tf_op jit(solution)/shard_map/kv_mid/ppermute | solution.py:145
  150.2 0.1 pad_maximum_fusion.2
  150.3 4.1 %collective-permute-start.4 = (bf16[10,128,256]{2,1,0:T(8,128)(2,1)S(1)}, bf16[10,128,256]{2,1,0:T(8,128)(2,1)S(1)}, u32[]{:S(2)}, u32[]{:S(2)}) collective-permute-start(bf16[10,128,256]{2,1,0:T(8,128)(2,1)S(1)} %get-tuple-element.18), channel_id=1, source_target_pairs={{0,248},{4,252},{8,0},{12,4},{16,8},{20,12},{24,16},{28,20},{32,24... | collective-permute-start | bytes 1966088 | tf_op jit(solution)/shard_map/kv_near/ppermute | solution.py:149
  154.4 6.7 %collective-permute-start.5 = (bf16[10,128,256]{2,1,0:T(8,128)(2,1)S(1)}, bf16[10,128,256]{2,1,0:T(8,128)(2,1)S(1)}, u32[]{:S(2)}, u32[]{:S(2)}) collective-permute-start(bf16[10,128,256]{2,1,0:T(8,128)(2,1)S(1)} %get-tuple-element.17), channel_id=1, source_target_pairs={{0,8},{4,12},{8,16},{12,20},{16,24},{20,28},{24,32},{28,36},{32,40... | collective-permute-start | bytes 1966088 | tf_op jit(solution)/shard_map/kv_near/ppermute | solution.py:150
  161.0 0.8 constant_dynamic-update-slice_fusion.4
  161.8 0.8 constant_dynamic-update-slice_fusion.3
  162.7 0.8 constant_dynamic-update-slice_fusion.2
  163.5 5.2 %collective-permute-done.4 = bf16[10,128,256]{2,1,0:T(8,128)(2,1)S(1)} collective-permute-done((bf16[10,128,256]{2,1,0:T(8,128)(2,1)S(1)}, bf16[10,128,256]{2,1,0:T(8,128)(2,1)S(1)}, u32[]{:S(2)}, u32[]{:S(2)}) %collective-permute-start.4) | collective-permute-done | bytes 655392 | tf_op jit(solution)/shard_map/kv_near/ppermute | solution.py:149
  168.7 0.0 copy-start.5
  168.7 0.0 copy-start.4
  168.7 1.2 constant_dynamic-update-slice_fusion.1
  169.9 0.0 collective-permute-done.5
  169.9 1.2 constant_dynamic-update-slice_fusion
  171.1 8.6 %collective-permute-start.6 = (bf16[32,128,256]{2,1,0:T(8,128)(2,1)}, bf16[32,128,256]{2,1,0:T(8,128)(2,1)}, u32[]{:S(2)}, u32[]{:S(2)}) collective-permute-start(bf16[32,128,256]{2,1,0:T(8,128)(2,1)} %get-tuple-element.7), channel_id=1, source_target_pairs={{0,4},{4,0},{8,12},{12,8},{16,20},{20,16},{24,28},{28,24},{32,36},... | collective-permute-start | bytes 6291464 | tf_op jit(solution)/shard_map/kv_core/ppermute | solution.py:154
  180.4 0.3 fusion.14
  180.7 0.3 slice_reduce_fusion.1
  181.1 0.1 maximum_convert_fusion
  181.1 0.2 select_reduce_fusion.2
  181.3 0.0 copy-done.5
  181.3 0.2 select_reduce_fusion.3
  181.5 0.0 copy-done.4
  181.5 0.1 select_reduce_fusion
  181.6 0.6 reduce-window.6
  182.2 0.2 slice_reduce_fusion
  182.5 0.1 fusion.6
  182.6 0.0 copy-done
  182.6 0.6 convolution_convert_fusion.q_ref
  183.1 0.7 collective-permute-done.6
  183.8 3.1 %constant_dynamic-update-slice_fusion.5.kv_ref = bf16[64,128,256]{2,1,0:T(8,128)(2,1)} fusion(bf16[64,128,256]{2,1,0:T(8,128)(2,1)} %get-tuple-element.8, bf16[32,128,256]{2,1,0:T(8,128)(2,1)} %collective-permute-done.6), kind=kLoop, calls=%fused_computation.44 | loop fusion | bytes 4194304 | tf_op jit(solution)/shard_map/concatenate | solution.py:155
  186.9 7.8 %attention.1 = bf16[512,1024]{1,0:T(8,128)(2,1)S(1)} custom-call(s32[64]{0:T(128)S(1)} %get-tuple-element.6.lens_ref, f32[1]{0:T(128)S(6)} %copy.29.gate_ref, bf16[512,1024]{1,0:T(8,128)(2,1)S(1)} %convolution_convert_fusion.q_ref, bf16[64,128,256]{2,1,0:T(8,128)(2,1)} %constant_dynamic-update-slice_fusion.5.kv_ref), custom_call_target="tpu_custom_call" | custom-call | tf_op jit(solution)/shard_map/attention/pallas_call | solution.py:86
  194.7 1.3 fusion
  (14 shorter events, 0.2 us)
Async XLA Ops:
  6.5 176.0 %copy-start = (bf16[1,256,1024]{2,1,0:T(8,128)(2,1)S(1)}, bf16[1,256,1024]{2,1,0:T(8,128)(2,1)}, u32[]{:S(2)}) copy-start(bf16[1,256,1024]{2,1,0:T(8,128)(2,1)} %param.8) | copy-start | bytes 1572868
  6.5 14.3 %copy-start.2 = (bf16[32,128]{1,0:T(8,128)(2,1)S(1)}, bf16[32,128]{1,0:T(8,128)(2,1)}, u32[]{:S(2)}) copy-start(bf16[32,128]{1,0:T(8,128)(2,1)} %param.11) | copy-start | bytes 24580
  6.5 14.3 %copy-start.3 = (bf16[32,128]{1,0:T(8,128)(2,1)S(1)}, bf16[32,128]{1,0:T(8,128)(2,1)}, u32[]{:S(2)}) copy-start(bf16[32,128]{1,0:T(8,128)(2,1)} %param.10) | copy-start | bytes 24580
  6.5 81.1 %all-gather.3.cloned.1.call-start = ((), (), s32[]{:S(2)}) async-start(), calls=%async_computation.2 | async-start | bytes 2621440 | tf_op jit(solution)/shard_map/vision_tensor/all_gather | solution.py:118
  64.9 9.4 %collective-permute-start = (bf16[16,48,256]{2,1,0:T(8,128)(2,1)S(1)}, bf16[16,48,256]{2,1,0:T(8,128)(2,1)S(1)}, u32[]{:S(2)}, u32[]{:S(2)}) collective-permute-start(bf16[16,48,256]{2,1,0:T(8,128)(2,1)S(1)} %bitcast.44), channel_id=1, source_target_pairs={{0,8},{4,12},{8,0},{12,4},{16,24},{20,28},{24,16},{28,20},{32,40},... | collective-permute-start | bytes 1179656 | tf_op jit(solution)/shard_map/weights_pair/ppermute | solution.py:128
  74.4 13.2 %collective-permute-start.1 = (bf16[32,48,256]{2,1,0:T(8,128)(2,1)S(1)}, bf16[32,48,256]{2,1,0:T(8,128)(2,1)S(1)}, u32[]{:S(2)}, u32[]{:S(2)}) collective-permute-start(bf16[32,48,256]{2,1,0:T(8,128)(2,1)S(1)} %pad_maximum_fusion.own_ref), channel_id=1, source_target_pairs={{0,4},{4,0},{8,12},{12,8},{16,20},{20,16},{24,28},{28,24},{32,36},... | collective-permute-start | bytes 2359304 | tf_op jit(solution)/shard_map/weights_core/ppermute | solution.py:131
  87.6 1.6 copy-start.1
  132.0 11.4 %collective-permute-start.3 = (bf16[4,128,256]{2,1,0:T(8,128)(2,1)S(1)}, bf16[4,128,256]{2,1,0:T(8,128)(2,1)S(1)}, u32[]{:S(2)}, u32[]{:S(2)}) collective-permute-start(bf16[4,128,256]{2,1,0:T(8,128)(2,1)S(1)} %all_gather.16), channel_id=1, source_target_pairs={{0,24},{4,28},{8,32},{12,36},{16,40},{20,44},{24,48},{28,52},{32,5... | collective-permute-start | bytes 786440 | tf_op jit(solution)/shard_map/kv_mid/ppermute | solution.py:146
  134.0 16.2 %collective-permute-start.2 = (bf16[4,128,256]{2,1,0:T(8,128)(2,1)S(1)}, bf16[4,128,256]{2,1,0:T(8,128)(2,1)S(1)}, u32[]{:S(2)}, u32[]{:S(2)}) collective-permute-start(bf16[4,128,256]{2,1,0:T(8,128)(2,1)S(1)} %all_gather.16), channel_id=1, source_target_pairs={{0,232},{4,236},{8,240},{12,244},{16,248},{20,252},{24,0},{28,4},{... | collective-permute-start | bytes 786440 | tf_op jit(solution)/shard_map/kv_mid/ppermute | solution.py:145
  150.3 18.4 %collective-permute-start.4 = (bf16[10,128,256]{2,1,0:T(8,128)(2,1)S(1)}, bf16[10,128,256]{2,1,0:T(8,128)(2,1)S(1)}, u32[]{:S(2)}, u32[]{:S(2)}) collective-permute-start(bf16[10,128,256]{2,1,0:T(8,128)(2,1)S(1)} %get-tuple-element.18), channel_id=1, source_target_pairs={{0,248},{4,252},{8,0},{12,4},{16,8},{20,12},{24,16},{28,20},{32,24... | collective-permute-start | bytes 1966088 | tf_op jit(solution)/shard_map/kv_near/ppermute | solution.py:149
  154.4 15.5 %collective-permute-start.5 = (bf16[10,128,256]{2,1,0:T(8,128)(2,1)S(1)}, bf16[10,128,256]{2,1,0:T(8,128)(2,1)S(1)}, u32[]{:S(2)}, u32[]{:S(2)}) collective-permute-start(bf16[10,128,256]{2,1,0:T(8,128)(2,1)S(1)} %get-tuple-element.17), channel_id=1, source_target_pairs={{0,8},{4,12},{8,16},{12,20},{16,24},{20,28},{24,32},{28,36},{32,40... | collective-permute-start | bytes 1966088 | tf_op jit(solution)/shard_map/kv_near/ppermute | solution.py:150
  168.7 12.6 %copy-start.5 = (s32[1,64]{1,0:T(1,128)S(1)}, s32[1,64]{1,0:T(1,128)}, u32[]{:S(2)}) copy-start(s32[1,64]{1,0:T(1,128)} %param.14) | copy-start | bytes 772
  168.7 12.8 %copy-start.4 = (s32[1,256,1]{1,2,0:T(1,128)S(1)}, s32[1,256,1]{1,2,0:T(1,128)}, u32[]{:S(2)}) copy-start(s32[1,256,1]{1,2,0:T(1,128)} %param.13) | copy-start | bytes 3076
  171.1 12.7 %collective-permute-start.6 = (bf16[32,128,256]{2,1,0:T(8,128)(2,1)}, bf16[32,128,256]{2,1,0:T(8,128)(2,1)}, u32[]{:S(2)}, u32[]{:S(2)}) collective-permute-start(bf16[32,128,256]{2,1,0:T(8,128)(2,1)} %get-tuple-element.7), channel_id=1, source_target_pairs={{0,4},{4,0},{8,12},{12,8},{16,20},{20,16},{24,28},{28,24},{32,36},... | collective-permute-start | bytes 6291464 | tf_op jit(solution)/shard_map/kv_core/ppermute | solution.py:154
Sparse Core Ops, SparseCore 0:
  20.3 56.9 all-gather.2

commit v3 on v2

v3 whole, which is shorter than its diff:
```python
import jax
import jax.numpy as jnp
import numpy as np
from jax import lax
from jax.experimental import pallas as pl
from jax.experimental.pallas import tpu as pltpu
from jax.sharding import PartitionSpec as P

HD = 128
CAP = 8
BF = jnp.bfloat16
F32 = jnp.float32


def head_norm(x):
    return x * lax.rsqrt(jnp.mean(x * x, axis=-1, keepdims=True) + 1e-06)


def project(place_ref, x_ref, own_ref, other_ref, out_ref, w_ref):
    @pl.when(pl.program_id(0) == 0)
    def _():
        rows = w_ref.shape[0] // (own_ref.shape[0] * 2)
        half = own_ref.shape[0] // 2
        core, odd = place_ref[0], place_ref[1]
        for k, ref in enumerate((own_ref, other_ref)):
            for o in range(2):
                for j in range(half):
                    owner = 2 * (2 * j + (o + odd) % 2) + (k + core) % 2
                    at = pl.ds(pl.multiple_of(owner * rows, rows), rows)
                    w_ref[at] = ref[o * half + j, :rows]

    out_ref[...] = jnp.dot(x_ref[...], w_ref[...], preferred_element_type=F32)


def projection(place, x, own, other, steps=4):
    rows, cols = x.shape[0] // steps, own.shape[2]
    whole = pl.BlockSpec(own.shape, lambda i: (0, 0, 0))
    return pl.pallas_call(
        project,
        grid=(steps,),
        out_shape=jax.ShapeDtypeStruct((x.shape[0], cols), F32),
        in_specs=[
            pl.BlockSpec(memory_space=pltpu.SMEM),
            pl.BlockSpec((rows, x.shape[1]), lambda i: (i, 0)),
            whole,
            whole,
        ],
        out_specs=pl.BlockSpec((rows, cols), lambda i: (i, 0)),
        scratch_shapes=[pltpu.VMEM((x.shape[1], cols), BF)],
        compiler_params=pltpu.CompilerParams(vmem_limit_bytes=48 * 1024 * 1024),
    )(place, x, own, other)


def attend(lens_ref, gate_ref, q_ref, own_ref, other_ref, out_ref):
    heads = q_ref.shape[1] // HD
    vtok = own_ref.shape[1]
    pairs = own_ref.shape[0]
    factor = jnp.tanh(jnp.full((1, 1), gate_ref[0], F32))
    col = lax.broadcasted_iota(jnp.int32, (1, 2 * vtok), 1)

    def one(i):
        rows = pl.ds(pl.multiple_of(i * 2 * CAP, 2 * CAP), 2 * CAP)
        q = jnp.concatenate([q_ref[rows, h * HD : (h + 1) * HD] for h in range(heads)], axis=0)
        kv = jnp.concatenate([own_ref[i], other_ref[i]], axis=0)
        k, v = kv[:, :HD], kv[:, HD:]
        s = lax.dot_general(q, k, (((1,), (1,)), ((), ())), preferred_element_type=F32)
        s = s.reshape(heads, 2, CAP, 2 * vtok) * (HD ** -0.5)
        ok0 = col < lens_ref[2 * i]
        ok1 = (col >= vtok) & (col < vtok + lens_ref[2 * i + 1])
        s0 = jnp.where(ok0[None], s[:, 0], -jnp.inf)
        s1 = jnp.where(ok1[None], s[:, 1], -jnp.inf)
        s = jnp.stack([s0, s1], axis=1).reshape(heads * 2 * CAP, 2 * vtok)
        top = jnp.max(s, axis=1, keepdims=True)
        p = jnp.exp(s - top)
        total = jnp.sum(p, axis=1, keepdims=True)
        mixed = jnp.dot(p.astype(BF), v, preferred_element_type=F32)
        ans = (mixed * (factor / total)).astype(BF)
        for h in range(heads):
            out_ref[rows, h * HD : (h + 1) * HD] = ans[h * 2 * CAP : (h + 1) * 2 * CAP]

    unroll = next(u for u in (4, 3, 1) if pairs % u == 0)
    if pairs < 12:
        unroll = pairs

    def body(i, carry):
        for u in range(unroll):
            one(i * unroll + u)
        return carry

    lax.fori_loop(0, pairs // unroll, body, 0)


def attention(lens, gate, q, own, other):
    smem = pl.BlockSpec(memory_space=pltpu.SMEM)
    vmem = pl.BlockSpec(memory_space=pltpu.VMEM)
    heads = q.shape[1] // HD
    pairs, vtok = own.shape[0], own.shape[1]
    scores = heads * 2 * CAP * 2 * vtok * pairs
    return pl.pallas_call(
        attend,
        out_shape=jax.ShapeDtypeStruct(q.shape, BF),
        in_specs=[smem, smem, vmem, vmem, vmem],
        out_specs=vmem,
        cost_estimate=pl.CostEstimate(
            flops=4 * scores * HD, bytes_accessed=4 * own.size * 2, transcendentals=scores
        ),
        compiler_params=pltpu.CompilerParams(vmem_limit_bytes=32 * 1024 * 1024),
    )(lens, gate, q, own, other)


def chip_shift(n_seq, d):
    return [(i, (i + 2 * d) % n_seq) for i in range(n_seq)]


def shards(queries, vision, w_key, w_value, attn_gate, token_image, image_owner, image_len):
    n_doc = lax.axis_size("doc")
    n_seq = lax.axis_size("seq")
    n_z = n_seq // 2
    seq = lax.axis_index("seq")
    core = seq % 2
    z = seq // 2
    rows32, width = vision.shape[2], vision.shape[3]
    slice_w = width // n_doc
    swap = [(i, i ^ 1) for i in range(n_seq)]

    with jax.named_scope("vision_doc"):
        cols = jnp.stack([vision[0, 0, :, i * slice_w : (i + 1) * slice_w] for i in range(n_doc)])
        cols = lax.all_to_all(cols, "doc", split_axis=0, concat_axis=0, tiled=True)
        cols = cols.reshape(n_doc * rows32, slice_w)
    with jax.named_scope("vision_tensor"):
        x = lax.all_gather(cols, "tensor", axis=0, tiled=True)

    wrows = w_key.shape[0]
    w = jnp.concatenate([w_key, w_value], axis=1)
    extra = jnp.broadcast_to(image_len.astype(BF), (8, w.shape[1]))
    packed = jnp.concatenate([w, extra], axis=0)
    groups = [[2 * (2 * j + o) + c for j in range(n_z // 2)] for o in range(2) for c in range(2)]
    with jax.named_scope("weights_z"):
        near = lax.all_gather(packed, "seq", axis=0, tiled=False, axis_index_groups=groups)
    with jax.named_scope("weights_pair"):
        beside = lax.ppermute(near, "seq", [(i, i ^ 2) for i in range(n_seq)])
    own = jnp.concatenate([near, beside], axis=0)
    with jax.named_scope("weights_core"):
        other = lax.ppermute(own, "seq", swap)
    with jax.named_scope("project"):
        part = projection(jnp.stack([core, z % 2]), x, own, other)
    with jax.named_scope("reduce_doc"):
        part = part.reshape(-1, n_doc, rows32, w.shape[1])
        part = lax.all_to_all(part, "doc", split_axis=1, concat_axis=1, tiled=True)
        kv = jnp.sum(part, axis=1).reshape(-1, w.shape[1])
    kv = jnp.concatenate([head_norm(kv[:, :HD]), kv[:, HD:]], axis=1).astype(BF)

    def from_chip(block, d):
        return lax.ppermute(block, "seq", chip_shift(n_seq, -d))

    kv = kv[None]
    with jax.named_scope("kv_far"):
        p9, m9 = from_chip(kv, 9), from_chip(kv, -9)
    with jax.named_scope("kv_mid"):
        three = jnp.concatenate([kv, p9, m9], axis=0)
        p15, m15 = from_chip(p9, 6), from_chip(m9, -6)
        p3, m3 = from_chip(three, 3), from_chip(three, -3)
    early = jnp.concatenate([three, p3, m3, p15, m15], axis=0)
    offsets = [0, 9, -9, 3, 12, -6, -3, 6, -12, 15, -15]
    with jax.named_scope("kv_near"):
        up, down = from_chip(early, 1), from_chip(early[:-1], -1)
    late = jnp.concatenate([up, down], axis=0)
    places = [*offsets, *(o + 1 for o in offsets), *(o - 1 for o in offsets[:-1])]
    places = np.array([o % n_z for o in places], np.int32)
    with jax.named_scope("kv_core"):
        early_other = lax.ppermute(early, "seq", swap)
        late_other = lax.ppermute(late, "seq", swap)

    owners = jnp.arange(n_seq, dtype=jnp.int32)
    oz, oc = owners // 2, owners % 2
    here = (oz - z) % n_z
    pair = jnp.sum(jnp.where(here[:, None] == places[None, :], jnp.arange(n_z)[None, :], 0), axis=1)
    pos = 2 * pair + (oc != core).astype(jnp.int32)
    at = owners[:, None] == pos[None, :]
    lens = jnp.concatenate([own[:, wrows, 0], other[:, wrows, 0]]).astype(jnp.int32)
    from_w = n_z * (oc != core).astype(jnp.int32) + (n_z // 2) * ((oz - z) % 2) + oz // 2
    lens = jnp.sum(jnp.where(from_w[:, None] == owners[None, :], lens[None, :], 0), axis=1)
    lens_at = jnp.sum(jnp.where(at, lens[None, :], 0), axis=1)

    image_ids = token_image[0, :, 0]
    owner_pos = jnp.sum(
        jnp.where(image_owner[0][:, None] == owners[None, :], pos[None, :], 0), axis=1
    )
    picked = image_ids[:, None] == owners[None, :]
    target = jnp.sum(jnp.where(picked, owner_pos[None, :], 0), axis=1)
    onehot = (target[:, None] == owners[None, :]).astype(jnp.int32)
    ranks = jnp.cumsum(onehot, axis=0) - onehot
    slot = target * CAP + jnp.sum(ranks * onehot, axis=1)
    dispatch = (slot[:, None] == jnp.arange(n_seq * CAP, dtype=jnp.int32)[None, :]).astype(BF)
    with jax.named_scope("dispatch"):
        q = jnp.dot(dispatch.T, queries[0], preferred_element_type=F32).astype(BF)
    cut = early.shape[0] * 2
    with jax.named_scope("attention_early"):
        first = attention(lens_at[:cut], attn_gate, q[: cut * CAP], early, early_other)
        out = jnp.dot(dispatch[:, : cut * CAP], first, preferred_element_type=F32)
    with jax.named_scope("attention_late"):
        last = attention(lens_at[cut:], attn_gate, q[cut * CAP :], late, late_other)
        out = out + jnp.dot(dispatch[:, cut * CAP :], last, preferred_element_type=F32)
    return out.astype(BF)[None]


def solution(mesh):
    placed = (
        P("doc", "seq", "tensor"),
        P("doc", "seq", "tensor", None),
        P(("doc", "seq"), "tensor"),
        P(("doc", "seq"), "tensor"),
        P(),
        P("doc", "seq", None),
        P("doc", None),
        P("doc", "seq"),
    )
    return jax.shard_map(
        shards, mesh=mesh, in_specs=placed, out_specs=P("doc", "seq", "tensor"), check_vma=False
    )
```

time: 207 us -> 214 us (1.034)
  blocking collectives: 97 us -> 67 us
  starting transfers between devices: 42.7 us -> 67.4 us
  waiting for transfers between devices: 23.1 us -> 43.4 us
  local copies, waits for them, and re-layouts: 11.9 us -> 3.71 us
    all_gather x1 -> x0, blocking collectives: 29.9 us -> none  [shards(): s0 = lax.all_gather(kv, 'seq', axis=0, tiled=False, axis_index_groups=far)]
    ppermute x5 -> x10, starting transfers between devices: 27.6 us -> 52.8 us  [the longest x8 46.6 us: from_chip(): return lax.ppermute(block, 'seq', chip_shift(n_seq, -d))]
    ppermute x5 -> x10, waiting for transfers between devices: 15.7 us -> 36.3 us  [the longest x8 34.9 us: from_chip(): return lax.ppermute(block, 'seq', chip_shift(n_seq, -d))]
    concatenate x2 -> x3, local copies, waits for them, and re-layouts: 4.32 us -> 0.06 us  [the longest x1 0.04 us: shards(): late = jnp.concatenate([up, down], axis=0)]
    unnamed x16 -> x23, local copies, waits for them, and re-layouts: 5.23 us -> 1.76 us
    pallas_call x1 -> x2, Pallas kernels: 7.81 us -> 6.69 us  [attention(): pl.pallas_call(attend, out_shape=jax.ShapeDtypeStruct(q.shape, BF), in_sp...]
  transfers between devices with their start and end apart: 8 -> 13, of which waited for: 6 -> 9; matrix products, arithmetic and copies ran while one was open for 3% -> 2% of each run, Pallas kernels for 0% -> 1%
where the time goes in v3:
time: 214 us; the launch traced here: 210 us
  starting transfers between devices  67.4 us (31%)
  blocking collectives  67 us (31%)
  waiting for transfers between devices  43.4 us (20%)
  between operations  15.2 us (7%)
  Pallas kernels  8.67 us (4%)
  local copies, waits for them, and re-layouts  3.71 us (2%)
  other arithmetic  2.34 us (1%)
  matrix products  2.16 us (1%)
    ppermute x8, starting transfers between devices, from_chip(): return lax.ppermute(block, 'seq', chip_shift(n_seq, -d))  46.6 us
    all_gather x1, blocking collectives, shards(): lax.all_gather(packed, 'seq', axis=0, tiled=False, axis_index_groups=groups)  43.5 us
    ppermute x8, waiting for transfers between devices, from_chip(): return lax.ppermute(block, 'seq', chip_shift(n_seq, -d))  34.9 us
    ppermute x1, starting transfers between devices, shards(): other = lax.ppermute(own, 'seq', swap)  11.9 us
    all_to_all x1, blocking collectives, shards(): cols = lax.all_to_all(cols, 'doc', split_axis=0, concat_axis=0, tiled=True)  11.9 us
    all_to_all x1, blocking collectives, shards(): part = lax.all_to_all(part, 'doc', split_axis=1, concat_axis=1, tiled=True)  11.6 us
    pallas_call x2, Pallas kernels, attention(): pl.pallas_call(attend, out_shape=jax.ShapeDtypeStruct(q.shape, BF), in_sp...  6.69 us
    ppermute x1, waiting for transfers between devices, shards(): beside = lax.ppermute(near, 'seq', [(i, i ^ 2) for i in range(n_seq)])  5.5 us
  transfers between devices with their start and end apart: 13, of which 9 were waited for; matrix products, arithmetic and copies ran while one was open for 2% of the time, Pallas kernels for 1%

profile of v3, /device:TPU:1, one launch (start us, length us, event | category | flops | bytes accessed | tf_op | source)
XLA Modules:
  0.0 209.9 jit_solution(18213673195369714823)
XLA Ops:
  6.5 0.0 copy-start
  6.5 0.0 all-gather.3.cloned.1.call-start
  6.5 1.2 slice_bitcast_fusion.3
  7.7 0.0 copy-start.4
  7.7 0.0 copy-start.5
  7.8 0.1 pad_maximum_fusion.1
  7.8 11.9 %all_to_all.10 = bf16[4,32,2048]{2,1,0:T(8,128)(2,1)} all-to-all(bf16[4,32,2048]{2,1,0:T(8,128)(2,1)S(1)} %pad_maximum_fusion.1), channel_id=1, replica_groups=mesh['doc'=4,'seq'=64,'tensor'=4] {'doc'}, dimensions={0} | all-to-all | bytes 1048576 | tf_op jit(solution)/shard_map/vision_doc/all_to_all | solution.py:128
  19.7 0.0 all-gather.3.cloned.1.call-update
  20.4 0.0 copy-done.4
  20.4 0.0 copy-done.5
  20.4 43.5 %all-gather = bf16[640,256]{1,0:T(8,128)(2,1)S(1)} all-gather(bf16[40,256]{1,0:T(8,128)(2,1)S(1)} %fusion.14), channel_id=2, replica_groups={{0,16,32,48,64,80,96,112,128,144,160,176,192,208,224,240},{4,20,36,52,6..., dimensions={0}, use_global_device_ids=true | all-gather | bytes 348160 | tf_op jit(solution)/shard_map/weights_z/all_gather | solution.py:139
  63.9 2.7 %collective-permute-start = (bf16[16,40,256]{2,1,0:T(8,128)(2,1)S(1)}, bf16[16,40,256]{2,1,0:T(8,128)(2,1)S(1)}, u32[]{:S(2)}, u32[]{:S(2)}) collective-permute-start(bf16[16,40,256]{2,1,0:T(8,128)(2,1)S(1)} %bitcast.51), channel_id=1, source_target_pairs={{0,8},{4,12},{8,0},{12,4},{16,24},{20,28},{24,16},{28,20},{32,40},... | collective-permute-start | bytes 983048 | tf_op jit(solution)/shard_map/weights_pair/ppermute | solution.py:141
  66.6 5.5 %collective-permute-done = bf16[16,40,256]{2,1,0:T(8,128)(2,1)S(1)} collective-permute-done((bf16[16,40,256]{2,1,0:T(8,128)(2,1)S(1)}, bf16[16,40,256]{2,1,0:T(8,128)(2,1)S(1)}, u32[]{:S(2)}, u32[]{:S(2)}) %collective-permute-start) | collective-permute-done | bytes 327712 | tf_op jit(solution)/shard_map/weights_pair/ppermute | solution.py:141
  72.1 0.1 pad_maximum_fusion.own_ref
  72.2 11.9 %collective-permute-start.1 = (bf16[32,40,256]{2,1,0:T(8,128)(2,1)S(1)}, bf16[32,40,256]{2,1,0:T(8,128)(2,1)S(1)}, u32[]{:S(2)}, u32[]{:S(2)}) collective-permute-start(bf16[32,40,256]{2,1,0:T(8,128)(2,1)S(1)} %pad_maximum_fusion.own_ref), channel_id=1, source_target_pairs={{0,4},{4,0},{8,12},{12,8},{16,20},{20,16},{24,28},{28,24},{32,36},... | collective-permute-start | bytes 1966088 | tf_op jit(solution)/shard_map/weights_core/ppermute | solution.py:144
  84.1 0.1 pad_add_fusion.place_ref
  84.2 1.6 collective-permute-done.1.other_ref
  85.8 1.6 copy-done.1
  87.4 2.0 project.1
  89.4 11.6 %all_to_all.11 = f32[4,4,32,256]{3,2,0,1:T(8,128)S(1)} all-to-all(f32[4,4,32,256]{3,2,0,1:T(8,128)S(1)} %copy.14), channel_id=1, replica_groups=mesh['doc'=4,'seq'=64,'tensor'=4] {'doc'}, dimensions={1} | all-to-all | bytes 1048576 | tf_op jit(solution)/shard_map/reduce_doc/all_to_all | solution.py:149
  101.1 0.1 multiply_reduce_fusion
  101.2 0.0 copy-start.8
  101.2 0.1 fusion.12
  101.3 7.9 %collective-permute-start.2 = (bf16[1,128,256]{2,1,0:T(8,128)(2,1)S(1)}, bf16[1,128,256]{2,1,0:T(8,128)(2,1)S(1)}, u32[]{:S(2)}, u32[]{:S(2)}) collective-permute-start(bf16[1,128,256]{2,1,0:T(8,128)(2,1)S(1)} %get-tuple-element.23), channel_id=1, source_target_pairs={{0,184},{4,188},{8,192},{12,196},{16,200},{20,204},{24,208},{28,21... | collective-permute-start | bytes 196616 | tf_op jit(solution)/shard_map/kv_far/ppermute | solution.py:154
  109.2 7.0 %collective-permute-start.3 = (bf16[1,128,256]{2,1,0:T(8,128)(2,1)S(1)}, bf16[1,128,256]{2,1,0:T(8,128)(2,1)S(1)}, u32[]{:S(2)}, u32[]{:S(2)}) collective-permute-start(bf16[1,128,256]{2,1,0:T(8,128)(2,1)S(1)} %get-tuple-element.23), channel_id=1, source_target_pairs={{0,72},{4,76},{8,80},{12,84},{16,88},{20,92},{24,96},{28,100},{32,... | collective-permute-start | bytes 196616 | tf_op jit(solution)/shard_map/kv_far/ppermute | solution.py:154
  116.3 6.5 %collective-permute-done.2 = bf16[1,128,256]{2,1,0:T(8,128)(2,1)S(1)} collective-permute-done((bf16[1,128,256]{2,1,0:T(8,128)(2,1)S(1)}, bf16[1,128,256]{2,1,0:T(8,128)(2,1)S(1)}, u32[]{:S(2)}, u32[]{:S(2)}) %collective-permute-start.2) | collective-permute-done | bytes 65568 | tf_op jit(solution)/shard_map/kv_far/ppermute | solution.py:154
  122.8 3.9 %collective-permute-done.3 = bf16[1,128,256]{2,1,0:T(8,128)(2,1)S(1)} collective-permute-done((bf16[1,128,256]{2,1,0:T(8,128)(2,1)S(1)}, bf16[1,128,256]{2,1,0:T(8,128)(2,1)S(1)}, u32[]{:S(2)}, u32[]{:S(2)}) %collective-permute-start.3) | collective-permute-done | bytes 65568 | tf_op jit(solution)/shard_map/kv_far/ppermute | solution.py:154
  126.8 3.2 %collective-permute-start.4 = (bf16[3,128,256]{2,1,0:T(8,128)(2,1)S(1)}, bf16[3,128,256]{2,1,0:T(8,128)(2,1)S(1)}, u32[]{:S(2)}, u32[]{:S(2)}) collective-permute-start(bf16[3,128,256]{2,1,0:T(8,128)(2,1)S(1)} %pad_maximum_fusion.2), channel_id=1, source_target_pairs={{0,232},{4,236},{8,240},{12,244},{16,248},{20,252},{24,0},{28,4},{... | collective-permute-start | bytes 589832 | tf_op jit(solution)/shard_map/kv_mid/ppermute | solution.py:154
  129.9 3.9 %collective-permute-start.5 = (bf16[3,128,256]{2,1,0:T(8,128)(2,1)S(1)}, bf16[3,128,256]{2,1,0:T(8,128)(2,1)S(1)}, u32[]{:S(2)}, u32[]{:S(2)}) collective-permute-start(bf16[3,128,256]{2,1,0:T(8,128)(2,1)S(1)} %pad_maximum_fusion.2), channel_id=1, source_target_pairs={{0,24},{4,28},{8,32},{12,36},{16,40},{20,44},{24,48},{28,52},{32,5... | collective-permute-start | bytes 589832 | tf_op jit(solution)/shard_map/kv_mid/ppermute | solution.py:154
  133.8 9.7 %collective-permute-start.6 = (bf16[1,128,256]{2,1,0:T(8,128)(2,1)S(1)}, bf16[1,128,256]{2,1,0:T(8,128)(2,1)S(1)}, u32[]{:S(2)}, u32[]{:S(2)}) collective-permute-start(bf16[1,128,256]{2,1,0:T(8,128)(2,1)S(1)} %collective-permute-done.2), channel_id=1, source_target_pairs={{0,208},{4,212},{8,216},{12,220},{16,224},{20,228},{24,232},{28,23... | collective-permute-start | bytes 196616 | tf_op jit(solution)/shard_map/kv_mid/ppermute | solution.py:154
  143.5 1.9 collective-permute-start.7
  145.5 0.0 collective-permute-done.4
  145.5 0.0 collective-permute-done.5
  145.6 4.2 %collective-permute-done.6 = bf16[1,128,256]{2,1,0:T(8,128)(2,1)S(1)} collective-permute-done((bf16[1,128,256]{2,1,0:T(8,128)(2,1)S(1)}, bf16[1,128,256]{2,1,0:T(8,128)(2,1)S(1)}, u32[]{:S(2)}, u32[]{:S(2)}) %collective-permute-start.6) | collective-permute-done | bytes 65568 | tf_op jit(solution)/shard_map/kv_mid/ppermute | solution.py:154
  149.8 8.1 %collective-permute-done.7 = bf16[1,128,256]{2,1,0:T(8,128)(2,1)S(1)} collective-permute-done((bf16[1,128,256]{2,1,0:T(8,128)(2,1)S(1)}, bf16[1,128,256]{2,1,0:T(8,128)(2,1)S(1)}, u32[]{:S(2)}, u32[]{:S(2)}) %collective-permute-start.7) | collective-permute-done | bytes 65568 | tf_op jit(solution)/shard_map/kv_mid/ppermute | solution.py:154
  157.9 8.4 %collective-permute-start.9 = (bf16[11,128,256]{2,1,0:T(8,128)(2,1)S(1)}, bf16[11,128,256]{2,1,0:T(8,128)(2,1)S(1)}, u32[]{:S(2)}, u32[]{:S(2)}) collective-permute-start(bf16[11,128,256]{2,1,0:T(8,128)(2,1)S(1)} %constant_dynamic-update-slice_fusion.own_ref), channel_id=1, source_target_pairs={{0,248},{4,252},{8,0},{12,4},{16,8},{20,12},{24,16},{28,20},{32,24... | collective-permute-start | bytes 2162696 | tf_op jit(solution)/shard_map/kv_near/ppermute | solution.py:154
  167.0 0.1 select_reduce_fusion.4
  167.1 4.7 %collective-permute-start.10 = (bf16[10,128,256]{2,1,0:T(8,128)(2,1)S(1)}, bf16[10,128,256]{2,1,0:T(8,128)(2,1)S(1)}, u32[]{:S(2)}, u32[]{:S(2)}) collective-permute-start(bf16[10,128,256]{2,1,0:T(8,128)(2,1)S(1)} %get-tuple-element.15), channel_id=1, source_target_pairs={{0,8},{4,12},{8,16},{12,20},{16,24},{20,28},{24,32},{28,36},{32,40... | collective-permute-start | bytes 1966088 | tf_op jit(solution)/shard_map/kv_near/ppermute | solution.py:154
  171.8 0.3 fusion.16
  172.1 0.3 slice_reduce_fusion.1
  172.4 0.1 maximum_convert_fusion
  172.5 0.2 select_reduce_fusion.2
  172.7 0.0 copy-start.7
  172.7 0.0 copy-start.6
  172.7 12.0 %collective-permute-done.9 = bf16[11,128,256]{2,1,0:T(8,128)(2,1)S(1)} collective-permute-done((bf16[11,128,256]{2,1,0:T(8,128)(2,1)S(1)}, bf16[11,128,256]{2,1,0:T(8,128)(2,1)S(1)}, u32[]{:S(2)}, u32[]{:S(2)}) %collective-permute-start.9) | collective-permute-done | bytes 720928 | tf_op jit(solution)/shard_map/kv_near/ppermute | solution.py:154
  184.7 0.2 collective-permute-done.10
  184.9 4.3 %collective-permute-start.11 = (bf16[21,128,256]{2,1,0:T(8,128)(2,1)S(1)}, bf16[21,128,256]{2,1,0:T(8,128)(2,1)S(1)}, u32[]{:S(2)}, u32[]{:S(2)}) collective-permute-start(bf16[21,128,256]{2,1,0:T(8,128)(2,1)S(1)} %constant_dynamic-update-slice_fusion.13.own_ref), channel_id=1, source_target_pairs={{0,4},{4,0},{8,12},{12,8},{16,20},{20,16},{24,28},{28,24},{32,36},... | collective-permute-start | bytes 4128776 | tf_op jit(solution)/shard_map/kv_core/ppermute | solution.py:172
  189.3 0.0 copy-done.7
  189.3 0.2 select_reduce_fusion.3
  189.5 0.1 select_reduce_fusion
  189.6 0.6 reduce-window.6
  190.2 0.2 slice_reduce_fusion
  190.4 1.9 collective-permute-start.8
  192.3 0.1 fusion.8
  192.4 0.0 copy-done
  192.5 0.6 convolution_convert_fusion
  193.1 0.1 slice.65.lens_ref
  193.2 0.1 iota_compare_fusion
  193.3 1.4 collective-permute-done.8.other_ref
  194.7 1.5 attention_early.1
  196.2 0.0 collective-permute-done.11.other_ref
  196.2 5.2 %attention_late.1 = bf16[336,1024]{1,0:T(8,128)(2,1)S(1)} custom-call(s32[42]{0:T(128)S(1)} %slice.65.lens_ref, f32[1]{0:T(128)S(6)} %copy.30.gate_ref, bf16[336,1024]{1,0:T(8,128)(2,1)S(1)} %slice.76.q_ref, bf16[21,128,256]{2,1,0:T(8,128)(2,1)S(1)} %constant_dynamic-update-slice_fusion.13.own_ref, bf16[21,128,256]{2,1,0:T(8,128)(2,1)S(1)} %collective-permute-done.11.other_ref), custom_call_target="tpu_custom_call" | custom-call | flops 352321536 | bytes 5505024 | tf_op jit(solution)/shard_map/attention_late/pallas_call | solution.py:99
  201.4 0.5 fusion.3
  201.9 1.1 fusion.1
  (32 shorter events, 0.5 us)
Async XLA Ops:
  6.5 185.9 %copy-start = (bf16[1,256,1024]{2,1,0:T(8,128)(2,1)S(1)}, bf16[1,256,1024]{2,1,0:T(8,128)(2,1)}, u32[]{:S(2)}) copy-start(bf16[1,256,1024]{2,1,0:T(8,128)(2,1)} %param.9) | copy-start | bytes 1572868
  6.5 79.2 %all-gather.3.cloned.1.call-start = ((), (), s32[]{:S(2)}) async-start(), calls=%async_computation.2 | async-start | bytes 2621440 | tf_op jit(solution)/shard_map/vision_tensor/all_gather | solution.py:131
  7.7 12.6 %copy-start.4 = (bf16[32,128]{1,0:T(8,128)(2,1)S(1)}, bf16[32,128]{1,0:T(8,128)(2,1)}, u32[]{:S(2)}) copy-start(bf16[32,128]{1,0:T(8,128)(2,1)} %param.12) | copy-start | bytes 24580
  7.7 12.6 %copy-start.5 = (bf16[32,128]{1,0:T(8,128)(2,1)S(1)}, bf16[32,128]{1,0:T(8,128)(2,1)}, u32[]{:S(2)}) copy-start(bf16[32,128]{1,0:T(8,128)(2,1)} %param.11) | copy-start | bytes 24580
  63.9 8.2 %collective-permute-start = (bf16[16,40,256]{2,1,0:T(8,128)(2,1)S(1)}, bf16[16,40,256]{2,1,0:T(8,128)(2,1)S(1)}, u32[]{:S(2)}, u32[]{:S(2)}) collective-permute-start(bf16[16,40,256]{2,1,0:T(8,128)(2,1)S(1)} %bitcast.51), channel_id=1, source_target_pairs={{0,8},{4,12},{8,0},{12,4},{16,24},{20,28},{24,16},{28,20},{32,40},... | collective-permute-start | bytes 983048 | tf_op jit(solution)/shard_map/weights_pair/ppermute | solution.py:141
  72.2 13.6 %collective-permute-start.1 = (bf16[32,40,256]{2,1,0:T(8,128)(2,1)S(1)}, bf16[32,40,256]{2,1,0:T(8,128)(2,1)S(1)}, u32[]{:S(2)}, u32[]{:S(2)}) collective-permute-start(bf16[32,40,256]{2,1,0:T(8,128)(2,1)S(1)} %pad_maximum_fusion.own_ref), channel_id=1, source_target_pairs={{0,4},{4,0},{8,12},{12,8},{16,20},{20,16},{24,28},{28,24},{32,36},... | collective-permute-start | bytes 1966088 | tf_op jit(solution)/shard_map/weights_core/ppermute | solution.py:144
  85.8 1.6 copy-start.1
  101.2 65.8 %copy-start.8 = (s32[32]{0:T(128)S(1)}, s32[32]{0:T(128)}, u32[]{:S(2)}) copy-start(s32[32]{0:T(128)} %constant.113) | copy-start | bytes 388
  101.3 21.5 %collective-permute-start.2 = (bf16[1,128,256]{2,1,0:T(8,128)(2,1)S(1)}, bf16[1,128,256]{2,1,0:T(8,128)(2,1)S(1)}, u32[]{:S(2)}, u32[]{:S(2)}) collective-permute-start(bf16[1,128,256]{2,1,0:T(8,128)(2,1)S(1)} %get-tuple-element.23), channel_id=1, source_target_pairs={{0,184},{4,188},{8,192},{12,196},{16,200},{20,204},{24,208},{28,21... | collective-permute-start | bytes 196616 | tf_op jit(solution)/shard_map/kv_far/ppermute | solution.py:154
  109.2 17.5 %collective-permute-start.3 = (bf16[1,128,256]{2,1,0:T(8,128)(2,1)S(1)}, bf16[1,128,256]{2,1,0:T(8,128)(2,1)S(1)}, u32[]{:S(2)}, u32[]{:S(2)}) collective-permute-start(bf16[1,128,256]{2,1,0:T(8,128)(2,1)S(1)} %get-tuple-element.23), channel_id=1, source_target_pairs={{0,72},{4,76},{8,80},{12,84},{16,88},{20,92},{24,96},{28,100},{32,... | collective-permute-start | bytes 196616 | tf_op jit(solution)/shard_map/kv_far/ppermute | solution.py:154
  126.8 18.7 %collective-permute-start.4 = (bf16[3,128,256]{2,1,0:T(8,128)(2,1)S(1)}, bf16[3,128,256]{2,1,0:T(8,128)(2,1)S(1)}, u32[]{:S(2)}, u32[]{:S(2)}) collective-permute-start(bf16[3,128,256]{2,1,0:T(8,128)(2,1)S(1)} %pad_maximum_fusion.2), channel_id=1, source_target_pairs={{0,232},{4,236},{8,240},{12,244},{16,248},{20,252},{24,0},{28,4},{... | collective-permute-start | bytes 589832 | tf_op jit(solution)/shard_map/kv_mid/ppermute | solution.py:154
  129.9 15.6 %collective-permute-start.5 = (bf16[3,128,256]{2,1,0:T(8,128)(2,1)S(1)}, bf16[3,128,256]{2,1,0:T(8,128)(2,1)S(1)}, u32[]{:S(2)}, u32[]{:S(2)}) collective-permute-start(bf16[3,128,256]{2,1,0:T(8,128)(2,1)S(1)} %pad_maximum_fusion.2), channel_id=1, source_target_pairs={{0,24},{4,28},{8,32},{12,36},{16,40},{20,44},{24,48},{28,52},{32,5... | collective-permute-start | bytes 589832 | tf_op jit(solution)/shard_map/kv_mid/ppermute | solution.py:154
  133.8 16.0 %collective-permute-start.6 = (bf16[1,128,256]{2,1,0:T(8,128)(2,1)S(1)}, bf16[1,128,256]{2,1,0:T(8,128)(2,1)S(1)}, u32[]{:S(2)}, u32[]{:S(2)}) collective-permute-start(bf16[1,128,256]{2,1,0:T(8,128)(2,1)S(1)} %collective-permute-done.2), channel_id=1, source_target_pairs={{0,208},{4,212},{8,216},{12,220},{16,224},{20,228},{24,232},{28,23... | collective-permute-start | bytes 196616 | tf_op jit(solution)/shard_map/kv_mid/ppermute | solution.py:154
  143.5 14.4 %collective-permute-start.7 = (bf16[1,128,256]{2,1,0:T(8,128)(2,1)S(1)}, bf16[1,128,256]{2,1,0:T(8,128)(2,1)S(1)}, u32[]{:S(2)}, u32[]{:S(2)}) collective-permute-start(bf16[1,128,256]{2,1,0:T(8,128)(2,1)S(1)} %collective-permute-done.3), channel_id=1, source_target_pairs={{0,48},{4,52},{8,56},{12,60},{16,64},{20,68},{24,72},{28,76},{32,8... | collective-permute-start | bytes 196616 | tf_op jit(solution)/shard_map/kv_mid/ppermute | solution.py:154
  157.9 14.7 %copy-start.2 = (bf16[11,128,256]{2,1,0:T(8,128)(2,1)}, bf16[11,128,256]{2,1,0:T(8,128)(2,1)S(1)}, u32[]{:S(2)}) copy-start(bf16[11,128,256]{2,1,0:T(8,128)(2,1)S(1)} %constant_dynamic-update-slice_fusion.own_ref) | copy-start | bytes 2162692
  157.9 26.7 %collective-permute-start.9 = (bf16[11,128,256]{2,1,0:T(8,128)(2,1)S(1)}, bf16[11,128,256]{2,1,0:T(8,128)(2,1)S(1)}, u32[]{:S(2)}, u32[]{:S(2)}) collective-permute-start(bf16[11,128,256]{2,1,0:T(8,128)(2,1)S(1)} %constant_dynamic-update-slice_fusion.own_ref), channel_id=1, source_target_pairs={{0,248},{4,252},{8,0},{12,4},{16,8},{20,12},{24,16},{28,20},{32,24... | collective-permute-start | bytes 2162696 | tf_op jit(solution)/shard_map/kv_near/ppermute | solution.py:154
  167.1 17.8 %collective-permute-start.10 = (bf16[10,128,256]{2,1,0:T(8,128)(2,1)S(1)}, bf16[10,128,256]{2,1,0:T(8,128)(2,1)S(1)}, u32[]{:S(2)}, u32[]{:S(2)}) collective-permute-start(bf16[10,128,256]{2,1,0:T(8,128)(2,1)S(1)} %get-tuple-element.15), channel_id=1, source_target_pairs={{0,8},{4,12},{8,16},{12,20},{16,24},{20,28},{24,32},{28,36},{32,40... | collective-permute-start | bytes 1966088 | tf_op jit(solution)/shard_map/kv_near/ppermute | solution.py:154
  172.7 16.6 %copy-start.7 = (s32[1,64]{1,0:T(1,128)S(1)}, s32[1,64]{1,0:T(1,128)}, u32[]{:S(2)}) copy-start(s32[1,64]{1,0:T(1,128)} %param.15) | copy-start | bytes 772
  172.7 16.8 %copy-start.6 = (s32[1,256,1]{1,2,0:T(1,128)S(1)}, s32[1,256,1]{1,2,0:T(1,128)}, u32[]{:S(2)}) copy-start(s32[1,256,1]{1,2,0:T(1,128)} %param.14) | copy-start | bytes 3076
  184.9 11.3 %collective-permute-start.11 = (bf16[21,128,256]{2,1,0:T(8,128)(2,1)S(1)}, bf16[21,128,256]{2,1,0:T(8,128)(2,1)S(1)}, u32[]{:S(2)}, u32[]{:S(2)}) collective-permute-start(bf16[21,128,256]{2,1,0:T(8,128)(2,1)S(1)} %constant_dynamic-update-slice_fusion.13.own_ref), channel_id=1, source_target_pairs={{0,4},{4,0},{8,12},{12,8},{16,20},{20,16},{24,28},{28,24},{32,36},... | collective-permute-start | bytes 4128776 | tf_op jit(solution)/shard_map/kv_core/ppermute | solution.py:172
  190.4 4.3 %collective-permute-start.8 = (bf16[11,128,256]{2,1,0:T(8,128)(2,1)}, bf16[11,128,256]{2,1,0:T(8,128)(2,1)S(1)}, u32[]{:S(2)}, u32[]{:S(2)}) collective-permute-start(bf16[11,128,256]{2,1,0:T(8,128)(2,1)} %copy-done.2), channel_id=1, source_target_pairs={{0,4},{4,0},{8,12},{12,8},{16,20},{20,16},{24,28},{28,24},{32,36},... | collective-permute-start | bytes 2162696 | tf_op jit(solution)/shard_map/kv_core/ppermute | solution.py:171
  193.0 1.7 copy-start.3
Sparse Core Ops, SparseCore 0:
  19.8 56.9 all-gather.2

commit v4 on v2

v4 whole, which is shorter than its diff:
```python
import jax
import jax.numpy as jnp
from jax import lax
from jax.experimental import pallas as pl
from jax.experimental.pallas import tpu as pltpu
from jax.sharding import PartitionSpec as P

HD = 128
CAP = 8
BF = jnp.bfloat16
F32 = jnp.float32
HF = jnp.float16
NOTES = 16
KEY_SCALE = 2048.0
TOP_LEVEL = 14.0


def head_norm(x):
    return x * lax.rsqrt(jnp.mean(x * x, axis=-1, keepdims=True) + 1e-06)


def project(place_ref, x_ref, own_ref, other_ref, out_ref, w_ref):
    rows = w_ref.shape[0] // (own_ref.shape[0] * 2)
    half = own_ref.shape[0] // 2
    core, odd = place_ref[0], place_ref[1]
    for k, ref in enumerate((own_ref, other_ref)):
        for o in range(2):
            for j in range(half):
                owner = 2 * (2 * j + (o + odd) % 2) + (k + core) % 2
                at = pl.ds(pl.multiple_of(owner * rows, rows), rows)
                w_ref[at] = ref[o * half + j]
    out_ref[...] = jnp.dot(x_ref[...], w_ref[...], preferred_element_type=F32)


def projection(place, x, own, other):
    cols = own.shape[2]
    return pl.pallas_call(
        project,
        out_shape=jax.ShapeDtypeStruct((x.shape[0], cols), F32),
        in_specs=[pl.BlockSpec(memory_space=pltpu.SMEM)]
        + [pl.BlockSpec(memory_space=pltpu.VMEM)] * 3,
        out_specs=pl.BlockSpec(memory_space=pltpu.VMEM),
        scratch_shapes=[pltpu.VMEM((x.shape[1], cols), BF)],
        compiler_params=pltpu.CompilerParams(vmem_limit_bytes=32 * 1024 * 1024),
    )(place, x, own, other)


UNROLL = 4


def attend(gate_ref, q_ref, kv_ref, out_ref):
    heads = q_ref.shape[1] // HD
    vtok = kv_ref.shape[1] - NOTES
    pairs = kv_ref.shape[0] // 2
    factor = jnp.tanh(jnp.full((1, 1), gate_ref[0], F32))
    key = lax.broadcasted_iota(jnp.int32, (1, vtok), 1).astype(F32)
    four = (heads, 2, CAP, HD)

    def one(i):
        rows = pl.ds(pl.multiple_of(i * 2 * CAP, 2 * CAP), 2 * CAP)
        q = jnp.concatenate([q_ref[rows, h * HD : (h + 1) * HD] for h in range(heads)], axis=0)
        kv = kv_ref[pl.ds(2 * i, 2), :vtok].reshape(2 * vtok, 2 * HD)
        k, v = kv[:, :HD], kv[:, HD:]
        note = [kv_ref[2 * i + e, vtok:].astype(F32)[:1] for e in range(2)]
        s = lax.dot_general(q, k, (((1,), (1,)), ((), ())), preferred_element_type=F32)
        s = s.reshape(heads, 2, CAP, 2 * vtok) * (HD ** -0.5 / KEY_SCALE)
        s = [
            jnp.where((key < note[e][:, :HD])[None], s[:, e, :, e * vtok : (e + 1) * vtok], -jnp.inf)
            for e in range(2)
        ]
        s = jnp.stack(s, axis=1)
        top = jnp.max(s, axis=-1, keepdims=True)
        p = jnp.exp(s - top)
        total = jnp.sum(p, axis=-1, keepdims=True)
        zero = jnp.zeros_like(p[:, 0])
        left = jnp.stack([p[:, 0], zero], axis=1).reshape(-1, vtok)
        right = jnp.stack([zero, p[:, 1]], axis=1).reshape(-1, vtok)
        p = jnp.concatenate([left, right], axis=1).astype(BF)
        mixed = jnp.dot(p, v, preferred_element_type=F32)
        level = jnp.exp2(jnp.stack([n[:, HD:] for n in note])[None] - TOP_LEVEL)
        ans = mixed.reshape(four) * (factor / total) * level
        ans = ans.reshape(-1, HD).astype(BF)
        for h in range(heads):
            out_ref[rows, h * HD : (h + 1) * HD] = ans[h * 2 * CAP : (h + 1) * 2 * CAP]

    def body(i, carry):
        for u in range(UNROLL):
            one(i * UNROLL + u)
        return carry

    lax.fori_loop(0, pairs // UNROLL, body, 0)


def attention(gate, q, kv):
    smem = pl.BlockSpec(memory_space=pltpu.SMEM)
    vmem = pl.BlockSpec(memory_space=pltpu.VMEM)
    scores = q.size // HD * 2 * kv.shape[1]
    return pl.pallas_call(
        attend,
        out_shape=jax.ShapeDtypeStruct(q.shape, BF),
        in_specs=[smem, vmem, vmem],
        out_specs=vmem,
        cost_estimate=pl.CostEstimate(
            flops=4 * scores * HD, bytes_accessed=2 * kv.size, transcendentals=scores
        ),
        compiler_params=pltpu.CompilerParams(vmem_limit_bytes=32 * 1024 * 1024),
    )(gate, q, kv)


def shards(queries, vision, w_key, w_value, attn_gate, token_image, image_owner, image_len):
    n_doc = lax.axis_size("doc")
    n_seq = lax.axis_size("seq")
    n_z = n_seq // 2
    seq = lax.axis_index("seq")
    core = seq % 2
    z = seq // 2
    rows32, width = vision.shape[2], vision.shape[3]
    slice_w = width // n_doc
    swap = [(i, i ^ 1) for i in range(n_seq)]

    with jax.named_scope("vision_doc"):
        cols = jnp.stack([vision[0, 0, :, i * slice_w : (i + 1) * slice_w] for i in range(n_doc)])
        cols = lax.all_to_all(cols, "doc", split_axis=0, concat_axis=0, tiled=True)
        cols = cols.reshape(n_doc * rows32, slice_w)
    with jax.named_scope("vision_tensor"):
        x = lax.all_gather(cols, "tensor", axis=0, tiled=True)

    owners = jnp.arange(n_seq, dtype=jnp.int32)
    image_ids = token_image[0, :, 0]
    picked = image_ids[:, None] == owners[None, :]
    target = jnp.sum(jnp.where(picked, image_owner[0][None, :], 0), axis=1)
    onehot = (target[:, None] == owners[None, :]).astype(jnp.int32)
    ranks = jnp.cumsum(onehot, axis=0) - onehot
    slot = target * CAP + jnp.sum(ranks * onehot, axis=1)
    dispatch = (slot[:, None] == jnp.arange(n_seq * CAP, dtype=jnp.int32)[None, :]).astype(BF)
    with jax.named_scope("dispatch"):
        q = jnp.dot(dispatch.T, queries[0], preferred_element_type=F32).astype(BF)

    w = jnp.concatenate([w_key, w_value], axis=1)
    groups = [[2 * (2 * j + o) + c for j in range(n_z // 2)] for o in range(2) for c in range(2)]
    with jax.named_scope("weights_z"):
        near = lax.all_gather(w, "seq", axis=0, tiled=False, axis_index_groups=groups)
    with jax.named_scope("weights_pair"):
        beside = lax.ppermute(near, "seq", [(i, i ^ 2) for i in range(n_seq)])
    own = jnp.concatenate([near, beside], axis=0)
    with jax.named_scope("weights_core"):
        other = lax.ppermute(own, "seq", swap)
    own, other, q = lax.optimization_barrier((own, other, q))
    with jax.named_scope("project"):
        part = projection(jnp.stack([core, z % 2]), x, own, other)
    with jax.named_scope("reduce_doc"):
        part = part.reshape(-1, n_doc, rows32, w.shape[1])
        part = lax.all_to_all(part, "doc", split_axis=1, concat_axis=1, tiled=True)
        kv = jnp.sum(part, axis=1).reshape(-1, w.shape[1])
    keys = lax.reduce_precision(head_norm(kv[:, :HD]), 8, 7)
    values = lax.reduce_precision(kv[:, HD:], 8, 7)

    with jax.named_scope("kv_seq"):
        largest = jnp.max(jnp.abs(values), keepdims=True)
        level = jnp.ceil(jnp.log2(jnp.maximum(largest, 1e-30)))
        block = jnp.concatenate([keys * KEY_SCALE, values * jnp.exp2(TOP_LEVEL - level)], axis=1)
        lane = lax.broadcasted_iota(jnp.int32, (NOTES, 2 * HD), 1)
        notes = jnp.where(lane < HD, image_len.astype(F32), level)
        block = jnp.concatenate([block, notes], axis=0).astype(HF)
        blocks = lax.all_gather(block, "seq", axis=0, tiled=False)
    with jax.named_scope("attention"):
        answer = attention(attn_gate, q, blocks.astype(BF))
    with jax.named_scope("combine"):
        out = jnp.dot(dispatch, answer, preferred_element_type=F32)
    return out.astype(BF)[None]


def solution(mesh):
    placed = (
        P("doc", "seq", "tensor"),
        P("doc", "seq", "tensor", None),
        P(("doc", "seq"), "tensor"),
        P(("doc", "seq"), "tensor"),
        P(),
        P("doc", "seq", None),
        P("doc", None),
        P("doc", "seq"),
    )
    return jax.shard_map(
        shards, mesh=mesh, in_specs=placed, out_specs=P("doc", "seq", "tensor"), check_vma=False
    )
```

time: 207 us -> 186 us (0.90); the launches traced: 203 us -> 185 us
  blocking collectives: 97 us -> 123 us
  starting transfers between devices: 42.7 us -> 18.3 us
  waiting for transfers between devices: 23.1 us -> 11.5 us
  local copies, waits for them, and re-layouts: 11.9 us -> 3.81 us
  Pallas kernels: 9.15 us -> 6.92 us
    all_gather x2, blocking collectives: 73.9 us -> 111 us  [the longest x1 68.6 us: shards(): blocks = lax.all_gather(block, 'seq', axis=0, tiled=False)]
    ppermute x5 -> x0, starting transfers between devices: 27.6 us -> none  [the longest x1 8.58 us: shards(): theirs = lax.ppermute(mine, 'seq', swap)]
    ppermute x5 -> x0, waiting for transfers between devices: 15.7 us -> none  [the longest x1 6.68 us: shards(): p3 = lax.ppermute(s0, 'seq', chip_shift(n_seq, -3))]
    all_to_all x2 -> x1, blocking collectives: 23.1 us -> 11.9 us  [shards(): cols = lax.all_to_all(cols, 'doc', split_axis=0, concat_axis=0, tiled=True)]
    all_to_all x0 -> x1, waiting for transfers between devices: none -> 7.9 us  [shards(): part = lax.all_to_all(part, 'doc', split_axis=1, concat_axis=1, tiled=True)]
    concatenate x3 -> x1, local copies, waits for them, and re-layouts: 4.33 us -> 0.01 us  [shards(): block = jnp.concatenate([block, notes], axis=0).astype(HF)]
    unnamed x16 -> x4, local copies, waits for them, and re-layouts: 5.23 us -> 1.6 us
    all_to_all x0 -> x1, starting transfers between devices: none -> 3.47 us  [shards(): part = lax.all_to_all(part, 'doc', split_axis=1, concat_axis=1, tiled=True)]
  transfers between devices with their start and end apart: 8 -> 4, of which waited for: 6 -> 3; matrix products, arithmetic and copies ran while one was open for 3% -> 2% of each run, Pallas kernels for 0% -> 0%
where the time goes in v4:
time: 186 us; the launch traced here: 185 us
  blocking collectives  123 us (66%)
  starting transfers between devices  18.3 us (10%)
  between operations  15.6 us (8%)
  waiting for transfers between devices  11.5 us (6%)
  Pallas kernels  6.92 us (4%)
  other arithmetic  4.04 us (2%)
  local copies, waits for them, and re-layouts  3.81 us (2%)
    all_gather x1, blocking collectives, shards(): blocks = lax.all_gather(block, 'seq', axis=0, tiled=False)  68.6 us
    all_gather x1, blocking collectives, shards(): lax.all_gather(w, 'seq', axis=0, tiled=False, axis_index_groups=groups)  42.9 us
    ppermute x1, starting transfers between devices, shards(): other = lax.ppermute(own, 'seq', swap)  11.9 us
    all_to_all x1, blocking collectives, shards(): cols = lax.all_to_all(cols, 'doc', split_axis=0, concat_axis=0, tiled=True)  11.9 us
    all_to_all x1, waiting for transfers between devices, shards(): part = lax.all_to_all(part, 'doc', split_axis=1, concat_axis=1, tiled=True)  7.9 us
    pallas_call x1, Pallas kernels, attention(): pl.pallas_call(attend, out_shape=jax.ShapeDtypeStruct(q.shape, BF), in_sp...  5.58 us
  transfers between devices with their start and end apart: 4, of which 3 were waited for; matrix products, arithmetic and copies ran while one was open for 2% of the time, Pallas kernels for 0%

profile of v4, /device:TPU:1, one launch (start us, length us, event | category | flops | bytes accessed | tf_op | source)
XLA Modules:
  0.0 185.4 jit_solution(13985517913776246709)
XLA Ops:
  6.5 0.0 copy-start
  6.5 0.0 all-gather.4.cloned.1.call-start
  6.5 1.2 slice_bitcast_fusion.3
  7.7 0.1 pad_maximum_fusion.1
  7.8 11.9 %all_to_all.10 = bf16[4,32,2048]{2,1,0:T(8,128)(2,1)} all-to-all(bf16[4,32,2048]{2,1,0:T(8,128)(2,1)S(1)} %pad_maximum_fusion.1), channel_id=1, replica_groups=mesh['doc'=4,'seq'=64,'tensor'=4] {'doc'}, dimensions={0} | all-to-all | bytes 1048576 | tf_op jit(solution)/shard_map/vision_doc/all_to_all | solution.py:123
  19.7 0.0 all-gather.4.cloned.1.call-update
  19.7 0.7 pad_maximum_fusion.3
  20.4 42.9 %all-gather = bf16[512,256]{1,0:T(8,128)(2,1)S(1)} all-gather(bf16[32,256]{1,0:T(8,128)(2,1)S(1)} %pad_maximum_fusion.3), channel_id=2, replica_groups={{0,16,32,48,64,80,96,112,128,144,160,176,192,208,224,240},{4,20,36,52,6..., dimensions={0}, use_global_device_ids=true | all-gather | bytes 278528 | tf_op jit(solution)/shard_map/weights_z/all_gather | solution.py:142
  63.3 3.0 %collective-permute-start = (bf16[16,32,256]{2,1,0:T(8,128)(2,1)S(1)}, bf16[16,32,256]{2,1,0:T(8,128)(2,1)S(1)}, u32[]{:S(2)}, u32[]{:S(2)}) collective-permute-start(bf16[16,32,256]{2,1,0:T(8,128)(2,1)S(1)} %bitcast.49), channel_id=1, source_target_pairs={{0,8},{4,12},{8,0},{12,4},{16,24},{20,28},{24,16},{28,20},{32,40},... | collective-permute-start | bytes 786440 | tf_op jit(solution)/shard_map/weights_pair/ppermute | solution.py:144
  66.2 0.8 select_reduce_fusion
  67.1 0.6 reduce-window.6
  67.7 0.2 slice_reduce_fusion
  67.9 0.1 fusion.6
  68.0 2.8 %collective-permute-done = bf16[16,32,256]{2,1,0:T(8,128)(2,1)S(1)} collective-permute-done((bf16[16,32,256]{2,1,0:T(8,128)(2,1)S(1)}, bf16[16,32,256]{2,1,0:T(8,128)(2,1)S(1)}, u32[]{:S(2)}, u32[]{:S(2)}) %collective-permute-start) | collective-permute-done | bytes 262176 | tf_op jit(solution)/shard_map/weights_pair/ppermute | solution.py:144
  70.8 11.9 %collective-permute-start.1 = (bf16[32,32,256]{2,1,0:T(8,128)(2,1)S(1)}, bf16[32,32,256]{2,1,0:T(8,128)(2,1)S(1)}, u32[]{:S(2)}, u32[]{:S(2)}) collective-permute-start(bf16[32,32,256]{2,1,0:T(8,128)(2,1)S(1)} %pad_maximum_fusion.own_ref), channel_id=1, source_target_pairs={{0,4},{4,0},{8,12},{12,8},{16,20},{20,16},{24,28},{28,24},{32,36},... | collective-permute-start | bytes 1572872 | tf_op jit(solution)/shard_map/weights_core/ppermute | solution.py:147
  82.7 0.1 pad_add_fusion.place_ref
  82.8 0.0 copy-done
  82.8 0.6 convolution_convert_fusion.q_ref
  83.4 0.9 collective-permute-done.1.other_ref
  84.2 0.0 all-gather.4.cloned.1.call-done.x_ref
  84.2 0.0 copy-start.1
  84.2 1.6 copy-done.1
  85.8 1.3 project.1
  87.2 0.8 copy.11
  88.0 3.5 %all-to-all-start.1 = ((f32[4,4,32,256]{3,2,0,1:T(8,128)}), f32[4,4,32,256]{3,2,0,1:T(8,128)S(1)}, u32[]{:S(2)}, u32[]{:S(2)}) async-start(f32[4,4,32,256]{3,2,0,1:T(8,128)} %copy.11), calls=%async_computation.1 | async-start | bytes 1048576 | tf_op jit(solution)/shard_map/reduce_doc/all_to_all | solution.py:153
  92.8 7.9 %all-to-all-done.1 = f32[4,4,32,256]{3,2,0,1:T(8,128)S(1)} async-done(((f32[4,4,32,256]{3,2,0,1:T(8,128)}), f32[4,4,32,256]{3,2,0,1:T(8,128)S(1)}, u32[]{:S(2)}, u32[]{:S(2)}) %all-to-all-start.1) | async-done | bytes 524320 | tf_op jit(solution)/shard_map/reduce_doc/all_to_all | solution.py:153
  100.7 0.6 multiply_reduce_fusion
  102.1 0.1 multiply_convert_fusion.1
  102.3 68.6 %all-gather.5 = f16[64,144,256]{2,1,0:T(8,128)(2,1)S(1)} all-gather(f16[1,144,256]{2,1,0:T(8,128)(2,1)S(1)} %pad_maximum_fusion.2), channel_id=1, replica_groups=mesh['doc'=4,'seq'=64,'tensor'=4] {'seq'}, dimensions={0}, use_global_device_ids=true | all-gather | bytes 4792320 | tf_op jit(solution)/shard_map/kv_seq/all_gather | solution.py:165
  170.9 0.8 convert_element_type.32.kv_ref
  171.7 5.6 %attention.1 = bf16[512,1024]{1,0:T(8,128)(2,1)S(1)} custom-call(f32[1]{0:T(128)S(6)} %copy.14.gate_ref, bf16[512,1024]{1,0:T(8,128)(2,1)S(1)} %convolution_convert_fusion.q_ref, bf16[64,144,256]{2,1,0:T(8,128)(2,1)S(1)} %convert_element_type.32.kv_ref), custom_call_target="tpu_custom_call" | custom-call | flops 603979776 | bytes 4718592 | tf_op jit(solution)/shard_map/attention/pallas_call | solution.py:98
  177.3 1.3 fusion
  (11 shorter events, 0.2 us)
Async XLA Ops:
  6.5 76.3 %copy-start = (bf16[1,256,1024]{2,1,0:T(8,128)(2,1)S(1)}, bf16[1,256,1024]{2,1,0:T(8,128)(2,1)}, u32[]{:S(2)}) copy-start(bf16[1,256,1024]{2,1,0:T(8,128)(2,1)} %param.8) | copy-start | bytes 1572868
  6.5 77.7 %all-gather.4.cloned.1.call-start = ((), (), s32[]{:S(2)}) async-start(), calls=%async_computation.2 | async-start | bytes 2621440 | tf_op jit(solution)/shard_map/vision_tensor/all_gather | solution.py:126
  63.3 7.5 %collective-permute-start = (bf16[16,32,256]{2,1,0:T(8,128)(2,1)S(1)}, bf16[16,32,256]{2,1,0:T(8,128)(2,1)S(1)}, u32[]{:S(2)}, u32[]{:S(2)}) collective-permute-start(bf16[16,32,256]{2,1,0:T(8,128)(2,1)S(1)} %bitcast.49), channel_id=1, source_target_pairs={{0,8},{4,12},{8,0},{12,4},{16,24},{20,28},{24,16},{28,20},{32,40},... | collective-permute-start | bytes 786440 | tf_op jit(solution)/shard_map/weights_pair/ppermute | solution.py:144
  70.8 13.4 %collective-permute-start.1 = (bf16[32,32,256]{2,1,0:T(8,128)(2,1)S(1)}, bf16[32,32,256]{2,1,0:T(8,128)(2,1)S(1)}, u32[]{:S(2)}, u32[]{:S(2)}) collective-permute-start(bf16[32,32,256]{2,1,0:T(8,128)(2,1)S(1)} %pad_maximum_fusion.own_ref), channel_id=1, source_target_pairs={{0,4},{4,0},{8,12},{12,8},{16,20},{20,16},{24,28},{28,24},{32,36},... | collective-permute-start | bytes 1572872 | tf_op jit(solution)/shard_map/weights_core/ppermute | solution.py:147
  84.2 1.6 copy-start.1
  88.0 12.7 %all-to-all-start.1 = ((f32[4,4,32,256]{3,2,0,1:T(8,128)}), f32[4,4,32,256]{3,2,0,1:T(8,128)S(1)}, u32[]{:S(2)}, u32[]{:S(2)}) async-start(f32[4,4,32,256]{3,2,0,1:T(8,128)} %copy.11), calls=%async_computation.1 | async-start | bytes 1048576 | tf_op jit(solution)/shard_map/reduce_doc/all_to_all | solution.py:153
Sparse Core Ops, SparseCore 0:
  19.8 56.9 all-gather.3

commit v5 on v4

--- a/solution.py
+++ b/solution.py
@@ -19,30 +19,39 @@
     return x * lax.rsqrt(jnp.mean(x * x, axis=-1, keepdims=True) + 1e-06)
 
 
-def project(place_ref, x_ref, own_ref, other_ref, out_ref, w_ref):
+def project(place_ref, *refs):
+    *x_refs, own_ref, other_ref, out_ref, w_ref = refs
     rows = w_ref.shape[0] // (own_ref.shape[0] * 2)
     half = own_ref.shape[0] // 2
-    core, odd = place_ref[0], place_ref[1]
+    core, odd, tensor = place_ref[0], place_ref[1], place_ref[2]
     for k, ref in enumerate((own_ref, other_ref)):
         for o in range(2):
             for j in range(half):
                 owner = 2 * (2 * j + (o + odd) % 2) + (k + core) % 2
                 at = pl.ds(pl.multiple_of(owner * rows, rows), rows)
                 w_ref[at] = ref[o * half + j]
-    out_ref[...] = jnp.dot(x_ref[...], w_ref[...], preferred_element_type=F32)
-
-
-def projection(place, x, own, other):
-    cols = own.shape[2]
+    x = jnp.concatenate([ref[...] for ref in x_refs], axis=0)
+    part = jnp.dot(x, w_ref[...], preferred_element_type=F32)
+    n, n_doc = len(x_refs), out_ref.shape[0]
+    each = x.shape[0] // (n * n_doc)
+    for k in range(n):
+        source = (tensor + n - k) % n
+        at = pl.ds(pl.multiple_of(source * each, each), each)
+        for d in range(n_doc):
+            out_ref[d, at] = part[(k * n_doc + d) * each : (k * n_doc + d + 1) * each]
+
+
+def projection(place, xs, own, other, n_doc):
+    cols, depth = own.shape[2], xs[0].shape[1]
+    vmem = pl.BlockSpec(memory_space=pltpu.VMEM)
     return pl.pallas_call(
         project,
-        out_shape=jax.ShapeDtypeStruct((x.shape[0], cols), F32),
-        in_specs=[pl.BlockSpec(memory_space=pltpu.SMEM)]
-        + [pl.BlockSpec(memory_space=pltpu.VMEM)] * 3,
-        out_specs=pl.BlockSpec(memory_space=pltpu.VMEM),
-        scratch_shapes=[pltpu.VMEM((x.shape[1], cols), BF)],
+        out_shape=jax.ShapeDtypeStruct((n_doc, len(xs) * xs[0].shape[0] // n_doc, cols), F32),
+        in_specs=[pl.BlockSpec(memory_space=pltpu.SMEM)] + [vmem] * (len(xs) + 2),
+        out_specs=vmem,
+        scratch_shapes=[pltpu.VMEM((depth, cols), BF)],
         compiler_params=pltpu.CompilerParams(vmem_limit_bytes=32 * 1024 * 1024),
-    )(place, x, own, other)
+    )(place, *xs, own, other)
 
 
 UNROLL = 4
@@ -122,9 +131,19 @@
         cols = jnp.stack([vision[0, 0, :, i * slice_w : (i + 1) * slice_w] for i in range(n_doc)])
         cols = lax.all_to_all(cols, "doc", split_axis=0, concat_axis=0, tiled=True)
         cols = cols.reshape(n_doc * rows32, slice_w)
+    w = jnp.concatenate([w_key, w_value], axis=1)
+    cols, w = lax.optimization_barrier((cols, w))
+    n_tensor = lax.axis_size("tensor")
     with jax.named_scope("vision_tensor"):
-        x = lax.all_gather(cols, "tensor", axis=0, tiled=True)
-
+        xs = [cols] + [
+            lax.ppermute(cols, "tensor", [(i, (i + k) % n_tensor) for i in range(n_tensor)])
+            for k in range(1, n_tensor)
+        ]
+
+    groups = [[2 * (2 * j + o) + c for j in range(n_z // 2)] for o in range(2) for c in range(2)]
+    with jax.named_scope("weights_z"):
+        near = lax.all_gather(w, "seq", axis=0, tiled=False, axis_index_groups=groups)
+    near, token_image, *xs = lax.optimization_barrier((near, token_image, *xs))
     owners = jnp.arange(n_seq, dtype=jnp.int32)
     image_ids = token_image[0, :, 0]
     picked = image_ids[:, None] == owners[None, :]
@@ -136,10 +155,6 @@
     with jax.named_scope("dispatch"):
         q = jnp.dot(dispatch.T, queries[0], preferred_element_type=F32).astype(BF)
 
-    w = jnp.concatenate([w_key, w_value], axis=1)
-    groups = [[2 * (2 * j + o) + c for j in range(n_z // 2)] for o in range(2) for c in range(2)]
-    with jax.named_scope("weights_z"):
-        near = lax.all_gather(w, "seq", axis=0, tiled=False, axis_index_groups=groups)
     with jax.named_scope("weights_pair"):
         beside = lax.ppermute(near, "seq", [(i, i ^ 2) for i in range(n_seq)])
     own = jnp.concatenate([near, beside], axis=0)
@@ -147,11 +162,11 @@
         other = lax.ppermute(own, "seq", swap)
     own, other, q = lax.optimization_barrier((own, other, q))
     with jax.named_scope("project"):
-        part = projection(jnp.stack([core, z % 2]), x, own, other)
+        place = jnp.stack([core, z % 2, lax.axis_index("tensor")])
+        part = projection(place, xs, own, other, n_doc)
     with jax.named_scope("reduce_doc"):
-        part = part.reshape(-1, n_doc, rows32, w.shape[1])
-        part = lax.all_to_all(part, "doc", split_axis=1, concat_axis=1, tiled=True)
-        kv = jnp.sum(part, axis=1).reshape(-1, w.shape[1])
+        part = lax.all_to_all(part, "doc", split_axis=0, concat_axis=0, tiled=True)
+        kv = jnp.sum(part, axis=0)
     keys = lax.reduce_precision(head_norm(kv[:, :HD]), 8, 7)
     values = lax.reduce_precision(kv[:, HD:], 8, 7)
 

time: 186 us -> 183 us (0.984)
  starting transfers between devices: 18.3 us -> 35.2 us
  between operations: 15.6 us -> 2.23 us
  blocking collectives: 123 us -> 111 us
  waiting for transfers between devices: 11.5 us -> 17.7 us
    ppermute x0 -> x3, starting transfers between devices: none -> 11.9 us  [shards(): lax.ppermute(cols, 'tensor', [(i, (i + k) % n_tensor) for i in range(n_te...]
    all_to_all x1 -> x0, blocking collectives: 11.9 us -> none  [shards(): cols = lax.all_to_all(cols, 'doc', split_axis=0, concat_axis=0, tiled=True)]
    all_to_all x1 -> x2, waiting for transfers between devices: 7.9 us -> 14.1 us  [the longest x1 7.9 us: shards(): part = lax.all_to_all(part, 'doc', split_axis=0, concat_axis=0, tiled=True)]
    all_to_all x1 -> x2, starting transfers between devices: 3.47 us -> 8.48 us  [the longest x1 5.01 us: shards(): cols = lax.all_to_all(cols, 'doc', split_axis=0, concat_axis=0, tiled=True)]
  transfers between devices with their start and end apart: 4 -> 7, of which waited for: 3 -> 4; matrix products, arithmetic and copies ran while one was open for 2% -> 2% of each run, Pallas kernels for 0% -> 0%
where the time goes in v5:
time: 183 us
  blocking collectives  111 us (61%)
  starting transfers between devices  35.2 us (19%)
  waiting for transfers between devices  17.7 us (10%)
  Pallas kernels  7.71 us (4%)
  other arithmetic  4.77 us (3%)
  local copies, waits for them, and re-layouts  2.48 us (1%)
  between operations  2.23 us (1%)
  matrix products  1.84 us (1%)
    all_gather x1, blocking collectives, shards(): blocks = lax.all_gather(block, 'seq', axis=0, tiled=False)  68.6 us
    all_gather x1, blocking collectives, shards(): lax.all_gather(w, 'seq', axis=0, tiled=False, axis_index_groups=groups)  42.5 us
    ppermute x1, starting transfers between devices, shards(): other = lax.ppermute(own, 'seq', swap)  12.1 us
    ppermute x3, starting transfers between devices, shards(): lax.ppermute(cols, 'tensor', [(i, (i + k) % n_tensor) for i in range(n_te...  11.9 us
    all_to_all x1, waiting for transfers between devices, shards(): part = lax.all_to_all(part, 'doc', split_axis=0, concat_axis=0, tiled=True)  7.9 us
    all_to_all x1, waiting for transfers between devices, shards(): cols = lax.all_to_all(cols, 'doc', split_axis=0, concat_axis=0, tiled=True)  6.22 us
    pallas_call x1, Pallas kernels, attention(): pl.pallas_call(attend, out_shape=jax.ShapeDtypeStruct(q.shape, BF), in_sp...  5.58 us
    all_to_all x1, starting transfers between devices, shards(): cols = lax.all_to_all(cols, 'doc', split_axis=0, concat_axis=0, tiled=True)  5.01 us
  transfers between devices with their start and end apart: 7, of which 4 were waited for; matrix products, arithmetic and copies ran while one was open for 2% of the time, Pallas kernels for 0%

profile of v5, /device:TPU:1, one launch (start us, length us, event | category | flops | bytes accessed | tf_op | source)
XLA Modules:
  0.0 183.0 jit_solution(10208479956710870049)
XLA Ops:
  0.0 0.0 copy-start
  0.0 1.2 slice_bitcast_fusion.3
  1.2 0.9 pad_maximum_fusion
  2.1 5.0 %all-to-all-start = ((bf16[4,32,2048]{2,1,0:T(8,128)(2,1)}), bf16[4,32,2048]{2,1,0:T(8,128)(2,1)S(1)}, u32[]{:S(2)}, u32[]{:S(2)}) async-start(bf16[4,32,2048]{2,1,0:T(8,128)(2,1)} %pad_maximum_fusion), calls=%async_computation | async-start | bytes 1048576 | tf_op jit(solution)/shard_map/vision_doc/all_to_all | solution.py:132
  7.1 0.7 pad_maximum_fusion.2
  7.8 6.2 %all-to-all-done = bf16[4,32,2048]{2,1,0:T(8,128)(2,1)S(1)} async-done(((bf16[4,32,2048]{2,1,0:T(8,128)(2,1)}), bf16[4,32,2048]{2,1,0:T(8,128)(2,1)S(1)}, u32[]{:S(2)}, u32[]{:S(2)}) %all-to-all-start) | async-done | bytes 524320 | tf_op jit(solution)/shard_map/vision_doc/all_to_all | solution.py:132
  14.0 4.4 %collective-permute-start = (bf16[128,2048]{1,0:T(8,128)(2,1)S(1)}, bf16[128,2048]{1,0:T(8,128)(2,1)S(1)}, u32[]{:S(2)}, u32[]{:S(2)}) collective-permute-start(bf16[128,2048]{1,0:T(8,128)(2,1)S(1)} %bitcast.44), channel_id=1, source_target_pairs={{0,1},{1,2},{2,3},{3,0},{4,5},{5,6},{6,7},{7,4},{8,9},{9,10},{10,1... | collective-permute-start | bytes 1572872 | tf_op jit(solution)/shard_map/vision_tensor/ppermute | solution.py:139
  18.5 4.4 %collective-permute-start.1 = (bf16[128,2048]{1,0:T(8,128)(2,1)S(1)}, bf16[128,2048]{1,0:T(8,128)(2,1)S(1)}, u32[]{:S(2)}, u32[]{:S(2)}) collective-permute-start(bf16[128,2048]{1,0:T(8,128)(2,1)S(1)} %bitcast.45), channel_id=1, source_target_pairs={{0,2},{1,3},{2,0},{3,1},{4,6},{5,7},{6,4},{7,5},{8,10},{9,11},{10,... | collective-permute-start | bytes 1572872 | tf_op jit(solution)/shard_map/vision_tensor/ppermute | solution.py:139
  22.8 3.1 %collective-permute-start.2 = (bf16[128,2048]{1,0:T(8,128)(2,1)S(1)}, bf16[128,2048]{1,0:T(8,128)(2,1)S(1)}, u32[]{:S(2)}, u32[]{:S(2)}) collective-permute-start(bf16[128,2048]{1,0:T(8,128)(2,1)S(1)} %bitcast.46), channel_id=1, source_target_pairs={{0,3},{1,0},{2,1},{3,2},{4,7},{5,4},{6,5},{7,6},{8,11},{9,8},{10,9... | collective-permute-start | bytes 1572872 | tf_op jit(solution)/shard_map/vision_tensor/ppermute | solution.py:139
  25.9 0.1 pad_add_fusion.place_ref
  26.0 42.5 %all-gather = bf16[512,256]{1,0:T(8,128)(2,1)S(1)} all-gather(bf16[32,256]{1,0:T(8,128)(2,1)S(1)} %pad_maximum_fusion.2), channel_id=2, replica_groups={{0,16,32,48,64,80,96,112,128,144,160,176,192,208,224,240},{4,20,36,52,6..., dimensions={0}, use_global_device_ids=true | all-gather | bytes 278528 | tf_op jit(solution)/shard_map/weights_z/all_gather | solution.py:145
  68.5 0.0 collective-permute-done.refs_1_
  68.5 0.0 collective-permute-done.1.refs_2_
  68.5 0.0 collective-permute-done.2.refs_3_
  68.5 0.0 copy-start.1
  68.5 2.7 %collective-permute-start.3 = (bf16[16,32,256]{2,1,0:T(8,128)(2,1)S(1)}, bf16[16,32,256]{2,1,0:T(8,128)(2,1)S(1)}, u32[]{:S(2)}, u32[]{:S(2)}) collective-permute-start(bf16[16,32,256]{2,1,0:T(8,128)(2,1)S(1)} %bitcast.48), channel_id=1, source_target_pairs={{0,8},{4,12},{8,0},{12,4},{16,24},{20,28},{24,16},{28,20},{32,40},... | collective-permute-start | bytes 786440 | tf_op jit(solution)/shard_map/weights_pair/ppermute | solution.py:159
  71.2 0.8 select_reduce_fusion
  72.0 0.6 reduce-window.6
  72.7 0.2 slice_reduce_fusion
  72.9 2.7 %collective-permute-done.3 = bf16[16,32,256]{2,1,0:T(8,128)(2,1)S(1)} collective-permute-done((bf16[16,32,256]{2,1,0:T(8,128)(2,1)S(1)}, bf16[16,32,256]{2,1,0:T(8,128)(2,1)S(1)}, u32[]{:S(2)}, u32[]{:S(2)}) %collective-permute-start.3) | collective-permute-done | bytes 262176 | tf_op jit(solution)/shard_map/weights_pair/ppermute | solution.py:159
  75.7 12.1 %collective-permute-start.4 = (bf16[32,32,256]{2,1,0:T(8,128)(2,1)S(1)}, bf16[32,32,256]{2,1,0:T(8,128)(2,1)S(1)}, u32[]{:S(2)}, u32[]{:S(2)}) collective-permute-start(bf16[32,32,256]{2,1,0:T(8,128)(2,1)S(1)} %constant_dynamic-update-slice_fusion.refs_4_), channel_id=1, source_target_pairs={{0,4},{4,0},{8,12},{12,8},{16,20},{20,16},{24,28},{28,24},{32,36},... | collective-permute-start | bytes 1572872 | tf_op jit(solution)/shard_map/weights_core/ppermute | solution.py:162
  87.8 0.1 fusion.6
  87.9 0.0 copy-done.1
  87.9 0.0 copy-done
  87.9 0.6 convolution_convert_fusion.q_ref
  88.5 0.8 collective-permute-done.4.refs_5_
  89.3 0.0 copy-start.2
  89.3 1.0 copy-done.2
  90.3 2.1 %project.1 = f32[4,128,256]{2,1,0:T(8,128)} custom-call(s32[3]{0:T(128)S(1)} %pad_add_fusion.place_ref, bf16[128,2048]{1,0:T(8,128)(2,1)S(1)} %bitcast.47, bf16[128,2048]{1,0:T(8,128)(2,1)S(1)} %collective-permute-done.refs_1_, bf16[128,2048]{1,0:T(8,128)(2,1)S(1)} %collective-permute-done.1.refs_2_, bf16[128,2048]{1,0:T(8,128)(2,1)S(1)} %copy-done.2, ...), custom_call_target="tpu_custom_call" | custom-call | tf_op jit(solution)/shard_map/project/pallas_call | solution.py:47
  92.5 3.5 %all-to-all-start.1 = ((f32[4,128,256]{2,1,0:T(8,128)}), f32[4,128,256]{2,1,0:T(8,128)S(1)}, u32[]{:S(2)}, u32[]{:S(2)}) async-start(f32[4,128,256]{2,1,0:T(8,128)} %project.1), calls=%async_computation.1 | async-start | bytes 1048576 | tf_op jit(solution)/shard_map/reduce_doc/all_to_all | solution.py:168
  97.2 7.9 %all-to-all-done.1 = f32[4,128,256]{2,1,0:T(8,128)S(1)} async-done(((f32[4,128,256]{2,1,0:T(8,128)}), f32[4,128,256]{2,1,0:T(8,128)S(1)}, u32[]{:S(2)}, u32[]{:S(2)}) %all-to-all-start.1) | async-done | bytes 524320 | tf_op jit(solution)/shard_map/reduce_doc/all_to_all | solution.py:168
  105.2 0.6 multiply_reduce_fusion
  106.6 0.1 multiply_convert_fusion.1
  106.7 68.6 %all-gather.2 = f16[64,144,256]{2,1,0:T(8,128)(2,1)S(1)} all-gather(f16[1,144,256]{2,1,0:T(8,128)(2,1)S(1)} %pad_maximum_fusion.1), channel_id=1, replica_groups=mesh['doc'=4,'seq'=64,'tensor'=4] {'seq'}, dimensions={0}, use_global_device_ids=true | all-gather | bytes 4792320 | tf_op jit(solution)/shard_map/kv_seq/all_gather | solution.py:180
  175.3 0.8 convert_element_type.32.kv_ref
  176.1 5.6 %attention.1 = bf16[512,1024]{1,0:T(8,128)(2,1)S(1)} custom-call(f32[1]{0:T(128)S(6)} %copy.14.gate_ref, bf16[512,1024]{1,0:T(8,128)(2,1)S(1)} %convolution_convert_fusion.q_ref, bf16[64,144,256]{2,1,0:T(8,128)(2,1)S(1)} %convert_element_type.32.kv_ref), custom_call_target="tpu_custom_call" | custom-call | flops 603979776 | bytes 4718592 | tf_op jit(solution)/shard_map/attention/pallas_call | solution.py:107
  181.7 1.3 fusion
  (12 shorter events, 0.2 us)
Async XLA Ops:
  0.0 87.9 %copy-start = (bf16[1,256,1024]{2,1,0:T(8,128)(2,1)S(1)}, bf16[1,256,1024]{2,1,0:T(8,128)(2,1)}, u32[]{:S(2)}) copy-start(bf16[1,256,1024]{2,1,0:T(8,128)(2,1)} %param.8) | copy-start | bytes 1572868
  2.1 11.9 %all-to-all-start = ((bf16[4,32,2048]{2,1,0:T(8,128)(2,1)}), bf16[4,32,2048]{2,1,0:T(8,128)(2,1)S(1)}, u32[]{:S(2)}, u32[]{:S(2)}) async-start(bf16[4,32,2048]{2,1,0:T(8,128)(2,1)} %pad_maximum_fusion), calls=%async_computation | async-start | bytes 1048576 | tf_op jit(solution)/shard_map/vision_doc/all_to_all | solution.py:132
  14.0 54.5 %collective-permute-start = (bf16[128,2048]{1,0:T(8,128)(2,1)S(1)}, bf16[128,2048]{1,0:T(8,128)(2,1)S(1)}, u32[]{:S(2)}, u32[]{:S(2)}) collective-permute-start(bf16[128,2048]{1,0:T(8,128)(2,1)S(1)} %bitcast.44), channel_id=1, source_target_pairs={{0,1},{1,2},{2,3},{3,0},{4,5},{5,6},{6,7},{7,4},{8,9},{9,10},{10,1... | collective-permute-start | bytes 1572872 | tf_op jit(solution)/shard_map/vision_tensor/ppermute | solution.py:139
  18.5 50.0 %collective-permute-start.1 = (bf16[128,2048]{1,0:T(8,128)(2,1)S(1)}, bf16[128,2048]{1,0:T(8,128)(2,1)S(1)}, u32[]{:S(2)}, u32[]{:S(2)}) collective-permute-start(bf16[128,2048]{1,0:T(8,128)(2,1)S(1)} %bitcast.45), channel_id=1, source_target_pairs={{0,2},{1,3},{2,0},{3,1},{4,6},{5,7},{6,4},{7,5},{8,10},{9,11},{10,... | collective-permute-start | bytes 1572872 | tf_op jit(solution)/shard_map/vision_tensor/ppermute | solution.py:139
  22.8 45.7 %collective-permute-start.2 = (bf16[128,2048]{1,0:T(8,128)(2,1)S(1)}, bf16[128,2048]{1,0:T(8,128)(2,1)S(1)}, u32[]{:S(2)}, u32[]{:S(2)}) collective-permute-start(bf16[128,2048]{1,0:T(8,128)(2,1)S(1)} %bitcast.46), channel_id=1, source_target_pairs={{0,3},{1,0},{2,1},{3,2},{4,7},{5,4},{6,5},{7,6},{8,11},{9,8},{10,9... | collective-permute-start | bytes 1572872 | tf_op jit(solution)/shard_map/vision_tensor/ppermute | solution.py:139
  68.5 19.4 %copy-start.1 = (bf16[128,2048]{1,0:T(8,128)(2,1)}, bf16[128,2048]{1,0:T(8,128)(2,1)S(1)}, u32[]{:S(2)}) copy-start(bf16[128,2048]{1,0:T(8,128)(2,1)S(1)} %collective-permute-done.2.refs_3_) | copy-start | bytes 1572868
  68.5 7.1 %collective-permute-start.3 = (bf16[16,32,256]{2,1,0:T(8,128)(2,1)S(1)}, bf16[16,32,256]{2,1,0:T(8,128)(2,1)S(1)}, u32[]{:S(2)}, u32[]{:S(2)}) collective-permute-start(bf16[16,32,256]{2,1,0:T(8,128)(2,1)S(1)} %bitcast.48), channel_id=1, source_target_pairs={{0,8},{4,12},{8,0},{12,4},{16,24},{20,28},{24,16},{28,20},{32,40},... | collective-permute-start | bytes 786440 | tf_op jit(solution)/shard_map/weights_pair/ppermute | solution.py:159
  75.7 13.6 %collective-permute-start.4 = (bf16[32,32,256]{2,1,0:T(8,128)(2,1)S(1)}, bf16[32,32,256]{2,1,0:T(8,128)(2,1)S(1)}, u32[]{:S(2)}, u32[]{:S(2)}) collective-permute-start(bf16[32,32,256]{2,1,0:T(8,128)(2,1)S(1)} %constant_dynamic-update-slice_fusion.refs_4_), channel_id=1, source_target_pairs={{0,4},{4,0},{8,12},{12,8},{16,20},{20,16},{24,28},{28,24},{32,36},... | collective-permute-start | bytes 1572872 | tf_op jit(solution)/shard_map/weights_core/ppermute | solution.py:162
  89.3 1.0 copy-start.2
  92.5 12.7 %all-to-all-start.1 = ((f32[4,128,256]{2,1,0:T(8,128)}), f32[4,128,256]{2,1,0:T(8,128)S(1)}, u32[]{:S(2)}, u32[]{:S(2)}) async-start(f32[4,128,256]{2,1,0:T(8,128)} %project.1), calls=%async_computation.1 | async-start | bytes 1048576 | tf_op jit(solution)/shard_map/reduce_doc/all_to_all | solution.py:168

commit v6 on v4

--- a/solution.py
+++ b/solution.py
@@ -17,6 +17,26 @@
 
 def head_norm(x):
     return x * lax.rsqrt(jnp.mean(x * x, axis=-1, keepdims=True) + 1e-06)
+
+
+def spread(v_ref, out_ref):
+    n_doc, copies, _, width = out_ref.shape
+    for d in range(n_doc):
+        part = v_ref[:, d * width : (d + 1) * width]
+        for t in range(copies):
+            out_ref[d, t] = part
+
+
+def spreading(v, n_doc, copies):
+    vmem = pl.BlockSpec(memory_space=pltpu.VMEM)
+    shape = (n_doc, copies, v.shape[0], v.shape[1] // n_doc)
+    return pl.pallas_call(
+        spread,
+        out_shape=jax.ShapeDtypeStruct(shape, v.dtype),
+        in_specs=[vmem],
+        out_specs=vmem,
+        compiler_params=pltpu.CompilerParams(vmem_limit_bytes=32 * 1024 * 1024),
+    )(v)
 
 
 def project(place_ref, x_ref, own_ref, other_ref, out_ref, w_ref):
@@ -34,12 +54,12 @@
 
 def projection(place, x, own, other):
     cols = own.shape[2]
+    vmem = pl.BlockSpec(memory_space=pltpu.VMEM)
     return pl.pallas_call(
         project,
         out_shape=jax.ShapeDtypeStruct((x.shape[0], cols), F32),
-        in_specs=[pl.BlockSpec(memory_space=pltpu.SMEM)]
-        + [pl.BlockSpec(memory_space=pltpu.VMEM)] * 3,
-        out_specs=pl.BlockSpec(memory_space=pltpu.VMEM),
+        in_specs=[pl.BlockSpec(memory_space=pltpu.SMEM), vmem, vmem, vmem],
+        out_specs=vmem,
         scratch_shapes=[pltpu.VMEM((x.shape[1], cols), BF)],
         compiler_params=pltpu.CompilerParams(vmem_limit_bytes=32 * 1024 * 1024),
     )(place, x, own, other)
@@ -118,13 +138,17 @@
     slice_w = width // n_doc
     swap = [(i, i ^ 1) for i in range(n_seq)]
 
-    with jax.named_scope("vision_doc"):
-        cols = jnp.stack([vision[0, 0, :, i * slice_w : (i + 1) * slice_w] for i in range(n_doc)])
-        cols = lax.all_to_all(cols, "doc", split_axis=0, concat_axis=0, tiled=True)
-        cols = cols.reshape(n_doc * rows32, slice_w)
-    with jax.named_scope("vision_tensor"):
-        x = lax.all_gather(cols, "tensor", axis=0, tiled=True)
-
+    n_tensor = lax.axis_size("tensor")
+    w = jnp.concatenate([w_key, w_value], axis=1)
+    with jax.named_scope("vision_doc_tensor"):
+        x = spreading(vision[0, 0], n_doc, n_tensor).reshape(-1, rows32, slice_w)
+        x = lax.all_to_all(x, ("doc", "tensor"), split_axis=0, concat_axis=0, tiled=True)
+        x = x.reshape(-1, slice_w)
+
+    groups = [[2 * (2 * j + o) + c for j in range(n_z // 2)] for o in range(2) for c in range(2)]
+    with jax.named_scope("weights_z"):
+        near = lax.all_gather(w, "seq", axis=0, tiled=False, axis_index_groups=groups)
+    near, token_image, x = lax.optimization_barrier((near, token_image, x))
     owners = jnp.arange(n_seq, dtype=jnp.int32)
     image_ids = token_image[0, :, 0]
     picked = image_ids[:, None] == owners[None, :]
@@ -136,10 +160,6 @@
     with jax.named_scope("dispatch"):
         q = jnp.dot(dispatch.T, queries[0], preferred_element_type=F32).astype(BF)
 
-    w = jnp.concatenate([w_key, w_value], axis=1)
-    groups = [[2 * (2 * j + o) + c for j in range(n_z // 2)] for o in range(2) for c in range(2)]
-    with jax.named_scope("weights_z"):
-        near = lax.all_gather(w, "seq", axis=0, tiled=False, axis_index_groups=groups)
     with jax.named_scope("weights_pair"):
         beside = lax.ppermute(near, "seq", [(i, i ^ 2) for i in range(n_seq)])
     own = jnp.concatenate([near, beside], axis=0)
@@ -149,9 +169,9 @@
     with jax.named_scope("project"):
         part = projection(jnp.stack([core, z % 2]), x, own, other)
     with jax.named_scope("reduce_doc"):
-        part = part.reshape(-1, n_doc, rows32, w.shape[1])
-        part = lax.all_to_all(part, "doc", split_axis=1, concat_axis=1, tiled=True)
-        kv = jnp.sum(part, axis=1).reshape(-1, w.shape[1])
+        part = part.reshape(n_doc, -1, w.shape[1])
+        part = lax.all_to_all(part, "doc", split_axis=0, concat_axis=0, tiled=True)
+        kv = jnp.sum(part, axis=0)
     keys = lax.reduce_precision(head_norm(kv[:, :HD]), 8, 7)
     values = lax.reduce_precision(kv[:, HD:], 8, 7)
 

time: 186 us -> 166 us (0.89)
  between operations: 15.6 us -> 2.21 us
  blocking collectives: 123 us -> 112 us
  starting transfers between devices: 18.3 us -> 23 us
  Pallas kernels: 6.92 us -> 9.22 us
  local copies, waits for them, and re-layouts: 3.81 us -> 1.8 us
    all_to_all x1 -> x0, blocking collectives: 11.9 us -> none  [shards(): cols = lax.all_to_all(cols, 'doc', split_axis=0, concat_axis=0, tiled=True)]
    all_to_all x1 -> x2, starting transfers between devices: 3.47 us -> 12.2 us  [the longest x1 7.73 us: shards(): lax.all_to_all(x, ('doc', 'tensor'), split_axis=0, concat_axis=0, tiled=T...]
    ppermute x1, starting transfers between devices: 11.9 us -> 8.72 us  [shards(): other = lax.ppermute(own, 'seq', swap)]
    all_to_all x1 -> x2, waiting for transfers between devices: 7.9 us -> 7.79 us  [the longest x1 7.78 us: shards(): part = lax.all_to_all(part, 'doc', split_axis=0, concat_axis=0, tiled=True)]
  transfers between devices with their start and end apart: 4 -> 4, of which waited for: 3 -> 2; matrix products, arithmetic and copies ran while one was open for 2% -> 2% of each run, Pallas kernels for 0% -> 0%
where the time goes in v6:
time: 166 us
  blocking collectives  112 us (67%)
  starting transfers between devices  23 us (14%)
  waiting for transfers between devices  11.8 us (7%)
  Pallas kernels  9.22 us (6%)
  matrix products  2.84 us (2%)
  other arithmetic  2.5 us (2%)
  between operations  2.21 us (1%)
  local copies, waits for them, and re-layouts  1.8 us (1%)
    all_gather x1, blocking collectives, shards(): blocks = lax.all_gather(block, 'seq', axis=0, tiled=False)  68.7 us
    all_gather x1, blocking collectives, shards(): lax.all_gather(w, 'seq', axis=0, tiled=False, axis_index_groups=groups)  43.6 us
    ppermute x1, starting transfers between devices, shards(): other = lax.ppermute(own, 'seq', swap)  8.72 us
    all_to_all x1, waiting for transfers between devices, shards(): part = lax.all_to_all(part, 'doc', split_axis=0, concat_axis=0, tiled=True)  7.78 us
    all_to_all x1, starting transfers between devices, shards(): lax.all_to_all(x, ('doc', 'tensor'), split_axis=0, concat_axis=0, tiled=T...  7.73 us
    pallas_call x1, Pallas kernels, attention(): pl.pallas_call(attend, out_shape=jax.ShapeDtypeStruct(q.shape, BF), in_sp...  5.61 us
    all_to_all x1, starting transfers between devices, shards(): part = lax.all_to_all(part, 'doc', split_axis=0, concat_axis=0, tiled=True)  4.52 us
    ppermute x1, waiting for transfers between devices, shards(): beside = lax.ppermute(near, 'seq', [(i, i ^ 2) for i in range(n_seq)])  4.05 us
  transfers between devices with their start and end apart: 4, of which 2 were waited for; matrix products, arithmetic and copies ran while one was open for 2% of the time, Pallas kernels for 0%

profile of v6, /device:TPU:1, one launch (start us, length us, event | category | flops | bytes accessed | tf_op | source)
XLA Modules:
  0.0 165.7 jit_solution(14478922809769678228)
XLA Ops:
  0.0 0.0 copy-start
  0.0 0.0 copy-start.2
  0.0 1.1 copy-done.2
  1.1 1.5 vision_doc_tensor.1
  2.6 0.0 copy-start.3
  2.6 0.0 copy-start.4
  2.6 0.0 copy-start.5
  2.6 0.0 copy-start.6
  2.6 7.7 %all-to-all-start = ((bf16[16,32,2048]{2,1,0:T(8,128)(2,1)}), bf16[16,32,2048]{2,1,0:T(8,128)(2,1)S(1)}, u32[]{:S(2)}, u32[]{:S(2)}) async-start(bf16[16,32,2048]{2,1,0:T(8,128)(2,1)} %bitcast.2), calls=%async_computation | async-start | bytes 4194304 | tf_op jit(solution)/shard_map/vision_doc_tensor/all_to_all | solution.py:145
  10.4 0.1 pad_add_fusion.place_ref
  10.4 0.0 copy-done.3
  10.4 0.0 copy-done.4
  10.5 43.6 %all-gather = bf16[512,256]{1,0:T(8,128)(2,1)S(1)} all-gather(bf16[32,256]{1,0:T(8,128)(2,1)S(1)} %pad_maximum_fusion.1), channel_id=2, replica_groups={{0,16,32,48,64,80,96,112,128,144,160,176,192,208,224,240},{4,20,36,52,6..., dimensions={0}, use_global_device_ids=true | all-gather | bytes 278528 | tf_op jit(solution)/shard_map/weights_z/all_gather | solution.py:150
  54.1 0.0 all-to-all-done
  54.1 2.1 %collective-permute-start = (bf16[16,32,256]{2,1,0:T(8,128)(2,1)S(1)}, bf16[16,32,256]{2,1,0:T(8,128)(2,1)S(1)}, u32[]{:S(2)}, u32[]{:S(2)}) collective-permute-start(bf16[16,32,256]{2,1,0:T(8,128)(2,1)S(1)} %bitcast.40), channel_id=1, source_target_pairs={{0,8},{4,12},{8,0},{12,4},{16,24},{20,28},{24,16},{28,20},{32,40},... | collective-permute-start | bytes 786440 | tf_op jit(solution)/shard_map/weights_pair/ppermute | solution.py:164
  56.1 0.0 copy-done.5
  56.1 0.0 copy-done.6
  56.1 0.1 select_reduce_fusion
  56.3 0.6 reduce-window.6
  56.9 0.2 slice_reduce_fusion
  57.1 4.0 %collective-permute-done = bf16[16,32,256]{2,1,0:T(8,128)(2,1)S(1)} collective-permute-done((bf16[16,32,256]{2,1,0:T(8,128)(2,1)S(1)}, bf16[16,32,256]{2,1,0:T(8,128)(2,1)S(1)}, u32[]{:S(2)}, u32[]{:S(2)}) %collective-permute-start) | collective-permute-done | bytes 262176 | tf_op jit(solution)/shard_map/weights_pair/ppermute | solution.py:164
  61.2 8.7 %collective-permute-start.1 = (bf16[32,32,256]{2,1,0:T(8,128)(2,1)S(1)}, bf16[32,32,256]{2,1,0:T(8,128)(2,1)S(1)}, u32[]{:S(2)}, u32[]{:S(2)}) collective-permute-start(bf16[32,32,256]{2,1,0:T(8,128)(2,1)S(1)} %constant_dynamic-update-slice_fusion.own_ref), channel_id=1, source_target_pairs={{0,4},{4,0},{8,12},{12,8},{16,20},{20,16},{24,28},{28,24},{32,36},... | collective-permute-start | bytes 1572872 | tf_op jit(solution)/shard_map/weights_core/ppermute | solution.py:167
  69.9 0.1 fusion.6
  70.0 0.0 copy-done
  70.0 1.5 convolution_convert_fusion.q_ref
  71.6 0.0 collective-permute-done.1.other_ref
  71.6 2.1 %project.1 = f32[512,256]{1,0:T(8,128)} custom-call(s32[2]{0:T(128)S(1)} %pad_add_fusion.place_ref, bf16[512,2048]{1,0:T(8,128)(2,1)S(1)} %bitcast.38, bf16[32,32,256]{2,1,0:T(8,128)(2,1)S(1)} %constant_dynamic-update-slice_fusion.own_ref, bf16[32,32,256]{2,1,0:T(8,128)(2,1)S(1)} %collective-permute-done.1.other_ref), custom_call_target="tpu_custom_call" | custom-call | tf_op jit(solution)/shard_map/project/pallas_call | solution.py:58
  73.7 4.5 %all-to-all-start.1 = ((f32[4,128,256]{2,1,0:T(8,128)}), f32[4,128,256]{2,1,0:T(8,128)S(1)}, u32[]{:S(2)}, u32[]{:S(2)}) async-start(f32[4,128,256]{2,1,0:T(8,128)} %bitcast.11), calls=%async_computation.1 | async-start | bytes 1048576 | tf_op jit(solution)/shard_map/reduce_doc/all_to_all | solution.py:173
  79.5 7.8 %all-to-all-done.1 = f32[4,128,256]{2,1,0:T(8,128)S(1)} async-done(((f32[4,128,256]{2,1,0:T(8,128)}), f32[4,128,256]{2,1,0:T(8,128)S(1)}, u32[]{:S(2)}, u32[]{:S(2)}) %all-to-all-start.1) | async-done | bytes 524320 | tf_op jit(solution)/shard_map/reduce_doc/all_to_all | solution.py:173
  87.4 0.6 multiply_reduce_fusion
  88.7 0.1 multiply_convert_fusion.1
  88.9 68.7 %all-gather.2 = f16[64,144,256]{2,1,0:T(8,128)(2,1)S(1)} all-gather(f16[1,144,256]{2,1,0:T(8,128)(2,1)S(1)} %pad_maximum_fusion), channel_id=1, replica_groups=mesh['doc'=4,'seq'=64,'tensor'=4] {'seq'}, dimensions={0}, use_global_device_ids=true | all-gather | bytes 4792320 | tf_op jit(solution)/shard_map/kv_seq/all_gather | solution.py:185
  157.6 0.0 copy-start.1
  157.6 0.8 convert_element_type.32.kv_ref
  158.4 0.4 copy-done.1
  158.8 5.6 %attention.1 = bf16[512,1024]{1,0:T(8,128)(2,1)S(1)} custom-call(f32[1]{0:T(128)S(6)} %copy.14.gate_ref, bf16[512,1024]{1,0:T(8,128)(2,1)S(1)} %copy-done.1, bf16[64,144,256]{2,1,0:T(8,128)(2,1)S(1)} %convert_element_type.32.kv_ref), custom_call_target="tpu_custom_call" | custom-call | flops 603979776 | bytes 4718592 | tf_op jit(solution)/shard_map/attention/pallas_call | solution.py:118
  164.5 1.3 fusion
  (13 shorter events, 0.2 us)
Async XLA Ops:
  0.0 70.0 %copy-start = (bf16[1,256,1024]{2,1,0:T(8,128)(2,1)S(1)}, bf16[1,256,1024]{2,1,0:T(8,128)(2,1)}, u32[]{:S(2)}) copy-start(bf16[1,256,1024]{2,1,0:T(8,128)(2,1)} %param.8) | copy-start | bytes 1572868
  0.0 1.1 copy-start.2
  2.6 7.9 %copy-start.3 = (bf16[32,128]{1,0:T(8,128)(2,1)S(1)}, bf16[32,128]{1,0:T(8,128)(2,1)}, u32[]{:S(2)}) copy-start(bf16[32,128]{1,0:T(8,128)(2,1)} %param.11) | copy-start | bytes 24580
  2.6 7.9 %copy-start.4 = (bf16[32,128]{1,0:T(8,128)(2,1)S(1)}, bf16[32,128]{1,0:T(8,128)(2,1)}, u32[]{:S(2)}) copy-start(bf16[32,128]{1,0:T(8,128)(2,1)} %param.10) | copy-start | bytes 24580
  2.6 53.5 %copy-start.5 = (s32[1,256,1]{1,2,0:T(1,128)S(1)}, s32[1,256,1]{1,2,0:T(1,128)}, u32[]{:S(2)}) copy-start(s32[1,256,1]{1,2,0:T(1,128)} %param.13) | copy-start | bytes 3076
  2.6 53.5 %copy-start.6 = (s32[1,64]{1,0:T(1,128)S(1)}, s32[1,64]{1,0:T(1,128)}, u32[]{:S(2)}) copy-start(s32[1,64]{1,0:T(1,128)} %param.14) | copy-start | bytes 772
  2.6 51.5 %all-to-all-start = ((bf16[16,32,2048]{2,1,0:T(8,128)(2,1)}), bf16[16,32,2048]{2,1,0:T(8,128)(2,1)S(1)}, u32[]{:S(2)}, u32[]{:S(2)}) async-start(bf16[16,32,2048]{2,1,0:T(8,128)(2,1)} %bitcast.2), calls=%async_computation | async-start | bytes 4194304 | tf_op jit(solution)/shard_map/vision_doc_tensor/all_to_all | solution.py:145
  54.1 7.1 %collective-permute-start = (bf16[16,32,256]{2,1,0:T(8,128)(2,1)S(1)}, bf16[16,32,256]{2,1,0:T(8,128)(2,1)S(1)}, u32[]{:S(2)}, u32[]{:S(2)}) collective-permute-start(bf16[16,32,256]{2,1,0:T(8,128)(2,1)S(1)} %bitcast.40), channel_id=1, source_target_pairs={{0,8},{4,12},{8,0},{12,4},{16,24},{20,28},{24,16},{28,20},{32,40},... | collective-permute-start | bytes 786440 | tf_op jit(solution)/shard_map/weights_pair/ppermute | solution.py:164
  61.2 10.4 %collective-permute-start.1 = (bf16[32,32,256]{2,1,0:T(8,128)(2,1)S(1)}, bf16[32,32,256]{2,1,0:T(8,128)(2,1)S(1)}, u32[]{:S(2)}, u32[]{:S(2)}) collective-permute-start(bf16[32,32,256]{2,1,0:T(8,128)(2,1)S(1)} %constant_dynamic-update-slice_fusion.own_ref), channel_id=1, source_target_pairs={{0,4},{4,0},{8,12},{12,8},{16,20},{20,16},{24,28},{28,24},{32,36},... | collective-permute-start | bytes 1572872 | tf_op jit(solution)/shard_map/weights_core/ppermute | solution.py:167
  73.7 13.6 %all-to-all-start.1 = ((f32[4,128,256]{2,1,0:T(8,128)}), f32[4,128,256]{2,1,0:T(8,128)S(1)}, u32[]{:S(2)}, u32[]{:S(2)}) async-start(f32[4,128,256]{2,1,0:T(8,128)} %bitcast.11), calls=%async_computation.1 | async-start | bytes 1048576 | tf_op jit(solution)/shard_map/reduce_doc/all_to_all | solution.py:173
  157.6 1.2 copy-start.1

commit v7 on v6

--- a/solution.py
+++ b/solution.py
@@ -155,7 +155,11 @@
     target = jnp.sum(jnp.where(picked, image_owner[0][None, :], 0), axis=1)
     onehot = (target[:, None] == owners[None, :]).astype(jnp.int32)
     ranks = jnp.cumsum(onehot, axis=0) - onehot
-    slot = target * CAP + jnp.sum(ranks * onehot, axis=1)
+    step, odd = target // 4, (target // 2 + z) % 2
+    half = n_seq // 8
+    later = n_seq // 2 + jnp.where(step // half == core, 0, 2 * half) + 2 * (step % half)
+    place = jnp.where(odd == 0, 2 * step, later) + target % 2
+    slot = place * CAP + jnp.sum(ranks * onehot, axis=1)
     dispatch = (slot[:, None] == jnp.arange(n_seq * CAP, dtype=jnp.int32)[None, :]).astype(BF)
     with jax.named_scope("dispatch"):
         q = jnp.dot(dispatch.T, queries[0], preferred_element_type=F32).astype(BF)
@@ -182,11 +186,33 @@
         lane = lax.broadcasted_iota(jnp.int32, (NOTES, 2 * HD), 1)
         notes = jnp.where(lane < HD, image_len.astype(F32), level)
         block = jnp.concatenate([block, notes], axis=0).astype(HF)
-        blocks = lax.all_gather(block, "seq", axis=0, tiled=False)
-    with jax.named_scope("attention"):
-        answer = attention(attn_gate, q, blocks.astype(BF))
+        groups = [[4 * j + 2 * o + c for j in range(n_z // 2) for c in range(2)] for o in range(2)]
+        blocks = lax.all_gather(block, "seq", axis=0, tiled=False, axis_index_groups=groups)
+        many = blocks.shape[0] // 2
+        give = lax.dynamic_slice_in_dim(blocks, core * many, many, axis=0)
+        beside = [(i, (i + (2 if i % 2 else -2)) % n_seq) for i in range(n_seq)]
+        fetched = lax.ppermute(give, "seq", beside)
+    answers, start = [], 0
+
+    def answer(held):
+        size = held.shape[0] * CAP
+        return attention(attn_gate, q[start : start + size], held.astype(BF))
+
+    with jax.named_scope("attention_first"):
+        first = answer(blocks)
+        fetched, first = lax.optimization_barrier((fetched, first))
+        answers, start = [first], first.shape[0]
+    with jax.named_scope("kv_core"):
+        swapped = lax.ppermute(fetched, "seq", swap)
+    with jax.named_scope("attention_rest"):
+        for held in (fetched, swapped):
+            answers.append(answer(held))
+            start += answers[-1].shape[0]
     with jax.named_scope("combine"):
-        out = jnp.dot(dispatch, answer, preferred_element_type=F32)
+        cut = start - answers[-1].shape[0]
+        early = jnp.concatenate(answers[:-1], axis=0)
+        out = jnp.dot(dispatch[:, :cut], early, preferred_element_type=F32)
+        out = out + jnp.dot(dispatch[:, cut:], answers[-1], preferred_element_type=F32)
     return out.astype(BF)[None]
 
 

time: 166 us -> 166 us (level); the launches traced: 166 us -> 163 us
  blocking collectives: 112 us -> 92.1 us
  waiting for transfers between devices: 11.8 us -> 24.3 us
  starting transfers between devices: 23 us -> 28 us
    all_gather x1, blocking collectives: 68.7 us -> 48.5 us  [shards(): lax.all_gather(block, 'seq', axis=0, tiled=False, axis_index_groups=groups)]
    ppermute x0 -> x2, waiting for transfers between devices: none -> 11.8 us  [the longest x1 11.3 us: shards(): fetched = lax.ppermute(give, 'seq', beside)]
    ppermute x0 -> x2, starting transfers between devices: none -> 4.97 us  [the longest x1 2.98 us: shards(): fetched = lax.ppermute(give, 'seq', beside)]
    pallas_call x1 -> x3, Pallas kernels: 5.61 us -> 5.59 us  [attention(): pl.pallas_call(attend, out_shape=jax.ShapeDtypeStruct(q.shape, BF), in_sp...]
  transfers between devices with their start and end apart: 4 -> 6, of which waited for: 2 -> 4; matrix products, arithmetic and copies ran while one was open for 2% -> 2% of each run, Pallas kernels for 0% -> 3%
where the time goes in v7:
time: 166 us; the launch traced here: 163 us
  blocking collectives  92.1 us (55%)
  starting transfers between devices  28 us (17%)
  waiting for transfers between devices  24.3 us (15%)
  Pallas kernels  9.21 us (6%)
  matrix products  3.08 us (2%)
  other arithmetic  2.72 us (2%)
  between operations  2.3 us (1%)
  local copies, waits for them, and re-layouts  1.71 us (1%)
    all_gather x1, blocking collectives, shards(): lax.all_gather(block, 'seq', axis=0, tiled=False, axis_index_groups=groups)  48.5 us
    all_gather x1, blocking collectives, shards(): lax.all_gather(w, 'seq', axis=0, tiled=False, axis_index_groups=groups)  43.6 us
    ppermute x1, waiting for transfers between devices, shards(): fetched = lax.ppermute(give, 'seq', beside)  11.3 us
    ppermute x1, starting transfers between devices, shards(): other = lax.ppermute(own, 'seq', swap)  8.72 us
    all_to_all x1, waiting for transfers between devices, shards(): part = lax.all_to_all(part, 'doc', split_axis=0, concat_axis=0, tiled=True)  8.45 us
    all_to_all x1, starting transfers between devices, shards(): lax.all_to_all(x, ('doc', 'tensor'), split_axis=0, concat_axis=0, tiled=T...  7.73 us
    pallas_call x3, Pallas kernels, attention(): pl.pallas_call(attend, out_shape=jax.ShapeDtypeStruct(q.shape, BF), in_sp...  5.59 us
    all_to_all x1, starting transfers between devices, shards(): part = lax.all_to_all(part, 'doc', split_axis=0, concat_axis=0, tiled=True)  4.51 us
  transfers between devices with their start and end apart: 6, of which 4 were waited for; matrix products, arithmetic and copies ran while one was open for 2% of the time, Pallas kernels for 3%

profile of v7, /device:TPU:1, one launch (start us, length us, event | category | flops | bytes accessed | tf_op | source)
XLA Modules:
  0.0 163.4 jit_solution(17139199833931768506)
XLA Ops:
  0.0 0.0 copy-start
  0.0 0.0 copy-start.1
  0.0 1.1 copy-done.1
  1.1 1.5 vision_doc_tensor.1
  2.6 0.0 copy-start.3
  2.6 0.0 copy-start.4
  2.6 0.0 copy-start.5
  2.6 0.0 copy-start.6
  2.6 7.7 %all-to-all-start = ((bf16[16,32,2048]{2,1,0:T(8,128)(2,1)}), bf16[16,32,2048]{2,1,0:T(8,128)(2,1)S(1)}, u32[]{:S(2)}, u32[]{:S(2)}) async-start(bf16[16,32,2048]{2,1,0:T(8,128)(2,1)} %bitcast.2), calls=%async_computation | async-start | bytes 4194304 | tf_op jit(solution)/shard_map/vision_doc_tensor/all_to_all | solution.py:145
  10.4 0.1 pad_add_fusion.place_ref
  10.4 0.0 copy-done.3
  10.5 0.0 copy-done.4
  10.5 43.6 %all-gather = bf16[512,256]{1,0:T(8,128)(2,1)S(1)} all-gather(bf16[32,256]{1,0:T(8,128)(2,1)S(1)} %pad_maximum_fusion.1), channel_id=2, replica_groups={{0,16,32,48,64,80,96,112,128,144,160,176,192,208,224,240},{4,20,36,52,6..., dimensions={0}, use_global_device_ids=true | all-gather | bytes 278528 | tf_op jit(solution)/shard_map/weights_z/all_gather | solution.py:150
  54.1 0.0 all-to-all-done
  54.1 2.1 %collective-permute-start = (bf16[16,32,256]{2,1,0:T(8,128)(2,1)S(1)}, bf16[16,32,256]{2,1,0:T(8,128)(2,1)S(1)}, u32[]{:S(2)}, u32[]{:S(2)}) collective-permute-start(bf16[16,32,256]{2,1,0:T(8,128)(2,1)S(1)} %bitcast.40), channel_id=1, source_target_pairs={{0,8},{4,12},{8,0},{12,4},{16,24},{20,28},{24,16},{28,20},{32,40},... | collective-permute-start | bytes 786440 | tf_op jit(solution)/shard_map/weights_pair/ppermute | solution.py:168
  56.1 0.0 copy-done.5
  56.1 0.0 copy-done.6
  56.1 0.1 select_reduce_fusion
  56.3 0.6 reduce-window.6
  56.9 0.2 slice_reduce_fusion
  57.1 4.0 %collective-permute-done = bf16[16,32,256]{2,1,0:T(8,128)(2,1)S(1)} collective-permute-done((bf16[16,32,256]{2,1,0:T(8,128)(2,1)S(1)}, bf16[16,32,256]{2,1,0:T(8,128)(2,1)S(1)}, u32[]{:S(2)}, u32[]{:S(2)}) %collective-permute-start) | collective-permute-done | bytes 262176 | tf_op jit(solution)/shard_map/weights_pair/ppermute | solution.py:168
  61.2 8.7 %collective-permute-start.1 = (bf16[32,32,256]{2,1,0:T(8,128)(2,1)S(1)}, bf16[32,32,256]{2,1,0:T(8,128)(2,1)S(1)}, u32[]{:S(2)}, u32[]{:S(2)}) collective-permute-start(bf16[32,32,256]{2,1,0:T(8,128)(2,1)S(1)} %constant_dynamic-update-slice_fusion.own_ref), channel_id=1, source_target_pairs={{0,4},{4,0},{8,12},{12,8},{16,20},{20,16},{24,28},{28,24},{32,36},... | collective-permute-start | bytes 1572872 | tf_op jit(solution)/shard_map/weights_core/ppermute | solution.py:171
  69.9 0.1 fusion.11
  70.1 0.0 copy-done
  70.1 1.5 convolution_convert_fusion
  71.6 0.0 collective-permute-done.1.other_ref
  71.6 2.1 %project.1 = f32[512,256]{1,0:T(8,128)} custom-call(s32[2]{0:T(128)S(1)} %pad_add_fusion.place_ref, bf16[512,2048]{1,0:T(8,128)(2,1)S(1)} %bitcast.38, bf16[32,32,256]{2,1,0:T(8,128)(2,1)S(1)} %constant_dynamic-update-slice_fusion.own_ref, bf16[32,32,256]{2,1,0:T(8,128)(2,1)S(1)} %collective-permute-done.1.other_ref), custom_call_target="tpu_custom_call" | custom-call | tf_op jit(solution)/shard_map/project/pallas_call | solution.py:58
  73.7 4.5 %all-to-all-start.1 = ((f32[4,128,256]{2,1,0:T(8,128)}), f32[4,128,256]{2,1,0:T(8,128)S(1)}, u32[]{:S(2)}, u32[]{:S(2)}) async-start(f32[4,128,256]{2,1,0:T(8,128)} %bitcast.11), calls=%async_computation.1 | async-start | bytes 1048576 | tf_op jit(solution)/shard_map/reduce_doc/all_to_all | solution.py:177
  78.9 8.5 %all-to-all-done.1 = f32[4,128,256]{2,1,0:T(8,128)S(1)} async-done(((f32[4,128,256]{2,1,0:T(8,128)}), f32[4,128,256]{2,1,0:T(8,128)S(1)}, u32[]{:S(2)}, u32[]{:S(2)}) %all-to-all-start.1) | async-done | bytes 524320 | tf_op jit(solution)/shard_map/reduce_doc/all_to_all | solution.py:177
  87.4 0.6 multiply_reduce_fusion
  88.8 0.1 multiply_convert_fusion.1
  88.9 48.5 %all-gather.2 = f16[32,144,256]{2,1,0:T(8,128)(2,1)S(1)} all-gather(f16[1,144,256]{2,1,0:T(8,128)(2,1)S(1)} %pad_maximum_fusion), channel_id=1, replica_groups={{0,4,16,20,32,36,48,52,64,68,80,84,96,100,112,116,128,132,144,148,160,1..., dimensions={0}, use_global_device_ids=true | all-gather | bytes 2433024 | tf_op jit(solution)/shard_map/kv_seq/all_gather | solution.py:190
  137.4 0.0 copy-start.2
  137.4 0.3 constant_dynamic-slice_fusion
  137.7 3.0 %collective-permute-start.2 = (f16[16,144,256]{2,1,0:T(8,128)(2,1)S(1)}, f16[16,144,256]{2,1,0:T(8,128)(2,1)S(1)}, u32[]{:S(2)}, u32[]{:S(2)}) collective-permute-start(f16[16,144,256]{2,1,0:T(8,128)(2,1)S(1)} %constant_dynamic-slice_fusion), channel_id=1, source_target_pairs={{0,248},{4,12},{8,0},{12,20},{16,8},{20,28},{24,16},{28,36},{32,24... | collective-permute-start | bytes 3538952 | tf_op jit(solution)/shard_map/kv_seq/ppermute | solution.py:194
  141.4 0.0 copy-done.2
  141.4 0.5 convert_element_type.38.kv_ref
  141.9 2.8 %attention_first.1 = bf16[256,1024]{1,0:T(8,128)(2,1)S(1)} custom-call(f32[1]{0:T(128)S(6)} %copy.15.gate_ref, bf16[256,1024]{1,0:T(8,128)(2,1)S(1)} %slice.32.q_ref, bf16[32,144,256]{2,1,0:T(8,128)(2,1)S(1)} %convert_element_type.38.kv_ref), custom_call_target="tpu_custom_call" | custom-call | flops 301989888 | bytes 2359296 | tf_op jit(solution)/shard_map/attention_first/pallas_call | solution.py:118
  144.7 11.3 %collective-permute-done.2 = f16[16,144,256]{2,1,0:T(8,128)(2,1)S(1)} collective-permute-done((f16[16,144,256]{2,1,0:T(8,128)(2,1)S(1)}, f16[16,144,256]{2,1,0:T(8,128)(2,1)S(1)}, u32[]{:S(2)}, u32[]{:S(2)}) %collective-permute-start.2) | collective-permute-done | bytes 1179680 | tf_op jit(solution)/shard_map/kv_seq/ppermute | solution.py:194
  156.0 2.0 %collective-permute-start.3 = (f16[16,144,256]{2,1,0:T(8,128)(2,1)S(1)}, f16[16,144,256]{2,1,0:T(8,128)(2,1)S(1)}, u32[]{:S(2)}, u32[]{:S(2)}) collective-permute-start(f16[16,144,256]{2,1,0:T(8,128)(2,1)S(1)} %collective-permute-done.2), channel_id=1, source_target_pairs={{0,4},{4,0},{8,12},{12,8},{16,20},{20,16},{24,28},{28,24},{32,36},... | collective-permute-start | bytes 3538952 | tf_op jit(solution)/shard_map/kv_core/ppermute | solution.py:206
  158.0 0.1 iota_compare_fusion
  158.2 0.2 convert_element_type.39.kv_ref
  158.4 1.4 attention_rest.2
  159.8 0.4 fusion.2
  160.3 0.5 collective-permute-done.3
  160.7 0.2 convert_element_type.40.kv_ref
  160.9 1.4 attention_rest.3
  162.3 1.1 fusion.1
  (15 shorter events, 0.3 us)
Async XLA Ops:
  0.0 70.1 %copy-start = (bf16[1,256,1024]{2,1,0:T(8,128)(2,1)S(1)}, bf16[1,256,1024]{2,1,0:T(8,128)(2,1)}, u32[]{:S(2)}) copy-start(bf16[1,256,1024]{2,1,0:T(8,128)(2,1)} %param.8) | copy-start | bytes 1572868
  0.0 1.1 copy-start.1
  2.6 7.9 %copy-start.3 = (bf16[32,128]{1,0:T(8,128)(2,1)S(1)}, bf16[32,128]{1,0:T(8,128)(2,1)}, u32[]{:S(2)}) copy-start(bf16[32,128]{1,0:T(8,128)(2,1)} %param.11) | copy-start | bytes 24580
  2.6 7.9 %copy-start.4 = (bf16[32,128]{1,0:T(8,128)(2,1)S(1)}, bf16[32,128]{1,0:T(8,128)(2,1)}, u32[]{:S(2)}) copy-start(bf16[32,128]{1,0:T(8,128)(2,1)} %param.10) | copy-start | bytes 24580
  2.6 53.5 %copy-start.5 = (s32[1,256,1]{1,2,0:T(1,128)S(1)}, s32[1,256,1]{1,2,0:T(1,128)}, u32[]{:S(2)}) copy-start(s32[1,256,1]{1,2,0:T(1,128)} %param.13) | copy-start | bytes 3076
  2.6 53.5 %copy-start.6 = (s32[1,64]{1,0:T(1,128)S(1)}, s32[1,64]{1,0:T(1,128)}, u32[]{:S(2)}) copy-start(s32[1,64]{1,0:T(1,128)} %param.14) | copy-start | bytes 772
  2.6 51.5 %all-to-all-start = ((bf16[16,32,2048]{2,1,0:T(8,128)(2,1)}), bf16[16,32,2048]{2,1,0:T(8,128)(2,1)S(1)}, u32[]{:S(2)}, u32[]{:S(2)}) async-start(bf16[16,32,2048]{2,1,0:T(8,128)(2,1)} %bitcast.2), calls=%async_computation | async-start | bytes 4194304 | tf_op jit(solution)/shard_map/vision_doc_tensor/all_to_all | solution.py:145
  54.1 7.1 %collective-permute-start = (bf16[16,32,256]{2,1,0:T(8,128)(2,1)S(1)}, bf16[16,32,256]{2,1,0:T(8,128)(2,1)S(1)}, u32[]{:S(2)}, u32[]{:S(2)}) collective-permute-start(bf16[16,32,256]{2,1,0:T(8,128)(2,1)S(1)} %bitcast.40), channel_id=1, source_target_pairs={{0,8},{4,12},{8,0},{12,4},{16,24},{20,28},{24,16},{28,20},{32,40},... | collective-permute-start | bytes 786440 | tf_op jit(solution)/shard_map/weights_pair/ppermute | solution.py:168
  61.2 10.4 %collective-permute-start.1 = (bf16[32,32,256]{2,1,0:T(8,128)(2,1)S(1)}, bf16[32,32,256]{2,1,0:T(8,128)(2,1)S(1)}, u32[]{:S(2)}, u32[]{:S(2)}) collective-permute-start(bf16[32,32,256]{2,1,0:T(8,128)(2,1)S(1)} %constant_dynamic-update-slice_fusion.own_ref), channel_id=1, source_target_pairs={{0,4},{4,0},{8,12},{12,8},{16,20},{20,16},{24,28},{28,24},{32,36},... | collective-permute-start | bytes 1572872 | tf_op jit(solution)/shard_map/weights_core/ppermute | solution.py:171
  73.7 13.6 %all-to-all-start.1 = ((f32[4,128,256]{2,1,0:T(8,128)}), f32[4,128,256]{2,1,0:T(8,128)S(1)}, u32[]{:S(2)}, u32[]{:S(2)}) async-start(f32[4,128,256]{2,1,0:T(8,128)} %bitcast.11), calls=%async_computation.1 | async-start | bytes 1048576 | tf_op jit(solution)/shard_map/reduce_doc/all_to_all | solution.py:177
  137.4 3.9 %copy-start.2 = (bf16[512,1024]{1,0:T(8,128)(2,1)S(1)}, bf16[512,1024]{1,0:T(8,128)(2,1)}, u32[]{:S(2)}) copy-start(bf16[512,1024]{1,0:T(8,128)(2,1)} %convolution_convert_fusion) | copy-start | bytes 3145732
  137.7 18.3 %collective-permute-start.2 = (f16[16,144,256]{2,1,0:T(8,128)(2,1)S(1)}, f16[16,144,256]{2,1,0:T(8,128)(2,1)S(1)}, u32[]{:S(2)}, u32[]{:S(2)}) collective-permute-start(f16[16,144,256]{2,1,0:T(8,128)(2,1)S(1)} %constant_dynamic-slice_fusion), channel_id=1, source_target_pairs={{0,248},{4,12},{8,0},{12,20},{16,8},{20,28},{24,16},{28,36},{32,24... | collective-permute-start | bytes 3538952 | tf_op jit(solution)/shard_map/kv_seq/ppermute | solution.py:194
  156.0 4.7 %collective-permute-start.3 = (f16[16,144,256]{2,1,0:T(8,128)(2,1)S(1)}, f16[16,144,256]{2,1,0:T(8,128)(2,1)S(1)}, u32[]{:S(2)}, u32[]{:S(2)}) collective-permute-start(f16[16,144,256]{2,1,0:T(8,128)(2,1)S(1)} %collective-permute-done.2), channel_id=1, source_target_pairs={{0,4},{4,0},{8,12},{12,8},{16,20},{20,16},{24,28},{28,24},{32,36},... | collective-permute-start | bytes 3538952 | tf_op jit(solution)/shard_map/kv_core/ppermute | solution.py:206

commit v8 on v7

--- a/solution.py
+++ b/solution.py
@@ -10,7 +10,7 @@
 BF = jnp.bfloat16
 F32 = jnp.float32
 HF = jnp.float16
-NOTES = 16
+NOTES = 8
 KEY_SCALE = 2048.0
 TOP_LEVEL = 14.0
 
@@ -65,12 +65,39 @@
     )(place, x, own, other)
 
 
-UNROLL = 4
+def finish(len_ref, part_ref, out_ref):
+    kv = part_ref[0]
+    for d in range(1, part_ref.shape[0]):
+        kv = kv + part_ref[d]
+    vtok = kv.shape[0]
+    keys = head_norm(kv[:, :HD]).astype(BF).astype(F32)
+    values = kv[:, HD:].astype(BF).astype(F32)
+    largest = jnp.max(jnp.max(jnp.abs(values), axis=1, keepdims=True), axis=0, keepdims=True)
+    level = jnp.ceil(jnp.log2(jnp.maximum(largest, 1e-30)))
+    length = jnp.full((NOTES, HD), len_ref[0, 0], jnp.int32).astype(F32)
+    out_ref[:vtok, :HD] = keys * KEY_SCALE
+    out_ref[:vtok, HD:] = values * jnp.exp2(TOP_LEVEL - level)
+    out_ref[vtok:, :HD] = length
+    out_ref[vtok:, HD:] = jnp.broadcast_to(level, (NOTES, HD))
+
+
+def finishing(length, part):
+    vmem = pl.BlockSpec(memory_space=pltpu.VMEM)
+    return pl.pallas_call(
+        finish,
+        out_shape=jax.ShapeDtypeStruct((part.shape[1] + NOTES, part.shape[2]), F32),
+        in_specs=[pl.BlockSpec(memory_space=pltpu.SMEM), vmem],
+        out_specs=vmem,
+        compiler_params=pltpu.CompilerParams(vmem_limit_bytes=32 * 1024 * 1024),
+    )(length, part)
+
+
+UNROLL = 8
 
 
 def attend(gate_ref, q_ref, kv_ref, out_ref):
     heads = q_ref.shape[1] // HD
-    vtok = kv_ref.shape[1] - NOTES
+    vtok = kv_ref.shape[1] - 2 * NOTES
     pairs = kv_ref.shape[0] // 2
     factor = jnp.tanh(jnp.full((1, 1), gate_ref[0], F32))
     key = lax.broadcasted_iota(jnp.int32, (1, vtok), 1).astype(F32)
@@ -104,11 +131,12 @@
             out_ref[rows, h * HD : (h + 1) * HD] = ans[h * 2 * CAP : (h + 1) * 2 * CAP]
 
     def body(i, carry):
-        for u in range(UNROLL):
-            one(i * UNROLL + u)
+        for u in range(unroll):
+            one(i * unroll + u)
         return carry
 
-    lax.fori_loop(0, pairs // UNROLL, body, 0)
+    unroll = min(UNROLL, pairs)
+    lax.fori_loop(0, pairs // unroll, body, 0)
 
 
 def attention(gate, q, kv):
@@ -175,17 +203,9 @@
     with jax.named_scope("reduce_doc"):
         part = part.reshape(n_doc, -1, w.shape[1])
         part = lax.all_to_all(part, "doc", split_axis=0, concat_axis=0, tiled=True)
-        kv = jnp.sum(part, axis=0)
-    keys = lax.reduce_precision(head_norm(kv[:, :HD]), 8, 7)
-    values = lax.reduce_precision(kv[:, HD:], 8, 7)
 
     with jax.named_scope("kv_seq"):
-        largest = jnp.max(jnp.abs(values), keepdims=True)
-        level = jnp.ceil(jnp.log2(jnp.maximum(largest, 1e-30)))
-        block = jnp.concatenate([keys * KEY_SCALE, values * jnp.exp2(TOP_LEVEL - level)], axis=1)
-        lane = lax.broadcasted_iota(jnp.int32, (NOTES, 2 * HD), 1)
-        notes = jnp.where(lane < HD, image_len.astype(F32), level)
-        block = jnp.concatenate([block, notes], axis=0).astype(HF)
+        block = finishing(image_len, part).astype(HF)
         groups = [[4 * j + 2 * o + c for j in range(n_z // 2) for c in range(2)] for o in range(2)]
         blocks = lax.all_gather(block, "seq", axis=0, tiled=False, axis_index_groups=groups)
         many = blocks.shape[0] // 2
@@ -196,7 +216,7 @@
 
     def answer(held):
         size = held.shape[0] * CAP
-        return attention(attn_gate, q[start : start + size], held.astype(BF))
+        return attention(attn_gate, q[start : start + size], jnp.pad(held.astype(BF), ((0, 0), (0, NOTES), (0, 0))))
 
     with jax.named_scope("attention_first"):
         first = answer(blocks)

time: 166 us -> 162 us (0.976)
  Pallas kernels: 9.21 us -> 7.08 us
    pallas_call x3, Pallas kernels: 5.59 us -> 3.35 us  [attention(): pl.pallas_call(attend, out_shape=jax.ShapeDtypeStruct(q.shape, BF), in_sp...]
  transfers between devices with their start and end apart: 6 -> 6, of which waited for: 4 -> 4; matrix products, arithmetic and copies ran while one was open for 2% -> 3% of each run, Pallas kernels for 3% -> 2%
where the time goes in v8:
time: 162 us; the launch traced here: 160 us
  blocking collectives  91 us (56%)
  starting transfers between devices  28.5 us (18%)
  waiting for transfers between devices  24.5 us (15%)
  Pallas kernels  7.08 us (4%)
  matrix products  3.07 us (2%)
  local copies, waits for them, and re-layouts  1.99 us (1%)
  other arithmetic  1.89 us (1%)
    all_gather x1, blocking collectives, shards(): lax.all_gather(block, 'seq', axis=0, tiled=False, axis_index_groups=groups)  47.4 us
    all_gather x1, blocking collectives, shards(): lax.all_gather(w, 'seq', axis=0, tiled=False, axis_index_groups=groups)  43.6 us
    ppermute x1, waiting for transfers between devices, shards(): fetched = lax.ppermute(give, 'seq', beside)  11.1 us
    ppermute x1, starting transfers between devices, shards(): other = lax.ppermute(own, 'seq', swap)  8.72 us
    all_to_all x1, waiting for transfers between devices, shards(): part = lax.all_to_all(part, 'doc', split_axis=0, concat_axis=0, tiled=True)  8.44 us
    all_to_all x1, starting transfers between devices, shards(): lax.all_to_all(x, ('doc', 'tensor'), split_axis=0, concat_axis=0, tiled=T...  7.73 us
    all_to_all x1, starting transfers between devices, shards(): part = lax.all_to_all(part, 'doc', split_axis=0, concat_axis=0, tiled=True)  4.52 us
    ppermute x1, waiting for transfers between devices, shards(): beside = lax.ppermute(near, 'seq', [(i, i ^ 2) for i in range(n_seq)])  4.05 us
  transfers between devices with their start and end apart: 6, of which 4 were waited for; matrix products, arithmetic and copies ran while one was open for 3% of the time, Pallas kernels for 2%

profile of v8, /device:TPU:1, one launch (start us, length us, event | category | flops | bytes accessed | tf_op | source)
XLA Modules:
  0.0 159.6 jit_solution(2642426143397621521)
XLA Ops:
  0.0 0.0 copy-start
  0.0 0.0 copy-start.1
  0.0 1.1 copy-done.1
  1.1 1.5 vision_doc_tensor.1
  2.6 0.0 copy-start.3
  2.6 0.0 copy-start.4
  2.6 0.0 copy-start.5
  2.6 0.0 copy-start.6
  2.6 7.7 %all-to-all-start = ((bf16[16,32,2048]{2,1,0:T(8,128)(2,1)}), bf16[16,32,2048]{2,1,0:T(8,128)(2,1)S(1)}, u32[]{:S(2)}, u32[]{:S(2)}) async-start(bf16[16,32,2048]{2,1,0:T(8,128)(2,1)} %bitcast.2), calls=%async_computation | async-start | bytes 4194304 | tf_op jit(solution)/shard_map/vision_doc_tensor/all_to_all | solution.py:173
  10.4 0.1 pad_add_fusion.place_ref
  10.4 0.0 copy-done.3
  10.4 0.0 copy-done.4
  10.5 43.6 %all-gather = bf16[512,256]{1,0:T(8,128)(2,1)S(1)} all-gather(bf16[32,256]{1,0:T(8,128)(2,1)S(1)} %pad_maximum_fusion), channel_id=2, replica_groups={{0,16,32,48,64,80,96,112,128,144,160,176,192,208,224,240},{4,20,36,52,6..., dimensions={0}, use_global_device_ids=true | all-gather | bytes 278528 | tf_op jit(solution)/shard_map/weights_z/all_gather | solution.py:178
  54.1 0.0 all-to-all-done
  54.1 2.1 %collective-permute-start = (bf16[16,32,256]{2,1,0:T(8,128)(2,1)S(1)}, bf16[16,32,256]{2,1,0:T(8,128)(2,1)S(1)}, u32[]{:S(2)}, u32[]{:S(2)}) collective-permute-start(bf16[16,32,256]{2,1,0:T(8,128)(2,1)S(1)} %bitcast.40), channel_id=1, source_target_pairs={{0,8},{4,12},{8,0},{12,4},{16,24},{20,28},{24,16},{28,20},{32,40},... | collective-permute-start | bytes 786440 | tf_op jit(solution)/shard_map/weights_pair/ppermute | solution.py:196
  56.1 0.0 copy-done.5
  56.1 0.0 copy-done.6
  56.1 0.1 select_reduce_fusion
  56.2 0.6 reduce-window.6
  56.9 0.2 slice_reduce_fusion
  57.1 4.0 %collective-permute-done = bf16[16,32,256]{2,1,0:T(8,128)(2,1)S(1)} collective-permute-done((bf16[16,32,256]{2,1,0:T(8,128)(2,1)S(1)}, bf16[16,32,256]{2,1,0:T(8,128)(2,1)S(1)}, u32[]{:S(2)}, u32[]{:S(2)}) %collective-permute-start) | collective-permute-done | bytes 262176 | tf_op jit(solution)/shard_map/weights_pair/ppermute | solution.py:196
  61.2 8.7 %collective-permute-start.1 = (bf16[32,32,256]{2,1,0:T(8,128)(2,1)S(1)}, bf16[32,32,256]{2,1,0:T(8,128)(2,1)S(1)}, u32[]{:S(2)}, u32[]{:S(2)}) collective-permute-start(bf16[32,32,256]{2,1,0:T(8,128)(2,1)S(1)} %constant_dynamic-update-slice_fusion.own_ref), channel_id=1, source_target_pairs={{0,4},{4,0},{8,12},{12,8},{16,20},{20,16},{24,28},{28,24},{32,36},... | collective-permute-start | bytes 1572872 | tf_op jit(solution)/shard_map/weights_core/ppermute | solution.py:199
  69.9 0.1 fusion.11
  70.0 0.0 copy-done
  70.1 1.5 convolution_convert_fusion
  71.6 0.0 collective-permute-done.1.other_ref
  71.6 2.1 %project.1 = f32[512,256]{1,0:T(8,128)} custom-call(s32[2]{0:T(128)S(1)} %pad_add_fusion.place_ref, bf16[512,2048]{1,0:T(8,128)(2,1)S(1)} %bitcast.36, bf16[32,32,256]{2,1,0:T(8,128)(2,1)S(1)} %constant_dynamic-update-slice_fusion.own_ref, bf16[32,32,256]{2,1,0:T(8,128)(2,1)S(1)} %collective-permute-done.1.other_ref), custom_call_target="tpu_custom_call" | custom-call | tf_op jit(solution)/shard_map/project/pallas_call | solution.py:58
  73.7 4.5 %all-to-all-start.1 = ((f32[4,128,256]{2,1,0:T(8,128)}), f32[4,128,256]{2,1,0:T(8,128)S(1)}, u32[]{:S(2)}, u32[]{:S(2)}) async-start(f32[4,128,256]{2,1,0:T(8,128)} %bitcast.11), calls=%async_computation.1 | async-start | bytes 1048576 | tf_op jit(solution)/shard_map/reduce_doc/all_to_all | solution.py:205
  78.9 8.4 %all-to-all-done.1.part_ref = f32[4,128,256]{2,1,0:T(8,128)S(1)} async-done(((f32[4,128,256]{2,1,0:T(8,128)}), f32[4,128,256]{2,1,0:T(8,128)S(1)}, u32[]{:S(2)}, u32[]{:S(2)}) %all-to-all-start.1) | async-done | bytes 524320 | tf_op jit(solution)/shard_map/reduce_doc/all_to_all | solution.py:205
  87.3 0.1 kv_seq.1
  87.5 47.4 %all-gather.3 = f16[4352,256]{1,0:T(8,128)(2,1)S(1)} all-gather(f16[136,256]{1,0:T(8,128)(2,1)S(1)} %convert_element_type.34), channel_id=3, replica_groups={{0,4,16,20,32,36,48,52,64,68,80,84,96,100,112,116,128,132,144,148,160,1..., dimensions={0}, use_global_device_ids=true | all-gather | bytes 2297856 | tf_op jit(solution)/shard_map/kv_seq/all_gather | solution.py:210
  134.9 0.0 copy-start.2
  134.9 0.3 constant_dynamic-slice_fusion
  135.1 3.5 %collective-permute-start.2 = (f16[16,136,256]{2,1,0:T(8,128)(2,1)S(1)}, f16[16,136,256]{2,1,0:T(8,128)(2,1)S(1)}, u32[]{:S(2)}, u32[]{:S(2)}) collective-permute-start(f16[16,136,256]{2,1,0:T(8,128)(2,1)S(1)} %constant_dynamic-slice_fusion), channel_id=1, source_target_pairs={{0,248},{4,12},{8,0},{12,20},{16,8},{20,28},{24,16},{28,36},{32,24... | collective-permute-start | bytes 3342344 | tf_op jit(solution)/shard_map/kv_seq/ppermute | solution.py:214
  139.3 0.0 copy-done.2
  139.3 0.4 convert_element_type.35
  139.8 0.2 pad.11.kv_ref
  139.9 1.7 %attention_first.1 = bf16[256,1024]{1,0:T(8,128)(2,1)S(1)} custom-call(f32[1]{0:T(128)S(6)} %copy.14.gate_ref, bf16[256,1024]{1,0:T(8,128)(2,1)S(1)} %slice.24.q_ref, bf16[32,144,256]{2,1,0:T(8,128)(2,1)S(1)} %pad.11.kv_ref), custom_call_target="tpu_custom_call" | custom-call | flops 301989888 | bytes 2359296 | tf_op jit(solution)/shard_map/attention_first/pallas_call | solution.py:146
  141.6 11.1 %collective-permute-done.2 = f16[16,136,256]{2,1,0:T(8,128)(2,1)S(1)} collective-permute-done((f16[16,136,256]{2,1,0:T(8,128)(2,1)S(1)}, f16[16,136,256]{2,1,0:T(8,128)(2,1)S(1)}, u32[]{:S(2)}, u32[]{:S(2)}) %collective-permute-start.2) | collective-permute-done | bytes 1114144 | tf_op jit(solution)/shard_map/kv_seq/ppermute | solution.py:214
  152.7 2.0 %collective-permute-start.3 = (f16[16,136,256]{2,1,0:T(8,128)(2,1)S(1)}, f16[16,136,256]{2,1,0:T(8,128)(2,1)S(1)}, u32[]{:S(2)}, u32[]{:S(2)}) collective-permute-start(f16[16,136,256]{2,1,0:T(8,128)(2,1)S(1)} %collective-permute-done.2), channel_id=1, source_target_pairs={{0,4},{4,0},{8,12},{12,8},{16,20},{20,16},{24,28},{28,24},{32,36},... | collective-permute-start | bytes 3342344 | tf_op jit(solution)/shard_map/kv_core/ppermute | solution.py:226
  154.7 0.1 iota_compare_fusion
  154.9 0.2 convert_element_type.36
  155.1 0.1 pad.12.kv_ref
  155.2 0.8 attention_rest.2
  156.0 0.5 fusion.2
  156.5 0.9 collective-permute-done.3
  157.4 0.2 convert_element_type.37
  157.5 0.1 pad.13.kv_ref
  157.6 0.8 attention_rest.3
  158.5 1.1 fusion.1
  (10 shorter events, 0.2 us)
Async XLA Ops:
  0.0 70.0 %copy-start = (bf16[1,256,1024]{2,1,0:T(8,128)(2,1)S(1)}, bf16[1,256,1024]{2,1,0:T(8,128)(2,1)}, u32[]{:S(2)}) copy-start(bf16[1,256,1024]{2,1,0:T(8,128)(2,1)} %param.8) | copy-start | bytes 1572868
  0.0 1.1 copy-start.1
  2.6 7.9 %copy-start.3 = (bf16[32,128]{1,0:T(8,128)(2,1)S(1)}, bf16[32,128]{1,0:T(8,128)(2,1)}, u32[]{:S(2)}) copy-start(bf16[32,128]{1,0:T(8,128)(2,1)} %param.11) | copy-start | bytes 24580
  2.6 7.9 %copy-start.4 = (bf16[32,128]{1,0:T(8,128)(2,1)S(1)}, bf16[32,128]{1,0:T(8,128)(2,1)}, u32[]{:S(2)}) copy-start(bf16[32,128]{1,0:T(8,128)(2,1)} %param.10) | copy-start | bytes 24580
  2.6 53.5 %copy-start.5 = (s32[1,256,1]{1,2,0:T(1,128)S(1)}, s32[1,256,1]{1,2,0:T(1,128)}, u32[]{:S(2)}) copy-start(s32[1,256,1]{1,2,0:T(1,128)} %param.13) | copy-start | bytes 3076
  2.6 53.5 %copy-start.6 = (s32[1,64]{1,0:T(1,128)S(1)}, s32[1,64]{1,0:T(1,128)}, u32[]{:S(2)}) copy-start(s32[1,64]{1,0:T(1,128)} %param.14) | copy-start | bytes 772
  2.6 51.5 %all-to-all-start = ((bf16[16,32,2048]{2,1,0:T(8,128)(2,1)}), bf16[16,32,2048]{2,1,0:T(8,128)(2,1)S(1)}, u32[]{:S(2)}, u32[]{:S(2)}) async-start(bf16[16,32,2048]{2,1,0:T(8,128)(2,1)} %bitcast.2), calls=%async_computation | async-start | bytes 4194304 | tf_op jit(solution)/shard_map/vision_doc_tensor/all_to_all | solution.py:173
  54.1 7.1 %collective-permute-start = (bf16[16,32,256]{2,1,0:T(8,128)(2,1)S(1)}, bf16[16,32,256]{2,1,0:T(8,128)(2,1)S(1)}, u32[]{:S(2)}, u32[]{:S(2)}) collective-permute-start(bf16[16,32,256]{2,1,0:T(8,128)(2,1)S(1)} %bitcast.40), channel_id=1, source_target_pairs={{0,8},{4,12},{8,0},{12,4},{16,24},{20,28},{24,16},{28,20},{32,40},... | collective-permute-start | bytes 786440 | tf_op jit(solution)/shard_map/weights_pair/ppermute | solution.py:196
  61.2 10.4 %collective-permute-start.1 = (bf16[32,32,256]{2,1,0:T(8,128)(2,1)S(1)}, bf16[32,32,256]{2,1,0:T(8,128)(2,1)S(1)}, u32[]{:S(2)}, u32[]{:S(2)}) collective-permute-start(bf16[32,32,256]{2,1,0:T(8,128)(2,1)S(1)} %constant_dynamic-update-slice_fusion.own_ref), channel_id=1, source_target_pairs={{0,4},{4,0},{8,12},{12,8},{16,20},{20,16},{24,28},{28,24},{32,36},... | collective-permute-start | bytes 1572872 | tf_op jit(solution)/shard_map/weights_core/ppermute | solution.py:199
  73.7 13.6 %all-to-all-start.1 = ((f32[4,128,256]{2,1,0:T(8,128)}), f32[4,128,256]{2,1,0:T(8,128)S(1)}, u32[]{:S(2)}, u32[]{:S(2)}) async-start(f32[4,128,256]{2,1,0:T(8,128)} %bitcast.11), calls=%async_computation.1 | async-start | bytes 1048576 | tf_op jit(solution)/shard_map/reduce_doc/all_to_all | solution.py:205
  134.9 4.4 %copy-start.2 = (bf16[512,1024]{1,0:T(8,128)(2,1)S(1)}, bf16[512,1024]{1,0:T(8,128)(2,1)}, u32[]{:S(2)}) copy-start(bf16[512,1024]{1,0:T(8,128)(2,1)} %convolution_convert_fusion) | copy-start | bytes 3145732
  135.1 17.6 %collective-permute-start.2 = (f16[16,136,256]{2,1,0:T(8,128)(2,1)S(1)}, f16[16,136,256]{2,1,0:T(8,128)(2,1)S(1)}, u32[]{:S(2)}, u32[]{:S(2)}) collective-permute-start(f16[16,136,256]{2,1,0:T(8,128)(2,1)S(1)} %constant_dynamic-slice_fusion), channel_id=1, source_target_pairs={{0,248},{4,12},{8,0},{12,20},{16,8},{20,28},{24,16},{28,36},{32,24... | collective-permute-start | bytes 3342344 | tf_op jit(solution)/shard_map/kv_seq/ppermute | solution.py:214
  152.7 4.6 %collective-permute-start.3 = (f16[16,136,256]{2,1,0:T(8,128)(2,1)S(1)}, f16[16,136,256]{2,1,0:T(8,128)(2,1)S(1)}, u32[]{:S(2)}, u32[]{:S(2)}) collective-permute-start(f16[16,136,256]{2,1,0:T(8,128)(2,1)S(1)} %collective-permute-done.2), channel_id=1, source_target_pairs={{0,4},{4,0},{8,12},{12,8},{16,20},{20,16},{24,28},{28,24},{32,36},... | collective-permute-start | bytes 3342344 | tf_op jit(solution)/shard_map/kv_core/ppermute | solution.py:226

commit v9 on v8

--- a/solution.py
+++ b/solution.py
@@ -183,11 +183,7 @@
     target = jnp.sum(jnp.where(picked, image_owner[0][None, :], 0), axis=1)
     onehot = (target[:, None] == owners[None, :]).astype(jnp.int32)
     ranks = jnp.cumsum(onehot, axis=0) - onehot
-    step, odd = target // 4, (target // 2 + z) % 2
-    half = n_seq // 8
-    later = n_seq // 2 + jnp.where(step // half == core, 0, 2 * half) + 2 * (step % half)
-    place = jnp.where(odd == 0, 2 * step, later) + target % 2
-    slot = place * CAP + jnp.sum(ranks * onehot, axis=1)
+    slot = target * CAP + jnp.sum(ranks * onehot, axis=1)
     dispatch = (slot[:, None] == jnp.arange(n_seq * CAP, dtype=jnp.int32)[None, :]).astype(BF)
     with jax.named_scope("dispatch"):
         q = jnp.dot(dispatch.T, queries[0], preferred_element_type=F32).astype(BF)
@@ -206,33 +202,11 @@
 
     with jax.named_scope("kv_seq"):
         block = finishing(image_len, part).astype(HF)
-        groups = [[4 * j + 2 * o + c for j in range(n_z // 2) for c in range(2)] for o in range(2)]
-        blocks = lax.all_gather(block, "seq", axis=0, tiled=False, axis_index_groups=groups)
-        many = blocks.shape[0] // 2
-        give = lax.dynamic_slice_in_dim(blocks, core * many, many, axis=0)
-        beside = [(i, (i + (2 if i % 2 else -2)) % n_seq) for i in range(n_seq)]
-        fetched = lax.ppermute(give, "seq", beside)
-    answers, start = [], 0
-
-    def answer(held):
-        size = held.shape[0] * CAP
-        return attention(attn_gate, q[start : start + size], jnp.pad(held.astype(BF), ((0, 0), (0, NOTES), (0, 0))))
-
-    with jax.named_scope("attention_first"):
-        first = answer(blocks)
-        fetched, first = lax.optimization_barrier((fetched, first))
-        answers, start = [first], first.shape[0]
-    with jax.named_scope("kv_core"):
-        swapped = lax.ppermute(fetched, "seq", swap)
-    with jax.named_scope("attention_rest"):
-        for held in (fetched, swapped):
-            answers.append(answer(held))
-            start += answers[-1].shape[0]
+        blocks = lax.all_gather(block, "seq", axis=0, tiled=False).astype(BF)
+    with jax.named_scope("attention"):
+        answer = attention(attn_gate, q, jnp.pad(blocks, ((0, 0), (0, NOTES), (0, 0))))
     with jax.named_scope("combine"):
-        cut = start - answers[-1].shape[0]
-        early = jnp.concatenate(answers[:-1], axis=0)
-        out = jnp.dot(dispatch[:, :cut], early, preferred_element_type=F32)
-        out = out + jnp.dot(dispatch[:, cut:], answers[-1], preferred_element_type=F32)
+        out = jnp.dot(dispatch, answer, preferred_element_type=F32)
     return out.astype(BF)[None]
 
 

time: 162 us -> 162 us (level); the launches traced: 160 us -> 162 us
  blocking collectives: 91 us -> 111 us
  waiting for transfers between devices: 24.5 us -> 11.8 us
  starting transfers between devices: 28.5 us -> 22.9 us
    all_gather x1, blocking collectives: 47.4 us -> 67.6 us  [shards(): blocks = lax.all_gather(block, 'seq', axis=0, tiled=False).astype(BF)]
    ppermute x2 -> x0, waiting for transfers between devices: 12 us -> none  [the longest x1 11.1 us: shards(): fetched = lax.ppermute(give, 'seq', beside)]
    ppermute x2 -> x0, starting transfers between devices: 5.49 us -> none  [the longest x1 3.5 us: shards(): fetched = lax.ppermute(give, 'seq', beside)]
    pallas_call x3 -> x1, Pallas kernels: 3.35 us -> 3.36 us  [attention(): pl.pallas_call(attend, out_shape=jax.ShapeDtypeStruct(q.shape, BF), in_sp...]
  transfers between devices with their start and end apart: 6 -> 4, of which waited for: 4 -> 2; matrix products, arithmetic and copies ran while one was open for 3% -> 2% of each run, Pallas kernels for 2% -> 0%
where the time goes in v9:
time: 162 us
  blocking collectives  111 us (69%)
  starting transfers between devices  22.9 us (14%)
  waiting for transfers between devices  11.8 us (7%)
  Pallas kernels  7.1 us (4%)
  matrix products  2.84 us (2%)
  local copies, waits for them, and re-layouts  2.55 us (2%)
  other arithmetic  1.69 us (1%)
    all_gather x1, blocking collectives, shards(): blocks = lax.all_gather(block, 'seq', axis=0, tiled=False).astype(BF)  67.6 us
    all_gather x1, blocking collectives, shards(): lax.all_gather(w, 'seq', axis=0, tiled=False, axis_index_groups=groups)  43.6 us
    ppermute x1, starting transfers between devices, shards(): other = lax.ppermute(own, 'seq', swap)  8.72 us
    all_to_all x1, waiting for transfers between devices, shards(): part = lax.all_to_all(part, 'doc', split_axis=0, concat_axis=0, tiled=True)  7.79 us
    all_to_all x1, starting transfers between devices, shards(): lax.all_to_all(x, ('doc', 'tensor'), split_axis=0, concat_axis=0, tiled=T...  7.58 us
    all_to_all x1, starting transfers between devices, shards(): part = lax.all_to_all(part, 'doc', split_axis=0, concat_axis=0, tiled=True)  4.52 us
    ppermute x1, waiting for transfers between devices, shards(): beside = lax.ppermute(near, 'seq', [(i, i ^ 2) for i in range(n_seq)])  4.05 us
    pallas_call x1, Pallas kernels, attention(): pl.pallas_call(attend, out_shape=jax.ShapeDtypeStruct(q.shape, BF), in_sp...  3.36 us
  transfers between devices with their start and end apart: 4, of which 2 were waited for; matrix products, arithmetic and copies ran while one was open for 2% of the time, Pallas kernels for 0%

profile of v9, /device:TPU:1, one launch (start us, length us, event | category | flops | bytes accessed | tf_op | source)
XLA Modules:
  0.0 161.6 jit_solution(4132842658508196135)
XLA Ops:
  0.0 0.0 copy-start
  0.0 0.0 copy-start.5
  0.0 0.0 copy-start.6
  0.0 0.0 copy-start.2
  0.0 1.1 copy-done.2
  1.1 0.0 copy-start.3
  1.1 0.0 copy-start.4
  1.1 1.5 vision_doc_tensor.1
  2.6 7.6 %all-to-all-start = ((bf16[16,32,2048]{2,1,0:T(8,128)(2,1)}), bf16[16,32,2048]{2,1,0:T(8,128)(2,1)S(1)}, u32[]{:S(2)}, u32[]{:S(2)}) async-start(bf16[16,32,2048]{2,1,0:T(8,128)(2,1)} %bitcast.2), calls=%async_computation | async-start | bytes 4194304 | tf_op jit(solution)/shard_map/vision_doc_tensor/all_to_all | solution.py:173
  10.2 0.1 pad_add_fusion.place_ref
  10.3 0.0 copy-done.3
  10.3 0.0 copy-done.4
  10.3 43.6 %all-gather = bf16[512,256]{1,0:T(8,128)(2,1)S(1)} all-gather(bf16[32,256]{1,0:T(8,128)(2,1)S(1)} %pad_maximum_fusion), channel_id=2, replica_groups={{0,16,32,48,64,80,96,112,128,144,160,176,192,208,224,240},{4,20,36,52,6..., dimensions={0}, use_global_device_ids=true | all-gather | bytes 278528 | tf_op jit(solution)/shard_map/weights_z/all_gather | solution.py:178
  53.9 0.0 all-to-all-done
  53.9 2.1 %collective-permute-start = (bf16[16,32,256]{2,1,0:T(8,128)(2,1)S(1)}, bf16[16,32,256]{2,1,0:T(8,128)(2,1)S(1)}, u32[]{:S(2)}, u32[]{:S(2)}) collective-permute-start(bf16[16,32,256]{2,1,0:T(8,128)(2,1)S(1)} %bitcast.39), channel_id=1, source_target_pairs={{0,8},{4,12},{8,0},{12,4},{16,24},{20,28},{24,16},{28,20},{32,40},... | collective-permute-start | bytes 786440 | tf_op jit(solution)/shard_map/weights_pair/ppermute | solution.py:192
  56.0 0.0 copy-done.5
  56.0 0.0 copy-done.6
  56.0 0.1 select_reduce_fusion
  56.1 0.6 reduce-window.6
  56.7 0.2 slice_reduce_fusion
  57.0 4.0 %collective-permute-done = bf16[16,32,256]{2,1,0:T(8,128)(2,1)S(1)} collective-permute-done((bf16[16,32,256]{2,1,0:T(8,128)(2,1)S(1)}, bf16[16,32,256]{2,1,0:T(8,128)(2,1)S(1)}, u32[]{:S(2)}, u32[]{:S(2)}) %collective-permute-start) | collective-permute-done | bytes 262176 | tf_op jit(solution)/shard_map/weights_pair/ppermute | solution.py:192
  61.1 8.7 %collective-permute-start.1 = (bf16[32,32,256]{2,1,0:T(8,128)(2,1)S(1)}, bf16[32,32,256]{2,1,0:T(8,128)(2,1)S(1)}, u32[]{:S(2)}, u32[]{:S(2)}) collective-permute-start(bf16[32,32,256]{2,1,0:T(8,128)(2,1)S(1)} %constant_dynamic-update-slice_fusion.own_ref), channel_id=1, source_target_pairs={{0,4},{4,0},{8,12},{12,8},{16,20},{20,16},{24,28},{28,24},{32,36},... | collective-permute-start | bytes 1572872 | tf_op jit(solution)/shard_map/weights_core/ppermute | solution.py:195
  69.8 0.1 fusion.6
  69.9 0.0 copy-done
  69.9 1.5 convolution_convert_fusion.q_ref
  71.4 0.0 collective-permute-done.1.other_ref
  71.5 2.1 %project.1 = f32[512,256]{1,0:T(8,128)} custom-call(s32[2]{0:T(128)S(1)} %pad_add_fusion.place_ref, bf16[512,2048]{1,0:T(8,128)(2,1)S(1)} %bitcast.36, bf16[32,32,256]{2,1,0:T(8,128)(2,1)S(1)} %constant_dynamic-update-slice_fusion.own_ref, bf16[32,32,256]{2,1,0:T(8,128)(2,1)S(1)} %collective-permute-done.1.other_ref), custom_call_target="tpu_custom_call" | custom-call | tf_op jit(solution)/shard_map/project/pallas_call | solution.py:58
  73.6 4.5 %all-to-all-start.1 = ((f32[4,128,256]{2,1,0:T(8,128)}), f32[4,128,256]{2,1,0:T(8,128)S(1)}, u32[]{:S(2)}, u32[]{:S(2)}) async-start(f32[4,128,256]{2,1,0:T(8,128)} %bitcast.11), calls=%async_computation.1 | async-start | bytes 1048576 | tf_op jit(solution)/shard_map/reduce_doc/all_to_all | solution.py:201
  79.4 7.8 %all-to-all-done.1.part_ref = f32[4,128,256]{2,1,0:T(8,128)S(1)} async-done(((f32[4,128,256]{2,1,0:T(8,128)}), f32[4,128,256]{2,1,0:T(8,128)S(1)}, u32[]{:S(2)}, u32[]{:S(2)}) %all-to-all-start.1) | async-done | bytes 524320 | tf_op jit(solution)/shard_map/reduce_doc/all_to_all | solution.py:201
  87.2 0.1 kv_seq.1
  87.3 67.6 %all-gather.3 = f16[8704,256]{1,0:T(8,128)(2,1)S(1)} all-gather(f16[136,256]{1,0:T(8,128)(2,1)S(1)} %convert_element_type.25), channel_id=3, replica_groups=mesh['doc'=4,'seq'=64,'tensor'=4] {'seq'}, dimensions={0}, use_global_device_ids=true | all-gather | bytes 4526080 | tf_op jit(solution)/shard_map/kv_seq/all_gather | solution.py:205
  154.9 0.7 convert_element_type.28
  155.7 0.0 copy-start.1
  155.7 0.3 pad.4.kv_ref
  156.1 0.9 copy-done.1
  156.9 3.4 %attention.1 = bf16[512,1024]{1,0:T(8,128)(2,1)S(1)} custom-call(f32[1]{0:T(128)S(6)} %copy.13.gate_ref, bf16[512,1024]{1,0:T(8,128)(2,1)S(1)} %copy-done.1, bf16[64,144,256]{2,1,0:T(8,128)(2,1)S(1)} %pad.4.kv_ref), custom_call_target="tpu_custom_call" | custom-call | flops 603979776 | bytes 4718592 | tf_op jit(solution)/shard_map/attention/pallas_call | solution.py:146
  160.3 1.3 fusion
  (8 shorter events, 0.1 us)
Async XLA Ops:
  0.0 69.9 %copy-start = (bf16[1,256,1024]{2,1,0:T(8,128)(2,1)S(1)}, bf16[1,256,1024]{2,1,0:T(8,128)(2,1)}, u32[]{:S(2)}) copy-start(bf16[1,256,1024]{2,1,0:T(8,128)(2,1)} %param.8) | copy-start | bytes 1572868
  0.0 56.0 %copy-start.5 = (s32[1,256,1]{1,2,0:T(1,128)S(1)}, s32[1,256,1]{1,2,0:T(1,128)}, u32[]{:S(2)}) copy-start(s32[1,256,1]{1,2,0:T(1,128)} %param.13) | copy-start | bytes 3076
  0.0 56.0 %copy-start.6 = (s32[1,64]{1,0:T(1,128)S(1)}, s32[1,64]{1,0:T(1,128)}, u32[]{:S(2)}) copy-start(s32[1,64]{1,0:T(1,128)} %param.14) | copy-start | bytes 772
  0.0 1.1 copy-start.2
  1.1 9.2 %copy-start.3 = (bf16[32,128]{1,0:T(8,128)(2,1)S(1)}, bf16[32,128]{1,0:T(8,128)(2,1)}, u32[]{:S(2)}) copy-start(bf16[32,128]{1,0:T(8,128)(2,1)} %param.11) | copy-start | bytes 24580
  1.1 9.2 %copy-start.4 = (bf16[32,128]{1,0:T(8,128)(2,1)S(1)}, bf16[32,128]{1,0:T(8,128)(2,1)}, u32[]{:S(2)}) copy-start(bf16[32,128]{1,0:T(8,128)(2,1)} %param.10) | copy-start | bytes 24580
  2.6 51.3 %all-to-all-start = ((bf16[16,32,2048]{2,1,0:T(8,128)(2,1)}), bf16[16,32,2048]{2,1,0:T(8,128)(2,1)S(1)}, u32[]{:S(2)}, u32[]{:S(2)}) async-start(bf16[16,32,2048]{2,1,0:T(8,128)(2,1)} %bitcast.2), calls=%async_computation | async-start | bytes 4194304 | tf_op jit(solution)/shard_map/vision_doc_tensor/all_to_all | solution.py:173
  53.9 7.1 %collective-permute-start = (bf16[16,32,256]{2,1,0:T(8,128)(2,1)S(1)}, bf16[16,32,256]{2,1,0:T(8,128)(2,1)S(1)}, u32[]{:S(2)}, u32[]{:S(2)}) collective-permute-start(bf16[16,32,256]{2,1,0:T(8,128)(2,1)S(1)} %bitcast.39), channel_id=1, source_target_pairs={{0,8},{4,12},{8,0},{12,4},{16,24},{20,28},{24,16},{28,20},{32,40},... | collective-permute-start | bytes 786440 | tf_op jit(solution)/shard_map/weights_pair/ppermute | solution.py:192
  61.1 10.4 %collective-permute-start.1 = (bf16[32,32,256]{2,1,0:T(8,128)(2,1)S(1)}, bf16[32,32,256]{2,1,0:T(8,128)(2,1)S(1)}, u32[]{:S(2)}, u32[]{:S(2)}) collective-permute-start(bf16[32,32,256]{2,1,0:T(8,128)(2,1)S(1)} %constant_dynamic-update-slice_fusion.own_ref), channel_id=1, source_target_pairs={{0,4},{4,0},{8,12},{12,8},{16,20},{20,16},{24,28},{28,24},{32,36},... | collective-permute-start | bytes 1572872 | tf_op jit(solution)/shard_map/weights_core/ppermute | solution.py:195
  73.6 13.6 %all-to-all-start.1 = ((f32[4,128,256]{2,1,0:T(8,128)}), f32[4,128,256]{2,1,0:T(8,128)S(1)}, u32[]{:S(2)}, u32[]{:S(2)}) async-start(f32[4,128,256]{2,1,0:T(8,128)} %bitcast.11), calls=%async_computation.1 | async-start | bytes 1048576 | tf_op jit(solution)/shard_map/reduce_doc/all_to_all | solution.py:201
  155.7 1.2 copy-start.1
